TPU v7x, 32 devices: a whole 2x2x4 slice. The times are simulated.
32 devices in a mesh: row: 16 (over z, y, core), proto: 2 (over x).
Axes of the slice: x: 2, y: 2, z: 4, core: 2. Of those that a mesh axis runs over, the one named last changes fastest.
Arguments:
- tokens: bfloat16 [8192, 4096], P('row'), may hold values from -6 to 6
- w_in: bfloat16 [4096, 8192], P('row', 'proto'), may hold values from -0.09375 to 0.09375
- w_out: bfloat16 [8192, 384], P('proto'), may hold values from -0.0625 to 0.0625
- teacher_z: bfloat16 [8192, 384], P(('row', 'proto')), may hold values from -6 to 6
- proto_student: bfloat16 [384, 49152], P(None, 'proto'), may hold values from -48 to 48
- proto_teacher: bfloat16 [384, 49152], P(None, 'proto'), may hold values from -48 to 48
- center: float32 [49152], P('proto'), may hold values from -0.6 to 0.6
- image_of: int32 [8192], P('row'), may hold values from 0 to 63
Outputs:
- loss: float32 [], replicated
- w_in_grad: float32 [4096, 8192], P('row', 'proto')
- w_out_grad: float32 [8192, 384], P('proto')
- proto_grad: float32 [384, 49152], P('row', 'proto')
All inputs are finite; a program needn't handle non-finite values.
Results may differ from a plain program's by a relative error of at most 0.015.
Values may be sent and summed in bfloat16 or wider, within the bound.
No kernel may reach another device: no remote copies, remote signals or barrier semaphores. Data moves between devices by JAX's collectives and lax.ppermute only.
A program may use at most 256 MiB of HBM per device.

v0:
```python
import jax
import jax.numpy as jnp
from jax import lax
from jax.sharding import PartitionSpec as P

tau_teacher = 0.07
tau_student = 0.1
loss_scale = 1048576.0
norm_eps = 1e-06


def joined(part, axis, combine):
    gathered = jax.tree.map(lambda a: lax.all_gather(a, axis), part)

    def take(source):
        return jax.tree.map(lambda a: lax.dynamic_index_in_dim(a, source, 0, False), gathered)

    return lax.fori_loop(
        1, lax.axis_size(axis), lambda source, state: combine(state, take(source)), take(0)
    )


def gelu_parts(values):
    cumul = 0.5 * (1.0 + jax.scipy.special.erf(values * 0.7071067811865476))
    density = jnp.exp(-0.5 * values * values) * 0.3989422804014327
    return (values * cumul, cumul + values * density)


def inner(left, right):
    return lax.dot_general(
        left, right, (((0,), (0,)), ((), ())), preferred_element_type=jnp.float32
    )


def outer_last(left, right):
    return lax.dot_general(
        left, right, (((1,), (1,)), ((), ())), preferred_element_type=jnp.float32
    )


def normalize(values):
    recip = lax.rsqrt(jnp.sum(values * values, axis=1, keepdims=True) + norm_eps)
    return (recip, values * recip)


def teacher_norm(teacher_z):
    teach = teacher_z.astype(jnp.float32)
    return (teach * lax.rsqrt(jnp.sum(teach * teach, axis=1, keepdims=True) + norm_eps)).astype(
        jnp.bfloat16
    )


def back_norm(dnorm, recip, unit):
    return (recip * (dnorm - unit * jnp.sum(unit * dnorm, axis=1, keepdims=True))).astype(
        jnp.bfloat16
    )


def combine_stats(first, second):
    top_t = jnp.maximum(first[0], second[0])
    top_s = jnp.maximum(first[2], second[2])
    total_t = first[1] * jnp.exp(first[0] - top_t) + second[1] * jnp.exp(second[0] - top_t)
    total_s = first[3] * jnp.exp(first[2] - top_s) + second[3] * jnp.exp(second[2] - top_s)
    return (top_t, total_t, top_s, total_s)


def on_device(tokens, w_in, w_out, teacher_z, proto_student, proto_teacher, center, image_of):
    row_count = tokens.shape[0]
    images = row_count * lax.axis_size("row") // 128
    onehot = (image_of[:, None] == jnp.arange(images, dtype=jnp.int32)[None, :]).astype(jnp.float32)
    counts = lax.psum(jnp.sum(onehot, axis=0), "row")
    weight = 1.0 / (images * jnp.sum(onehot * counts[None, :], axis=1))
    pre = jnp.dot(
        tokens, lax.all_gather(w_in, "row", axis=0, tiled=True), preferred_element_type=jnp.float32
    )
    act, slope = gelu_parts(pre)
    hidden = act.astype(jnp.bfloat16)
    partial_value = jnp.dot(hidden, w_out, preferred_element_type=jnp.float32)
    bott = lax.psum(partial_value, "proto")
    recip, unit = normalize(bott)
    student_n = unit.astype(jnp.bfloat16)
    teacher_n = lax.all_gather(teacher_norm(teacher_z), "proto", axis=0, tiled=True)
    logit_t = (
        jnp.dot(teacher_n, proto_teacher, preferred_element_type=jnp.float32) - center[None, :]
    ) / tau_teacher
    logit_s = jnp.dot(student_n, proto_student, preferred_element_type=jnp.float32) / tau_student
    local_t = jnp.max(logit_t, axis=1)
    local_s = jnp.max(logit_s, axis=1)
    exp_t = jnp.exp(logit_t - local_t[:, None])
    exp_s = jnp.exp(logit_s - local_s[:, None])
    top_t, total_t, top_s, total_s = joined(
        (local_t, jnp.sum(exp_t, axis=1), local_s, jnp.sum(exp_s, axis=1)), "proto", combine_stats
    )
    exp_t = exp_t * jnp.exp(local_t - top_t)[:, None]
    exp_s = exp_s * jnp.exp(local_s - top_s)[:, None]
    prob_t = exp_t / total_t[:, None]
    prob_s = exp_s / total_s[:, None]
    logp_s = logit_s - top_s[:, None] - jnp.log(total_s)[:, None]
    cross = -jnp.sum(prob_t * logp_s, axis=1)
    loss = lax.psum(jnp.sum(weight * cross), ("row", "proto"))
    grad_s = (loss_scale * weight[:, None] * (prob_s - prob_t) / tau_student).astype(jnp.bfloat16)
    proto_grad = lax.psum_scatter(
        inner(student_n, grad_s).astype(jnp.bfloat16), "row", scatter_dimension=0, tiled=True
    ).astype(jnp.float32)
    dnorm_part = outer_last(grad_s, proto_student)
    dnorm = lax.psum(dnorm_part, "proto")
    dbott = back_norm(dnorm, recip, unit)
    w_out_grad = lax.psum(inner(hidden, dbott).astype(jnp.bfloat16), "row").astype(jnp.float32)
    dpre = (outer_last(dbott, w_out) * slope).astype(jnp.bfloat16)
    w_in_grad = lax.psum_scatter(
        inner(tokens, dpre).astype(jnp.bfloat16), "row", scatter_dimension=0, tiled=True
    ).astype(jnp.float32)
    return (loss, w_in_grad, w_out_grad, proto_grad)


def solution(mesh):
    return jax.shard_map(
        on_device,
        mesh=mesh,
        in_specs=(
            P("row", None),
            P("row", "proto"),
            P("proto", None),
            P(("row", "proto"), None),
            P(None, "proto"),
            P(None, "proto"),
            P("proto"),
            P("row"),
        ),
        out_specs=(P(), P("row", "proto"), P("proto", None), P("row", "proto")),
        check_vma=False,
    )
```

profile of v0, /device:TPU:0, one launch (start us, length us, event | category | flops | bytes accessed | tf_op | source)
XLA Modules:
  0.0 1063.1 jit_solution(12767168301606984746)
XLA Ops:
  7.2 0.0 all-gather.10.cloned.1.call-start
  7.2 0.7 all-gather.10.cloned.1.call-update
  7.9 0.0 all-reduce.4.cloned.1.call-start
  8.0 1.0 convert_reduce_fusion
  8.9 35.7 %psum.35 = f32[64]{0:T(128)S(1)} all-reduce(f32[64]{0:T(128)S(1)} %convert_reduce_fusion), channel_id=1, replica_groups=mesh['row'=16,'proto'=2] {'row'}, use_global_device_ids=true, to_apply=%region_1.0 | all-reduce | flops 64 | bytes 512 | tf_op jit(solution)/shard_map/psum | solution.py:71
  44.6 1.1 fusion.10
  45.7 1.0 fusion.11
  46.7 6.3 all_gather.30
  53.1 27.4 %fusion = (f32[512]{0:T(512)S(1)}, f32[512,24576]{1,0:T(8,128)}) fusion(f32[24576]{0:T(1024)} %param.14, bf16[512,384]{1,0:T(8,128)(2,1)S(1)} %all_gather.30, bf16[384,24576]{1,0:T(8,128)(2,1)} %param.13), kind=kOutput, calls=%fused_computation.6 | convolution fusion | flops 9701425152 | bytes 69699584 | tf_op jit(solution)/shard_map/dot_general | solution.py:84
  80.5 22.1 %fusion.2 = f32[512]{0:T(512)S(1)} fusion(f32[512,24576]{1,0:T(8,128)} %get-tuple-element.67, f32[512]{0:T(512)S(1)} %get-tuple-element.66, f32[24576]{0:T(1024)S(1)} %copy-done.1), kind=kLoop, calls=%fused_computation.9 | loop fusion | flops 50331136 | bytes 50434048 | tf_op jit(solution)/shard_map/reduce_sum | solution.py:92
  102.5 4.3 all-gather.5
  106.9 4.3 all-gather.4
  111.2 0.1 select_reduce_fusion
  111.3 69.3 %all-gather.10.cloned.1.call-done = bf16[4096,4096]{1,0:T(8,128)(2,1)} async-done(((bf16[256,4096]{1,0:T(8,128)(2,1)}), bf16[4096,4096]{1,0:T(8,128)(2,1)}) %all-gather.10.cloned.1.call-update) | async-done | bytes 33554448 | tf_op jit(solution)/shard_map/all_gather | solution.py:74
  180.6 24.4 %multiply_convert_fusion.1 = (bf16[512,4096]{1,0:T(8,128)(2,1)S(1)}, f32[512,4096]{1,0:T(8,128)}) fusion(bf16[512,4096]{1,0:T(8,128)(2,1)} %param.8, bf16[4096,4096]{1,0:T(8,128)(2,1)} %all-gather.10.cloned.1.call-done), kind=kOutput, calls=%fused_computation.19 | convolution fusion | flops 17190354944 | bytes 50331648 | tf_op jit(solution)/shard_map/dot_general | solution.py:73
  205.0 2.0 copy-done.5
  207.0 3.2 fusion.21
  210.2 0.0 all-reduce.4.cloned.1.call-update
  210.3 0.2 all-reduce.6.cloned.1.call-start
  210.6 34.5 %all-reduce.4.cloned.1.call-done = f32[512,384]{1,0:T(8,128)} async-done(((f32[512,384]{1,0:T(8,128)}), f32[512,384]{1,0:T(8,128)}) %all-reduce.4.cloned.1.call-update) | async-done | bytes 786448 | tf_op jit(solution)/shard_map/psum | solution.py:79
  245.1 1.3 multiply_reduce_fusion.3
  246.4 25.9 %multiply_reduce_fusion.1 = (f32[512]{0:T(512)S(1)}, f32[512,24576]{1,0:T(8,128)}) fusion(bf16[384,24576]{1,0:T(8,128)(2,1)} %param.12, f32[512,384]{1,0:T(8,128)} %all-reduce.4.cloned.1.call-done, f32[512]{0:T(512)S(1)} %add_rsqrt_fusion), kind=kOutput, calls=%fused_computation.8 | convolution fusion | flops 9689235456 | bytes 69996544 | tf_op jit(solution)/shard_map/dot_general | solution.py:86
  272.2 20.5 %fusion.1 = f32[512]{0:T(512)S(1)} fusion(f32[512,24576]{1,0:T(8,128)} %get-tuple-element.65, f32[512]{0:T(512)S(1)} %get-tuple-element.64), kind=kLoop, calls=%fused_computation.7 | loop fusion | flops 37748224 | bytes 50335744 | tf_op jit(solution)/shard_map/reduce_sum | solution.py:92
  292.7 4.3 all-gather.7
  297.1 4.3 all-gather.6
  301.4 48.7 %multiply_convert_fusion = (bf16[512,24576]{1,0:T(8,128)(2,1)}, f32[512]{0:T(512)S(1)}) fusion(f32[512,24576]{1,0:T(8,128)} %get-tuple-element.65, f32[512]{0:T(512)S(1)} %get-tuple-element.49, f32[512]{0:T(512)S(1)} %get-tuple-element.46, f32[512]{0:T(512)S(1)} %broadcast_multiply_fusion, f32[512]{0:T(512)S(1)} %get-tuple-element.64, ...), kind=kLoop, calls=%fused_computation | loop fusion | flops 213908992 | bytes 125947904 | tf_op jit(solution)/shard_map/convert_element_type | solution.py:101
  350.2 20.2 %fusion.22 = f32[512,384]{1,0:T(8,128)} fusion(bf16[512,24576]{1,0:T(8,128)(2,1)} %get-tuple-element.50, bf16[384,24576]{1,0:T(8,128)(2,1)} %param.12), kind=kOutput, calls=%fused_computation.53 | convolution fusion | flops 9663676416 | bytes 44826624 | tf_op jit(solution)/shard_map/dot_general | solution.py:36
  370.4 0.0 all-reduce.6.cloned.1.call-update
  370.4 0.3 all-reduce.8.cloned.1.call-start
  370.7 34.2 %all-reduce.6.cloned.1.call-done = f32[512,384]{1,0:T(8,128)} async-done(((f32[512,384]{1,0:T(8,128)}), f32[512,384]{1,0:T(8,128)}) %all-reduce.6.cloned.1.call-update) | async-done | bytes 786448 | tf_op jit(solution)/shard_map/psum | solution.py:106
  404.9 1.6 multiply_reduce_fusion.2
  406.5 1.6 multiply_convert_fusion.2
  408.1 6.2 convolution_convert_fusion.1
  414.4 0.0 all-reduce.8.cloned.1.call-update
  414.4 0.0 reduce-scatter.5.cloned.1.call-start
  414.5 21.3 %convolution_convert_fusion = bf16[384,24576]{1,0:T(8,128)(2,1)} fusion(bf16[512,24576]{1,0:T(8,128)(2,1)} %get-tuple-element.50, f32[512,384]{1,0:T(8,128)} %all-reduce.4.cloned.1.call-done, f32[512]{0:T(512)S(1)} %add_rsqrt_fusion), kind=kOutput, calls=%fused_computation.10 | convolution fusion | flops 9673506816 | bytes 44828672 | tf_op jit(solution)/shard_map/dot_general | solution.py:30
  435.8 0.0 reduce-scatter.5.cloned.1.call-update
  435.8 0.0 reduce-scatter.3.cloned.1.call-start
  435.8 28.1 %convert_bitcast_fusion = bf16[4096,4096]{0,1:T(8,128)(2,1)} fusion(bf16[512,4096]{1,0:T(8,128)(2,1)} %param.8, f32[512,4096]{1,0:T(8,128)} %get-tuple-element.63, bf16[512,384]{1,0:T(8,128)(2,1)S(1)} %multiply_convert_fusion.2, bf16[4096,384]{1,0:T(8,128)(2,1)S(1)} %copy-done), kind=kOutput, calls=%fused_computation.11 | convolution fusion | flops 18828230656 | bytes 49676288 | tf_op jit(solution)/shard_map/dot_general | solution.py:30
  463.9 0.6 copy-done.3
  464.6 0.6 multiply_reduce_fusion.4
  465.2 39.8 %psum.37 = f32[]{:T(128)} all-reduce(f32[]{:T(128)} %multiply_reduce_fusion.4), channel_id=1, replica_groups=mesh['row'=16,'proto'=2] {'row','proto'}, use_global_device_ids=true, to_apply=%region_12.13 | all-reduce | flops 1 | bytes 8 | tf_op jit(solution)/shard_map/psum | solution.py:100
  505.0 13.0 %all-reduce.8.cloned.1.call-done = bf16[4096,384]{1,0:T(8,128)(2,1)} async-done(((bf16[4096,384]{1,0:T(8,128)(2,1)}), bf16[4096,384]{1,0:T(8,128)(2,1)}) %all-reduce.8.cloned.1.call-update) | async-done | bytes 3145744 | tf_op jit(solution)/shard_map/psum | solution.py:108
  518.0 5.0 convert_element_type.57
  523.0 193.1 %reduce-scatter.5.cloned.1.call-done = bf16[24,24576]{1,0:T(8,128)(2,1)} async-done(((bf16[384,24576]{1,0:T(8,128)(2,1)}), bf16[24,24576]{1,0:T(8,128)(2,1)}) %reduce-scatter.5.cloned.1.call-update) | async-done | bytes 1179664 | tf_op jit(solution)/shard_map/reduce_scatter | solution.py:102
  716.1 2.8 convert_element_type.59
  718.9 333.1 %reduce-scatter.3.cloned.1.call-done = bf16[256,4096]{0,1:T(8,128)(2,1)} async-done(((bf16[4096,4096]{0,1:T(8,128)(2,1)}), bf16[256,4096]{0,1:T(8,128)(2,1)}) %reduce-scatter.3.cloned.1.call-update) | async-done | bytes 2097168 | tf_op jit(solution)/shard_map/reduce_scatter | solution.py:110
  1052.0 4.3 copy.14
  (21 shorter events, 0.1 us)
Async XLA Ops:
  7.2 199.9 %copy-start = (bf16[4096,384]{1,0:T(8,128)(2,1)S(1)}, bf16[4096,384]{1,0:T(8,128)(2,1)}, u32[]{:S(2)}) copy-start(bf16[4096,384]{1,0:T(8,128)(2,1)} %param.10) | copy-start | bytes 9437188
  7.2 173.4 %all-gather.10.cloned.1.call-start = ((), (), s32[]{:S(2)}) async-start(), calls=%async_computation.2 | async-start | bytes 35651584 | tf_op jit(solution)/shard_map/all_gather | solution.py:74
  7.9 237.1 %all-reduce.4.cloned.1.call-start = ((), (), s32[]{:S(2)}) async-start(), calls=%async_computation.3 | async-start | bytes 1572864 | tf_op jit(solution)/shard_map/psum | solution.py:79
  53.1 27.4 %copy-start.1 = (f32[24576]{0:T(1024)S(1)}, f32[24576]{0:T(1024)}, u32[]{:S(2)}) copy-start(f32[24576]{0:T(1024)} %param.14) | copy-start | bytes 294916
  80.5 30.7 %copy-start.4 = (s32[512]{0:T(512)S(1)}, s32[512]{0:T(512)}, u32[]{:S(2)}) copy-start(s32[512]{0:T(512)} %param.15) | copy-start | bytes 6148
  111.3 99.2 %copy-start.2 = (f32[512]{0:T(512)}, f32[512]{0:T(512)S(1)}, u32[]{:S(2)}) copy-start(f32[512]{0:T(512)S(1)} %select_reduce_fusion) | copy-start | bytes 6148
  205.0 2.0 copy-start.5
  210.3 194.7 %all-reduce.6.cloned.1.call-start = ((), (), s32[]{:S(2)}) async-start(), calls=%async_computation.4 | async-start | bytes 1572864 | tf_op jit(solution)/shard_map/psum | solution.py:106
  370.4 147.5 %all-reduce.8.cloned.1.call-start = ((), (), s32[]{:S(2)}) async-start(), calls=%async_computation.6 | async-start | bytes 6291456 | tf_op jit(solution)/shard_map/psum | solution.py:108
  414.4 301.7 %reduce-scatter.5.cloned.1.call-start = ((), (), s32[]{:S(2)}) async-start(), calls=%async_computation.7 | async-start | bytes 20054016 | tf_op jit(solution)/shard_map/reduce_scatter | solution.py:102
  435.8 616.2 %reduce-scatter.3.cloned.1.call-start = ((), (), s32[]{:S(2)}) async-start(), calls=%async_computation.5 | async-start | bytes 35651584 | tf_op jit(solution)/shard_map/reduce_scatter | solution.py:110
  463.9 0.7 copy-start.3
Sparse Core Ops, SparseCore 0:
  9.6 170.9 all-gather.9
  210.4 34.6 all-reduce.3
  370.6 34.3 all-reduce.5
  414.5 103.4 all-reduce.7
  522.0 194.1 reduce-scatter.4
  720.2 331.7 reduce-scatter.2
where the time goes:
time: 1060 us
  waiting for transfers between devices  678 us (64%)
  matrix products  157 us (15%)
  other arithmetic  107 us (10%)
  blocking collectives  99.2 us (9%)
  between operations  14.2 us (1%)
    reduce_scatter x1, waiting for transfers between devices, on_device(): lax.psum_scatter(inner(tokens, dpre).astype(jnp.bfloat16), 'row', scatter...  333 us
    reduce_scatter x1, waiting for transfers between devices, on_device(): lax.psum_scatter(inner(student_n, grad_s).astype(jnp.bfloat16), 'row', sc...  193 us
    all_gather x1, waiting for transfers between devices, on_device(): lax.all_gather(w_in, 'row', axis=0, tiled=True)  69.3 us
    dot_general x3, matrix products, inner(): lax.dot_general(left, right, (((0,), (0,)), ((), ())), preferred_element_...  55.6 us
    convert_element_type x1, other arithmetic, on_device(): (loss_scale * weight[:, None] * (prob_s - prob_t) / tau_student).astype(j...  48.7 us
    psum x1, blocking collectives, on_device(): loss = lax.psum(jnp.sum(weight * cross), ('row', 'proto'))  39.8 us
    psum x1, blocking collectives, on_device(): counts = lax.psum(jnp.sum(onehot, axis=0), 'row')  35.7 us
    psum x1, waiting for transfers between devices, on_device(): bott = lax.psum(partial_value, 'proto')  34.5 us
  transfers between devices with their start and end apart: 6, of which 6 were waited for; matrix products, arithmetic and copies ran while one was open for 10% of the time, Pallas kernels for 0%

commit v1 on v0

v1 whole, which is shorter than its diff:
```python
import functools
import math

import jax
import jax.numpy as jnp
from jax import lax
from jax.experimental import pallas as pl
from jax.experimental.pallas import tpu as pltpu
from jax.sharding import PartitionSpec as P

tau_teacher = 0.07
tau_student = 0.1
loss_scale = 1048576.0
norm_eps = 1e-06
log2e = 1.4426950408889634
bf16 = jnp.bfloat16
f32 = jnp.float32


def swap(value, bit, axis="row"):
    size = lax.axis_size(axis)
    return lax.ppermute(value, axis, [(i, i ^ bit) for i in range(size)])


def bits_of(size):
    return [1 << i for i in reversed(range(size.bit_length() - 1))]


def own_bit(axis, bit):
    return (lax.axis_index(axis) // bit) % 2


def halves(value, bit, axis, dim):
    half = value.shape[dim] // 2
    mine = own_bit(axis, bit)
    keep = lax.dynamic_slice_in_dim(value, mine * half, half, dim)
    send = lax.dynamic_slice_in_dim(value, (1 - mine) * half, half, dim)
    return keep, send


def in_order(own, other, bit, axis, dim):
    mine = own_bit(axis, bit)
    return jnp.where(
        mine == 0, jnp.concatenate([own, other], dim), jnp.concatenate([other, own], dim)
    )


def collect(value, axis, bits, dim):
    for bit in reversed(bits):
        value = in_order(value, swap(value, bit, axis), bit, axis, dim)
    return value


def tile_of(size, cap):
    best = 128
    for tile in range(128, cap + 1, 128):
        if size % tile == 0:
            best = tile
    return best


def log2_sum(first, second):
    top = jnp.maximum(first, second)
    return top + jnp.log2(jnp.exp2(first - top) + jnp.exp2(second - top))


def inner(left, right):
    return lax.dot_general(left, right, (((0,), (0,)), ((), ())), preferred_element_type=f32)


def outer_last(left, right):
    return lax.dot_general(left, right, (((1,), (1,)), ((), ())), preferred_element_type=f32)


def dot(left, right):
    return jnp.dot(left, right, preferred_element_type=f32)


def after(value, *others):
    return lax.optimization_barrier((value,) + others)[0] if others else value


def permute_body(order_ref, first_ref, second_ref, out_ref):
    rows, pair = first_ref.shape
    width = pair // 2
    flip = order_ref[0] % 2

    def place(low, high):
        for k, ref in enumerate((first_ref, second_ref)):
            at = pl.ds(k * rows, rows)
            out_ref[at, low : low + width] = ref[:, :width]
            out_ref[at, high : high + width] = ref[:, width:]

    @pl.when(flip == 0)
    def _():
        place(0, width)

    @pl.when(flip == 1)
    def _():
        place(width, 0)


def permute_columns(first, second, order):
    rows, columns = first.shape
    count = order.shape[0]
    width = 2 * columns // count
    block = pl.BlockSpec((rows, width), lambda j, order: (0, order[2 * j] // 2))
    return pl.pallas_call(
        permute_body,
        out_shape=jax.ShapeDtypeStruct((2 * rows, columns), first.dtype),
        grid_spec=pltpu.PrefetchScalarGridSpec(
            num_scalar_prefetch=1,
            grid=(count // 2,),
            in_specs=[block, block],
            out_specs=pl.BlockSpec((2 * rows, width), lambda j, order: (0, j)),
        ),
        compiler_params=pltpu.CompilerParams(vmem_limit_bytes=32 * 1024 * 1024),
        cost_estimate=pl.CostEstimate(
            flops=0, bytes_accessed=4 * rows * columns, transcendentals=0
        ),
        name="permute_columns",
    )(order, first, second)


def turn_body(in_ref, out_ref):
    out_ref[...] = in_ref[...].T


def turn_rows(value):
    rows, columns = value.shape
    wide = tile_of(columns, 512)
    return pl.pallas_call(
        turn_body,
        out_shape=jax.ShapeDtypeStruct((columns, rows), value.dtype),
        grid=(columns // wide,),
        in_specs=[pl.BlockSpec((rows, wide), lambda j: (0, j))],
        out_specs=pl.BlockSpec((wide, rows), lambda j: (j, 0)),
        compiler_params=pltpu.CompilerParams(vmem_limit_bytes=32 * 1024 * 1024),
        cost_estimate=pl.CostEstimate(
            flops=0, bytes_accessed=rows * columns, transcendentals=0
        ),
        name="turn_rows",
    )(value)


def grad_body(near_ref, far_ref, dnear_ref, dfar_ref, out_ref):
    total = dot(near_ref[...], dnear_ref[...]) + dot(far_ref[...], dfar_ref[...])
    out_ref[...] = total.astype(out_ref.dtype)


def grad_pass(near, far, dnear, dfar, piece, pieces):
    features, rows = near.shape
    wide = dnear.shape[1] // pieces
    high = tile_of(features, 512)
    block = pl.BlockSpec((high, rows), lambda i: (i, 0))
    strip = pl.BlockSpec((rows, wide), lambda i: (0, piece))
    return pl.pallas_call(
        grad_body,
        out_shape=jax.ShapeDtypeStruct((features, wide), bf16),
        grid=(features // high,),
        in_specs=[block, block, strip, strip],
        out_specs=pl.BlockSpec((high, wide), lambda i: (i, 0)),
        compiler_params=pltpu.CompilerParams(vmem_limit_bytes=32 * 1024 * 1024),
        cost_estimate=pl.CostEstimate(
            flops=features * rows * wide,
            bytes_accessed=2 * features * rows,
            transcendentals=0,
        ),
        name="grad_pass",
    )(near, far, dnear, dfar)


def softmax_body(scale, step, with_center, *refs):
    if with_center:
        _, n_ref, left_ref, center_ref, value_ref, e_ref, o_ref, lse_ref, logit = refs
    else:
        _, n_ref, left_ref, value_ref, e_ref, o_ref, lse_ref, logit = refs
    count = left_ref.shape[1]
    normed = n_ref[...]
    top = None
    for at in range(0, count, step):
        part = dot(normed, left_ref[:, at : at + step])
        if with_center:
            part = part - center_ref[:, at : at + step]
        logit[:, at : at + step] = part
        for k in range(0, step, 128):
            lanes = part[:, k : k + 128]
            top = lanes if top is None else jnp.maximum(top, lanes)
    top = jnp.max(top, axis=1, keepdims=True) * scale
    total, out = None, None
    for at in range(0, count, step):
        e = jnp.exp2(logit[:, at : at + step] * scale - top)
        for k in range(0, step, 128):
            lanes = e[:, k : k + 128]
            total = lanes if total is None else total + lanes
        low = e.astype(bf16)
        e_ref[:, at : at + step] = low
        product = outer_last(low, value_ref[:, at : at + step])
        out = product if out is None else out + product
    total = jnp.sum(total, axis=1, keepdims=True)
    o_ref[...] = out / total
    lane = lax.broadcasted_iota(jnp.int32, lse_ref.shape, 1)
    lse_ref[...] = jnp.where(lane == 0, top + jnp.log2(total), top)


def softmax_pass(normed, left, value, center, part, parts, tau):
    rows, width = normed.shape
    count = left.shape[1] // parts
    high = min(rows, 256)
    offset = part.astype(jnp.int32).reshape((1,))
    block = pl.BlockSpec((width, count), lambda i, off: (0, off[0]))
    by_row = lambda i, off: (i, 0)
    in_specs = [pl.BlockSpec((high, width), by_row), block]
    operands = [normed, left]
    if center is not None:
        in_specs.append(pl.BlockSpec((1, count), lambda i, off: (0, off[0])))
        operands.append(center.reshape((1, -1)))
    in_specs.append(block)
    operands.append(value)
    e, out, lse = pl.pallas_call(
        functools.partial(
            softmax_body, log2e / tau, tile_of(count, 1024), center is not None
        ),
        out_shape=(
            jax.ShapeDtypeStruct((rows, count), bf16),
            jax.ShapeDtypeStruct((rows, width), f32),
            jax.ShapeDtypeStruct((rows, 128), f32),
        ),
        grid_spec=pltpu.PrefetchScalarGridSpec(
            num_scalar_prefetch=1,
            grid=(rows // high,),
            in_specs=in_specs,
            out_specs=[
                pl.BlockSpec((high, count), by_row),
                pl.BlockSpec((high, width), by_row),
                pl.BlockSpec((high, 128), by_row),
            ],
            scratch_shapes=[pltpu.VMEM((high, count), f32)],
        ),
        compiler_params=pltpu.CompilerParams(vmem_limit_bytes=48 * 1024 * 1024),
        cost_estimate=pl.CostEstimate(
            flops=rows * width * count // 4,
            bytes_accessed=rows * count // 4,
            transcendentals=rows * count // 8,
        ),
        name="softmax_pass",
    )(offset, *operands)
    return e, out, lse[:, 0], lse[:, 1]


def head_body(rows_ref, early_ref, late_ref, w_ref, base_ref, hidden_ref, slope_ref, bott_ref):
    pre = early_ref[...] + dot(rows_ref[...], late_ref[...])
    size = jnp.abs(pre)
    gauss = jnp.exp2(pre * pre * (-0.5 * log2e))
    t = 1.0 / (1.0 + (0.3275911 * 0.7071067811865476) * size)
    poly = 1.061405429 * t - 1.453152027
    poly = poly * t + 1.421413741
    poly = poly * t - 0.284496736
    poly = poly * t + 0.254829592
    tail = (0.5 * poly) * t * gauss
    cumul = jnp.where(pre < 0.0, tail, 1.0 - tail)
    hidden = (pre * cumul).astype(bf16)
    hidden_ref[...] = hidden
    slope_ref[...] = (cumul + pre * gauss * 0.3989422804014327).astype(slope_ref.dtype)
    bott_ref[...] = base_ref[...] + dot(hidden, w_ref[...])


def head_pass(rows, early, late, w_out, base):
    count, wide = early.shape
    depth = late.shape[0]
    width = w_out.shape[1]
    last = rows.shape[1] // depth - 1
    high = min(count, 256)
    by_row = lambda i: (i, 0)
    whole = lambda i: (0, 0)
    return pl.pallas_call(
        head_body,
        out_shape=(
            jax.ShapeDtypeStruct((count, wide), bf16),
            jax.ShapeDtypeStruct((count, wide), bf16),
            jax.ShapeDtypeStruct((count, width), f32),
        ),
        grid=(count // high,),
        in_specs=[
            pl.BlockSpec((high, depth), lambda i: (i, last)),
            pl.BlockSpec((high, wide), by_row),
            pl.BlockSpec((depth, wide), whole),
            pl.BlockSpec((wide, width), whole),
            pl.BlockSpec((high, width), by_row),
        ],
        out_specs=[
            pl.BlockSpec((high, wide), by_row),
            pl.BlockSpec((high, wide), by_row),
            pl.BlockSpec((high, width), by_row),
        ],
        compiler_params=pltpu.CompilerParams(vmem_limit_bytes=32 * 1024 * 1024),
        cost_estimate=pl.CostEstimate(
            flops=2 * count * wide * (depth + width),
            bytes_accessed=8 * count * wide,
            transcendentals=2 * count * wide,
        ),
        name="head_pass",
    )(rows, early, late, w_out, base)


def proto_body(groups, n_ref, *refs):
    out_ref = refs[-1]
    total, at = None, 0
    for g in range(groups):
        es_ref, fs_ref, et_ref, ft_ref = refs[4 * g : 4 * g + 4]
        rows = es_ref.shape[0]
        grad = es_ref[...].astype(f32) * fs_ref[:, :1] - et_ref[...].astype(f32) * ft_ref[:, :1]
        product = dot(n_ref[:, at : at + rows], grad.astype(bf16))
        total = product if total is None else total + product
        at += rows
    out_ref[...] = total.astype(out_ref.dtype)


def proto_pass(turned, blocks, piece, pieces):
    width, rows = turned.shape
    count = blocks[0][0].shape[1]
    tile = tile_of(count // pieces, 512)
    tiles = count // pieces // tile
    first = piece * tiles
    whole = lambda j: (0, 0)
    strip = lambda j: (0, first + j)
    in_specs, operands = [pl.BlockSpec((width, rows), whole)], [turned]
    for block in blocks:
        for k, value in enumerate(block):
            if k % 2 == 0:
                in_specs.append(pl.BlockSpec((value.shape[0], tile), strip))
            else:
                in_specs.append(pl.BlockSpec(value.shape, whole))
            operands.append(value)
    return pl.pallas_call(
        functools.partial(proto_body, len(blocks)),
        out_shape=jax.ShapeDtypeStruct((width, count // pieces), bf16),
        grid=(tiles,),
        in_specs=in_specs,
        out_specs=pl.BlockSpec((width, tile), lambda j: (0, j)),
        compiler_params=pltpu.CompilerParams(vmem_limit_bytes=44 * 1024 * 1024),
        cost_estimate=pl.CostEstimate(
            flops=4 * rows * width * count // pieces,
            bytes_accessed=4 * rows * count // pieces,
            transcendentals=0,
        ),
        name="proto_pass",
    )(*operands)


def on_device(tokens, w_in, w_out, teacher_z, proto_student, proto_teacher, center, image_of):
    row_size = lax.axis_size("row")
    proto_size = lax.axis_size("proto")
    proto_bits = bits_of(proto_size)
    zhi, zlo, ybit, core = bits_of(row_size)
    row_index = lax.axis_index("row")
    proto_index = lax.axis_index("proto")
    part = own_bit("row", zlo) * 2 + own_bit("row", core)
    local = tokens.shape[0]
    features = tokens.shape[1]
    quarter = w_in.shape[1] // 4

    images = local * row_size // 128
    onehot = (image_of[:, None] == jnp.arange(images, dtype=jnp.int32)[None, :]).astype(f32)
    counts = jnp.sum(onehot, axis=0)
    for bit in (ybit, zhi, zlo, core):
        counts = counts + swap(counts, bit)

    def columns(index):
        return lax.dynamic_slice_in_dim(w_in, index * quarter, quarter, 1)

    chunks = 2 if quarter % 256 == 0 else 1
    chunk = quarter // chunks

    def cut(value, c):
        return lax.slice_in_dim(value, c * chunk, (c + 1) * chunk, axis=1)

    near, near_c = columns(part), columns(part ^ 1)
    far, far_c = columns(part ^ 2), columns(part ^ 3)
    from_core = after(swap(jnp.concatenate([near_c, far_c], 1), core), counts)
    mine = jnp.concatenate([near, from_core[:, :quarter]], 0)
    theirs = jnp.concatenate([far, from_core[:, quarter:]], 0)
    low = swap(theirs, zlo)
    own_h = [swap(cut(mine, 0), zhi)]
    for c in range(1, chunks):
        own_h.append(swap(after(cut(mine, c), own_h[-1]), zhi))
    own_y = swap(mine, ybit)

    strip = features // proto_size
    order = (jnp.arange(row_size, dtype=jnp.int32) ^ row_index).astype(jnp.int32)
    tokens_near = permute_columns(tokens, swap(tokens, core), order)

    def group_rows(value):
        value = collect(value, "proto", proto_bits, 0)
        far = swap(value, zlo)
        return [[value, swap(value, core)], [far, swap(far, core)]]

    def own_rows(value):
        for bit in proto_bits:
            value, _ = halves(value, bit, "proto", 0)
        return value

    def own_part(value, upto):
        for bit in proto_bits:
            if bit == upto:
                break
            value, _ = halves(value, bit, "proto", 0)
        return value

    def gather_passes(first, second, third):
        lse = jnp.stack([jnp.stack([first[2], third[2]]), second[2].reshape((2, local))])
        return [(p[0], p[3]) for p in (first, second, third)], (first[1], third[1]), lse

    def merge(near_out, far_out, lse):
        other = jnp.flip(swap(lse, zlo), 0)
        joint = log2_sum(lse, other)
        far_out = far_out.reshape((2, local, -1))
        out = [
            near_out[c] * jnp.exp2(lse[0, c] - joint[0, c])[:, None]
            + far_out[c].astype(f32) * jnp.exp2(other[0, c] - joint[0, c])[:, None]
            for c in (0, 1)
        ]
        lse = joint
        marks = [out[1]]
        got = swap(out[1].astype(bf16), core)
        other = jnp.flip(swap(lse, core), 1)
        joint = log2_sum(lse, other)
        out = (
            out[0] * jnp.exp2(lse[0, 0] - joint[0, 0])[:, None]
            + got.astype(f32) * jnp.exp2(other[0, 0] - joint[0, 0])[:, None]
        )
        lse = joint
        marks.append(out)
        own_lse = lse[0, 0]
        for bit in proto_bits:
            keep, given = halves(out, bit, "proto", 0)
            got = swap(given.astype(bf16), bit, "proto")
            other = swap(lse, bit, "proto")
            joint = log2_sum(lse, other)
            old, _ = halves(own_lse, bit, "proto", 0)
            new, _ = halves(own_part(joint[0, 0], bit), bit, "proto", 0)
            from_other, _ = halves(own_part(other[0, 0], bit), bit, "proto", 0)
            out = (
                keep * jnp.exp2(old - new)[:, None]
                + got.astype(f32) * jnp.exp2(from_other - new)[:, None]
            )
            lse = joint
            own_lse = new
        return out, own_lse, lse, marks

    teach = teacher_z.astype(f32)
    teacher_own = (
        teach * lax.rsqrt(jnp.sum(teach * teach, axis=1, keepdims=True) + norm_eps)
    ).astype(bf16)
    teacher_n = group_rows(teacher_own)
    run = functools.partial(
        softmax_pass,
        left=proto_teacher,
        value=proto_student,
        center=center,
        part=part,
        parts=4,
        tau=tau_teacher,
    )
    first = run(after(teacher_n[0][0], counts, tokens_near))
    low_y = swap(after(low, first[2]), ybit)
    third = run(after(teacher_n[0][1], first[2], own_y))
    piece = lax.dynamic_slice_in_dim(tokens, proto_index * strip, strip, 1)
    first_half = swap(after(piece[:, : strip // 2], low, third[2]), zlo)
    own_hy = [swap(value, ybit) for value in own_h]
    low_h = [swap(after(cut(low, 0), own_h[-1]), zhi)]
    second_half = swap(after(piece[:, strip // 2 :], first_half, own_h[-1]), zlo)
    turned_near = turn_rows(after(tokens_near, third[2]))
    second = run(after(jnp.concatenate(teacher_n[1], 0), third[2], *own_h, low_y, first_half, turned_near))
    far_t = swap(second[1].astype(bf16), zlo)
    low_h += [swap(after(cut(low, c), second[2]), zhi) for c in range(1, chunks)]
    low_hy = [swap(after(value, second[2]), ybit) for value in low_h]
    strips = [[first_half, second_half]]
    for bit in reversed(proto_bits):
        strips = strips + [[swap(value, bit, "proto") for value in pair] for pair in strips]
    tokens_far = jnp.concatenate([value for pair in strips for value in pair], 1)
    each = row_size // proto_size
    order_far = ((order // each) ^ proto_index) * each + order % each
    tokens_far = permute_columns(tokens_far, swap(tokens_far, core), order_far)
    et, near_t, lse_t = gather_passes(first, second, third)
    mean_t, _, lse_t, _ = merge(near_t, far_t, lse_t)

    weight = 1.0 / (images * jnp.sum(onehot * counts[None, :], axis=1))
    weight_far = swap(weight, zlo)
    pair = swap(jnp.stack([weight, weight_far]), core)
    weight = [[weight, pair[0]], [weight_far, pair[1]]]

    w_out_part = lax.dynamic_slice_in_dim(w_out, part * quarter, quarter, 0)
    slopes, hiddens = [[], []], [[], []]
    bott = [jnp.zeros((2 * local, w_out.shape[1]), f32)] * 2
    for c in range(chunks):
        early = [cut(value, c) for value in (mine, own_y, low, low_y)]
        early = jnp.concatenate(early + [own_h[c], own_hy[c]], 0)
        late = jnp.concatenate([low_h[c], low_hy[c]], 0)
        w_cut = w_out_part[c * chunk : (c + 1) * chunk]
        for z, rows in enumerate((tokens_near, tokens_far)):
            total = dot(rows[:, : early.shape[0]], early)
            hidden, slope, bott[z] = head_pass(rows, total, late, w_cut, bott[z])
            slopes[z].append(slope)
            hiddens[z].append(hidden)

    bott = [value[:local] + swap(value[local:], core) for value in bott]
    bott = bott[0] + swap(bott[1], zlo)
    for bit in proto_bits:
        keep, given = halves(bott, bit, "proto", 0)
        bott = keep + swap(given, bit, "proto")
    recip = lax.rsqrt(jnp.sum(bott * bott, axis=1, keepdims=True) + norm_eps)
    unit = bott * recip
    student_own = unit.astype(bf16)
    student_blocks = group_rows(student_own)
    run = functools.partial(
        softmax_pass,
        left=proto_student,
        value=proto_student,
        center=None,
        part=part,
        parts=4,
        tau=tau_student,
    )
    turned_far = turn_rows(tokens_far)
    first = run(after(student_blocks[0][0], turned_far))
    second = run(after(jnp.concatenate(student_blocks[1], 0), first[2]))
    far_s = swap(second[1].astype(bf16), zlo)
    third = run(after(student_blocks[0][1], second[2]))
    es, near_s, lse_s = gather_passes(first, second, third)
    mean_s, own_lse, lse_s, marks = merge(near_s, far_s, lse_s)

    weight_own = own_rows(weight[0][0])
    cross = own_lse / log2e - jnp.sum(student_own.astype(f32) * mean_t, axis=1) / tau_student
    loss = jnp.sum(weight_own * cross).reshape((1,))
    loss = loss + swap(loss, ybit)
    loss_y = loss
    loss = loss + swap(loss, zhi)

    coef = loss_scale / tau_student
    dnorm = (coef * weight_own)[:, None] * (mean_s - mean_t)
    dbott_own = (recip * (dnorm - unit * jnp.sum(unit * dnorm, axis=1, keepdims=True))).astype(bf16)
    dbott = group_rows(dbott_own)
    dbott = [jnp.concatenate(pair, 0) for pair in dbott]

    student_n = jnp.concatenate(
        [student_blocks[0][0], student_blocks[1][0], student_blocks[1][1], student_blocks[0][1]], 0
    )
    width = student_n.shape[1]
    share = width // row_size
    unit_index = jnp.arange(width, dtype=jnp.int32)
    source = ((unit_index // share) ^ row_index) * share + unit_index % share
    perm = (unit_index[:, None] == source[None, :]).astype(bf16)
    turned = lax.dot_general(
        perm, student_n, (((0,), (1,)), ((), ())), preferred_element_type=f32
    ).astype(bf16)

    def factors(passed, lse):
        out = []
        for (_, top), at in zip(passed, order_of):
            rows = jnp.concatenate([lse[z, c] for z, c in at])
            scale = jnp.concatenate([weight[z][c] for z, c in at])
            value = jnp.exp2(top - rows) * (coef * scale)
            out.append(jnp.broadcast_to(value[:, None], (value.shape[0], 128)))
        return out

    order_of = ([(0, 0)], [(1, 0), (1, 1)], [(0, 1)])
    scale_s = factors(es, lse_s)
    scale_t = factors(et, lse_t)
    count = es[0][0].shape[1]
    blocks = [(es[i][0], scale_s[i], et[i][0], scale_t[i]) for i in range(3)]

    def fold(value, ready=(), before=()):
        columns = value.shape[1]
        value = value.reshape((2, 2, 2, -1, columns))
        sent = swap(after(value[:, :, 1], *before), ybit)
        value = after(value[:, :, 0] + sent, *ready)
        value = value[0] + swap(value[1], zhi)
        value = value.reshape((2, 2, -1, columns))
        value = jnp.stack([value[:, 0], swap(value[:, 1], core)], 1)
        value = jnp.stack([value[0], swap(value[1], zlo)])
        return value.reshape((4, -1, columns)), sent

    def spread(pieces):
        whole = jnp.concatenate(pieces, 2)
        return jnp.concatenate(
            [lax.dynamic_index_in_dim(whole, part ^ q, 0, False) for q in range(4)], 1
        ).astype(f32)

    pieces = 2 if (count // 2) % 128 == 0 else 1
    proto_pieces, sent = [], []
    for i in range(pieces):
        value = proto_pass(after(turned, marks[i]), blocks, i, pieces)
        value, got = fold(value, tuple(dbott), (loss_y,))
        proto_pieces.append(value)
        sent.append(got)

    hidden = [jnp.concatenate(pair, 1) for pair in hiddens]
    w_out_grad = (inner(hidden[0], dbott[0]) + inner(hidden[1], dbott[1])).astype(bf16)
    product = w_out_grad
    loss = after(loss, product)
    for bit in (core, zlo):
        loss = loss + swap(loss, bit)
    for bit in proto_bits:
        loss = loss + swap(loss, bit, "proto")
    loss = loss[0]
    for bit in (ybit, zhi):
        keep, given = halves(w_out_grad, bit, "row", 0)
        w_out_grad = keep + swap(given, bit)
    for bit in (zhi, ybit):
        w_out_grad = in_order(w_out_grad, swap(w_out_grad, bit), bit, "row", 0)
    summed = w_out_grad
    w_out_grad = in_order(w_out_grad, swap(w_out_grad, zlo), zlo, "row", 0)
    w_out_grad = w_out_grad.reshape((2, 1, quarter, -1))
    w_out_grad = in_order(w_out_grad, swap(w_out_grad, core), core, "row", 1)
    w_out_grad = w_out_grad.reshape((4 * quarter, -1))

    w_in_pieces = []
    parts = 4 if quarter % 1024 == 0 else 2
    back = [
        outer_last(after(dbott[z], product), w_out_part)
        * jnp.concatenate(slopes[z], 1).astype(f32)
        for z in (0, 1)
    ]
    back = lax.optimization_barrier([value.astype(bf16) for value in back])
    grads = []
    for i in range(parts // 2):
        grad = grad_pass(turned_near, turned_far, *back, i, parts // 2)
        grads += jnp.split(grad, 2, axis=1)
    for i, grad in enumerate(grads):
        earlier = (sent[-2], summed) if i >= 2 else ()
        value, got = fold(grad, before=earlier)
        w_in_pieces.append(value)
        sent.append(got)
    return (loss, spread(w_in_pieces), w_out_grad.astype(f32), spread(proto_pieces))


def solution(mesh):
    return jax.shard_map(
        on_device,
        mesh=mesh,
        in_specs=(
            P("row", None),
            P("row", "proto"),
            P("proto", None),
            P(("row", "proto"), None),
            P(None, "proto"),
            P(None, "proto"),
            P("proto"),
            P("row"),
        ),
        out_specs=(P(), P("row", "proto"), P("proto", None), P("row", "proto")),
        check_vma=False,
    )
```

time: 1060 us -> 753 us (0.71); the launches traced: 1060 us -> 742 us
  waiting for transfers between devices: 678 us -> 326 us
  Pallas kernels: 0 us -> 185 us
  matrix products: 157 us -> 25.6 us
  blocking collectives: 99.2 us -> 0 us
  starting transfers between devices: 0.65 us -> 82.8 us
  local copies, waits for them, and re-layouts: 6.98 us -> 82.2 us
  other arithmetic: 107 us -> 32.5 us
    reduce_scatter x2 -> x0, waiting for transfers between devices: 526 us -> none  [the longest x1 333 us: on_device(): lax.psum_scatter(inner(tokens, dpre).astype(jnp.bfloat16), 'row', scatter...]
    ppermute x0 -> x87, waiting for transfers between devices: none -> 326 us  [swap(): return lax.ppermute(value, axis, [(i, i ^ bit) for i in range(size)])]
    pallas_call x0 -> x18, Pallas kernels: none -> 185 us  [the longest x6 99.1 us: softmax_pass(): pl.pallas_call(functools.partial(softmax_body, log2e / tau, tile_of(count...]
    ppermute x0 -> x87, starting transfers between devices: none -> 82.8 us  [swap(): return lax.ppermute(value, axis, [(i, i ^ bit) for i in range(size)])]
    psum x3 -> x0, waiting for transfers between devices: 81.7 us -> none  [the longest x1 34.5 us: on_device(): bott = lax.psum(partial_value, 'proto')]
    psum x2 -> x0, blocking collectives: 75.5 us -> none  [the longest x1 39.8 us: on_device(): loss = lax.psum(jnp.sum(weight * cross), ('row', 'proto'))]
    all_gather x1 -> x0, waiting for transfers between devices: 69.3 us -> none  [on_device(): lax.all_gather(w_in, 'row', axis=0, tiled=True)]
    dot_general x4 -> x5, matrix products: 80.9 us -> 20.4 us  [the longest x4 18.1 us: dot(): return jnp.dot(left, right, preferred_element_type=f32)]
  transfers between devices with their start and end apart: 6 -> 87, of which waited for: 6 -> 40; matrix products, arithmetic and copies ran while one was open for 10% -> 12% of each run, Pallas kernels for 0% -> 22%
where the time goes in v1:
time: 753 us; the launch traced here: 742 us
  waiting for transfers between devices  326 us (43%)
  Pallas kernels  185 us (25%)
  starting transfers between devices  82.8 us (11%)
  local copies, waits for them, and re-layouts  82.2 us (11%)
  other arithmetic  32.5 us (4%)
  matrix products  25.6 us (3%)
  between operations  8.02 us (1%)
    ppermute x87, waiting for transfers between devices, swap(): return lax.ppermute(value, axis, [(i, i ^ bit) for i in range(size)])  326 us
    pallas_call x6, Pallas kernels, softmax_pass(): pl.pallas_call(functools.partial(softmax_body, log2e / tau, tile_of(count...  99.1 us
    ppermute x87, starting transfers between devices, swap(): return lax.ppermute(value, axis, [(i, i ^ bit) for i in range(size)])  82.8 us
    unnamed x166, local copies, waits for them, and re-layouts  51.4 us
    pallas_call x2, Pallas kernels, proto_pass(): pl.pallas_call(functools.partial(proto_body, len(blocks)), out_shape=jax....  25.6 us
    pallas_call x2, Pallas kernels, grad_pass(): pl.pallas_call(grad_body, out_shape=jax.ShapeDtypeStruct((features, wide)...  23 us
    dot_general x4, matrix products, dot(): return jnp.dot(left, right, preferred_element_type=f32)  18.1 us
    pallas_call x4, Pallas kernels, head_pass(): pl.pallas_call(head_body, out_shape=(jax.ShapeDtypeStruct((count, wide),...  16.6 us
  transfers between devices with their start and end apart: 87, of which 40 were waited for; matrix products, arithmetic and copies ran while one was open for 12% of the time, Pallas kernels for 22%

profile of v1, /device:TPU:0, one launch (start us, length us, event | category | flops | bytes accessed | tf_op | source)
XLA Modules:
  0.0 741.9 jit_solution(16882650796356746116)
XLA Ops:
  33.4 6.1 permute_columns.2.in_ref.rows_ref
  42.7 13.2 %softmax_pass.6 = (bf16[512,6144]{1,0:T(8,128)(2,1)}, f32[512,384]{1,0:T(8,128)S(1)}, f32[512,128]{1,0:T(8,128)S(1)}) custom-call(s32[1]{0:T(128)} %bitcast.refs_0_, bf16[512,384]{1,0:T(8,128)(2,1)S(1)} %maximum_select_fusion.3.refs_1_, bf16[384,24576]{1,0:T(8,128)(2,1)} %refs_2_.8, f32[1,24576]{1,0:T(1,128)S(1)} %bitcast.246, bf16[384,24576]{1,0:T(8,128)(2,1)} %refs_3_.5), custom_call_target="tpu_custom_call" | custom-call | flops 301989888 | bytes 786432 | tf_op jit(solution)/shard_map/softmax_pass/pallas_call | solution.py:220
  57.5 13.2 %softmax_pass.7 = (bf16[512,6144]{1,0:T(8,128)(2,1)}, f32[512,384]{1,0:T(8,128)S(1)}, f32[512,128]{1,0:T(8,128)S(1)}) custom-call(s32[1]{0:T(128)} %bitcast.refs_0_, bf16[512,384]{1,0:T(8,128)(2,1)S(1)} %collective-permute-done.15.refs_1_, bf16[384,24576]{1,0:T(8,128)(2,1)} %refs_2_.8, f32[1,24576]{1,0:T(1,128)S(1)} %bitcast.247, bf16[384,24576]{1,0:T(8,128)(2,1)} %refs_3_.5), custom_call_target="tpu_custom_call" | custom-call | flops 301989888 | bytes 786432 | tf_op jit(solution)/shard_map/softmax_pass/pallas_call | solution.py:220
  71.7 33.7 %collective-permute-done.11 = bf16[512,512]{1,0:T(8,128)(2,1)} collective-permute-done((bf16[512,512]{1,0:T(8,128)(2,1)S(1)}, bf16[512,512]{1,0:T(8,128)(2,1)}, u32[]{:S(2)}, u32[]{:S(2)}) %collective-permute-start.11) | collective-permute-done | bytes 524320 | tf_op jit(solution)/shard_map/ppermute | solution.py:22
  109.5 22.7 %collective-permute-done.23 = bf16[512,1024]{1,0:T(8,128)(2,1)S(1)} collective-permute-done((bf16[512,1024]{1,0:T(8,128)(2,1)S(1)}, bf16[512,1024]{1,0:T(8,128)(2,1)S(1)}, u32[]{:S(2)}, u32[]{:S(2)}) %collective-permute-start.23) | collective-permute-done | bytes 1048608 | tf_op jit(solution)/shard_map/ppermute | solution.py:22
  137.2 18.6 %collective-permute-done.25 = bf16[512,1024]{1,0:T(8,128)(2,1)S(1)} collective-permute-done((bf16[512,1024]{1,0:T(8,128)(2,1)S(1)}, bf16[512,1024]{1,0:T(8,128)(2,1)S(1)}, u32[]{:S(2)}, u32[]{:S(2)}) %collective-permute-start.25) | collective-permute-done | bytes 1048608 | tf_op jit(solution)/shard_map/ppermute | solution.py:22
  167.3 19.8 %collective-permute-done.20 = bf16[512,512]{1,0:T(8,128)(2,1)} collective-permute-done((bf16[512,512]{1,0:T(8,128)(2,1)S(1)}, bf16[512,512]{1,0:T(8,128)(2,1)}, u32[]{:S(2)}, u32[]{:S(2)}) %collective-permute-start.20) | collective-permute-done | bytes 524320 | tf_op jit(solution)/shard_map/ppermute | solution.py:22
  191.6 3.5 turn_rows.2.near_ref
  198.4 22.9 %softmax_pass.8 = (bf16[1024,6144]{1,0:T(8,128)(2,1)}, f32[1024,384]{1,0:T(8,128)S(1)}, f32[1024,128]{1,0:T(8,128)S(1)}) custom-call(s32[1]{0:T(128)} %bitcast.refs_0_, bf16[1024,384]{1,0:T(8,128)(2,1)S(1)} %pad_maximum_fusion.4.refs_1_, bf16[384,24576]{1,0:T(8,128)(2,1)} %refs_2_.8, f32[1,24576]{1,0:T(1,128)S(1)} %bitcast.248, bf16[384,24576]{1,0:T(8,128)(2,1)} %refs_3_.5), custom_call_target="tpu_custom_call" | custom-call | flops 603979776 | bytes 1572864 | tf_op jit(solution)/shard_map/softmax_pass/pallas_call | solution.py:220
  226.6 6.6 fusion.4.early_ref
  236.5 10.2 %collective-permute-done.17 = bf16[512,512]{1,0:T(8,128)(2,1)S(1)} collective-permute-done((bf16[512,512]{1,0:T(8,128)(2,1)}, bf16[512,512]{1,0:T(8,128)(2,1)S(1)}, u32[]{:S(2)}, u32[]{:S(2)}) %collective-permute-start.17) | collective-permute-done | bytes 524320 | tf_op jit(solution)/shard_map/ppermute | solution.py:22
  252.1 8.3 %collective-permute-done.18 = bf16[512,512]{1,0:T(8,128)(2,1)S(1)} collective-permute-done((bf16[512,512]{1,0:T(8,128)(2,1)S(1)}, bf16[512,512]{1,0:T(8,128)(2,1)S(1)}, u32[]{:S(2)}, u32[]{:S(2)}) %collective-permute-start.18) | collective-permute-done | bytes 524320 | tf_op jit(solution)/shard_map/ppermute | solution.py:22
  260.5 7.4 permute_columns.3.rows_ref.in_ref
  268.0 3.4 fusion.early_ref
  272.2 3.4 fusion.2.early_ref
  275.7 4.5 head_pass.6
  284.7 4.0 head_pass.7
  289.8 4.7 fusion.6.early_ref
  304.5 4.0 head_pass.4
  313.9 4.0 head_pass.5
  323.7 16.0 %collective-permute-done.28 = f32[512,384]{1,0:T(8,128)S(1)} collective-permute-done((f32[512,384]{1,0:T(8,128)S(1)}, f32[512,384]{1,0:T(8,128)S(1)}, u32[]{:S(2)}, u32[]{:S(2)}) %collective-permute-start.28) | collective-permute-done | bytes 786464 | tf_op jit(solution)/shard_map/ppermute | solution.py:22
  343.5 8.5 %collective-permute-done.29 = f32[256,384]{1,0:T(8,128)S(1)} collective-permute-done((f32[256,384]{1,0:T(8,128)S(1)}, f32[256,384]{1,0:T(8,128)S(1)}, u32[]{:S(2)}, u32[]{:S(2)}) %collective-permute-start.29) | collective-permute-done | bytes 393248 | tf_op jit(solution)/shard_map/ppermute | solution.py:22
  365.9 3.4 copy-done.1
  369.3 3.5 turn_rows.3.far_ref
  376.6 13.5 %softmax_pass.9 = (bf16[512,6144]{1,0:T(8,128)(2,1)}, f32[512,384]{1,0:T(8,128)S(1)}, f32[512,128]{1,0:T(8,128)S(1)}) custom-call(s32[1]{0:T(128)} %bitcast.refs_0_, bf16[512,384]{1,0:T(8,128)(2,1)S(1)} %maximum_select_fusion.4.refs_1_, bf16[384,24576]{1,0:T(8,128)(2,1)} %refs_3_.5, bf16[384,24576]{1,0:T(8,128)(2,1)} %refs_3_.5), custom_call_target="tpu_custom_call" | custom-call | flops 301989888 | bytes 786432 | tf_op jit(solution)/shard_map/softmax_pass/pallas_call | solution.py:220
  392.2 13.3 %softmax_pass.10 = (bf16[512,6144]{1,0:T(8,128)(2,1)}, f32[512,384]{1,0:T(8,128)S(1)}, f32[512,128]{1,0:T(8,128)S(1)}) custom-call(s32[1]{0:T(128)} %bitcast.refs_0_, bf16[512,384]{1,0:T(8,128)(2,1)S(1)} %copy-done.31, bf16[384,24576]{1,0:T(8,128)(2,1)} %refs_3_.5, bf16[384,24576]{1,0:T(8,128)(2,1)} %refs_3_.5), custom_call_target="tpu_custom_call" | custom-call | flops 301989888 | bytes 786432 | tf_op jit(solution)/shard_map/softmax_pass/pallas_call | solution.py:220
  406.6 23.0 %softmax_pass.11 = (bf16[1024,6144]{1,0:T(8,128)(2,1)}, f32[1024,384]{1,0:T(8,128)S(1)}, f32[1024,128]{1,0:T(8,128)S(1)}) custom-call(s32[1]{0:T(128)} %bitcast.refs_0_, bf16[1024,384]{1,0:T(8,128)(2,1)S(1)} %pad_maximum_fusion.5.refs_1_, bf16[384,24576]{1,0:T(8,128)(2,1)} %refs_3_.5, bf16[384,24576]{1,0:T(8,128)(2,1)} %refs_3_.5), custom_call_target="tpu_custom_call" | custom-call | flops 603979776 | bytes 1572864 | tf_op jit(solution)/shard_map/softmax_pass/pallas_call | solution.py:220
  465.1 12.7 %proto_pass.2 = bf16[384,3072]{1,0:T(8,128)(2,1)S(1)} custom-call(bf16[384,2048]{1,0:T(8,128)(2,1)S(1)} %convolution_convert_fusion.n_ref, bf16[512,6144]{1,0:T(8,128)(2,1)} %get-tuple-element.107.refs_0_, f32[512,128]{1,0:T(8,128)S(1)} %broadcast_in_dim.28.refs_1_, bf16[512,6144]{1,0:T(8,128)(2,1)} %get-tuple-element.108.refs_2_, ...), custom_call_target="tpu_custom_call" | custom-call | flops 9663676416 | bytes 25165824 | tf_op jit(solution)/shard_map/proto_pass/pallas_call | solution.py:335
  481.6 5.2 collective-permute-done.47
  488.8 12.9 %proto_pass.3 = bf16[384,3072]{1,0:T(8,128)(2,1)S(1)} custom-call(bf16[384,2048]{1,0:T(8,128)(2,1)S(1)} %convolution_convert_fusion.n_ref, bf16[512,6144]{1,0:T(8,128)(2,1)} %get-tuple-element.107.refs_0_, f32[512,128]{1,0:T(8,128)S(1)} %broadcast_in_dim.28.refs_1_, bf16[512,6144]{1,0:T(8,128)(2,1)} %get-tuple-element.108.refs_2_, ...), custom_call_target="tpu_custom_call" | custom-call | flops 9663676416 | bytes 25165824 | tf_op jit(solution)/shard_map/proto_pass/pallas_call | solution.py:335
  502.7 9.7 %collective-permute-done.50 = bf16[512,384]{1,0:T(8,128)(2,1)S(1)} collective-permute-done((bf16[512,384]{1,0:T(8,128)(2,1)S(1)}, bf16[512,384]{1,0:T(8,128)(2,1)S(1)}, u32[]{:S(2)}, u32[]{:S(2)}) %collective-permute-start.50) | collective-permute-done | bytes 393248 | tf_op jit(solution)/shard_map/ppermute | solution.py:22
  521.2 11.4 %grad_pass.3 = bf16[4096,512]{1,0:T(8,128)(2,1)S(1)} custom-call(bf16[4096,1024]{1,0:T(8,128)(2,1)S(1)} %bitcast.241, bf16[4096,1024]{1,0:T(8,128)(2,1)} %copy-done.7, bf16[1024,1024]{1,0:T(8,128)(2,1)S(1)} %multiply_convert_fusion.1.dnear_ref, bf16[1024,1024]{1,0:T(8,128)(2,1)S(1)} %multiply_convert_fusion.dfar_ref), custom_call_target="tpu_custom_call" | custom-call | flops 2147483648 | bytes 8388608 | tf_op jit(solution)/shard_map/grad_pass/pallas_call | solution.py:157
  532.6 11.7 %grad_pass.2 = bf16[4096,512]{1,0:T(8,128)(2,1)S(1)} custom-call(bf16[4096,1024]{1,0:T(8,128)(2,1)S(1)} %bitcast.241, bf16[4096,1024]{1,0:T(8,128)(2,1)} %copy-done.7, bf16[1024,1024]{1,0:T(8,128)(2,1)S(1)} %multiply_convert_fusion.1.dnear_ref, bf16[1024,1024]{1,0:T(8,128)(2,1)S(1)} %multiply_convert_fusion.dfar_ref), custom_call_target="tpu_custom_call" | custom-call | flops 2147483648 | bytes 8388608 | tf_op jit(solution)/shard_map/grad_pass/pallas_call | solution.py:157
  550.3 7.4 collective-permute-done.63
  559.4 4.6 collective-permute-start.53
  571.6 24.1 %collective-permute-done.64 = bf16[256,384]{1,0:T(8,128)(2,1)S(1)} collective-permute-done((bf16[256,384]{1,0:T(8,128)(2,1)S(1)}, bf16[256,384]{1,0:T(8,128)(2,1)S(1)}, u32[]{:S(2)}, u32[]{:S(2)}) %collective-permute-start.64) | collective-permute-done | bytes 196640 | tf_op jit(solution)/shard_map/ppermute | solution.py:22
  596.1 16.5 %collective-permute-done.84 = bf16[2,48,3072]{2,1,0:T(8,128)(2,1)S(1)} collective-permute-done((bf16[2,48,3072]{2,1,0:T(8,128)(2,1)S(1)}, bf16[2,48,3072]{2,1,0:T(8,128)(2,1)S(1)}, u32[]{:S(2)}, u32[]{:S(2)}) %collective-permute-start.84) | collective-permute-done | bytes 589856 | tf_op jit(solution)/shard_map/ppermute | solution.py:22
  612.8 3.9 collective-permute-done.65
  624.1 3.9 collective-permute-done.66
  628.4 9.0 %collective-permute-done.82 = bf16[2,24,3072]{2,1,0:T(8,128)(2,1)S(1)} collective-permute-done((bf16[2,24,3072]{2,1,0:T(8,128)(2,1)S(1)}, bf16[2,24,3072]{2,1,0:T(8,128)(2,1)S(1)}, u32[]{:S(2)}, u32[]{:S(2)}) %collective-permute-start.82) | collective-permute-done | bytes 294944 | tf_op jit(solution)/shard_map/ppermute | solution.py:22
  638.0 5.7 collective-permute-done.86
  646.0 13.3 %collective-permute-done.56 = bf16[2,512,256]{2,1,0:T(8,128)(2,1)S(1)} collective-permute-done((bf16[2,512,256]{2,1,0:T(8,128)(2,1)S(1)}, bf16[2,512,256]{2,1,0:T(8,128)(2,1)S(1)}, u32[]{:S(2)}, u32[]{:S(2)}) %collective-permute-start.56) | collective-permute-done | bytes 524320 | tf_op jit(solution)/shard_map/ppermute | solution.py:22
  659.5 9.2 %collective-permute-done.60 = bf16[2,512,256]{2,1,0:T(8,128)(2,1)S(1)} collective-permute-done((bf16[2,512,256]{2,1,0:T(8,128)(2,1)S(1)}, bf16[2,512,256]{2,1,0:T(8,128)(2,1)S(1)}, u32[]{:S(2)}, u32[]{:S(2)}) %collective-permute-start.60) | collective-permute-done | bytes 524320 | tf_op jit(solution)/shard_map/ppermute | solution.py:22
  670.6 11.9 %collective-permute-done.71 = bf16[2,2,512,256]{3,2,1,0:T(8,128)(2,1)S(1)} collective-permute-done((bf16[2,2,512,256]{3,2,1,0:T(8,128)(2,1)S(1)}, bf16[2,2,512,256]{3,2,1,0:T(8,128)(2,1)S(1)}, u32[]{:S(2)}, u32[]{:S(2)}) %collective-permute-start.71) | collective-permute-done | bytes 1048608 | tf_op jit(solution)/shard_map/ppermute | solution.py:22
  685.9 21.5 %collective-permute-done.68 = bf16[2,512,256]{2,1,0:T(8,128)(2,1)S(1)} collective-permute-done((bf16[2,512,256]{2,1,0:T(8,128)(2,1)S(1)}, bf16[2,512,256]{2,1,0:T(8,128)(2,1)S(1)}, u32[]{:S(2)}, u32[]{:S(2)}) %collective-permute-start.68) | collective-permute-done | bytes 524320 | tf_op jit(solution)/shard_map/ppermute | solution.py:22
  707.6 10.6 %collective-permute-done.72 = bf16[2,512,256]{2,1,0:T(8,128)(2,1)S(1)} collective-permute-done((bf16[2,512,256]{2,1,0:T(8,128)(2,1)S(1)}, bf16[2,512,256]{2,1,0:T(8,128)(2,1)S(1)}, u32[]{:S(2)}, u32[]{:S(2)}) %collective-permute-start.72) | collective-permute-done | bytes 524320 | tf_op jit(solution)/shard_map/ppermute | solution.py:22
  721.9 6.9 collective-permute-done.70
  728.8 4.6 collective-permute-done.74
  (481 shorter events, 221.6 us)
Async XLA Ops:
  0.6 32.7 %collective-permute-start.4 = (bf16[512,4096]{1,0:T(8,128)(2,1)}, bf16[512,4096]{1,0:T(8,128)(2,1)}, u32[]{:S(2)}, u32[]{:S(2)}) collective-permute-start(bf16[512,4096]{1,0:T(8,128)(2,1)} %first_ref.1), channel_id=1, source_target_pairs={{0,2},{2,0},{4,6},{6,4},{8,10},{10,8},{12,14},{14,12},{16,18},{18,... | collective-permute-start | bytes 12582920 | tf_op jit(solution)/shard_map/ppermute | solution.py:22
  18.2 39.3 %collective-permute-start.6 = (bf16[512,1024]{1,0:T(8,128)(2,1)}, bf16[512,1024]{1,0:T(8,128)(2,1)}, u32[]{:S(2)}, u32[]{:S(2)}) collective-permute-start(bf16[512,1024]{1,0:T(8,128)(2,1)} %pad_maximum_fusion.1), channel_id=1, source_target_pairs={{0,4},{2,6},{4,0},{6,2},{8,12},{10,14},{12,8},{14,10},{16,20},{18,... | collective-permute-start | bytes 3145736 | tf_op jit(solution)/shard_map/ppermute | solution.py:22
  21.1 49.7 %collective-permute-start.7 = (bf16[512,1024]{1,0:T(8,128)(2,1)}, bf16[512,1024]{1,0:T(8,128)(2,1)S(1)}, u32[]{:S(2)}, u32[]{:S(2)}) collective-permute-start(bf16[512,1024]{1,0:T(8,128)(2,1)} %pad_maximum_fusion.3), channel_id=1, source_target_pairs={{0,8},{2,10},{4,12},{6,14},{8,0},{10,2},{12,4},{14,6},{16,24},{18,... | collective-permute-start | bytes 3145736 | tf_op jit(solution)/shard_map/ppermute | solution.py:22
  29.4 27.5 %collective-permute-start.15 = (bf16[512,384]{1,0:T(8,128)(2,1)S(1)}, bf16[512,384]{1,0:T(8,128)(2,1)S(1)}, u32[]{:S(2)}, u32[]{:S(2)}) collective-permute-start(bf16[512,384]{1,0:T(8,128)(2,1)S(1)} %maximum_select_fusion.3.refs_1_), channel_id=1, source_target_pairs={{0,2},{2,0},{4,6},{6,4},{8,10},{10,8},{12,14},{14,12},{16,18},{18,... | collective-permute-start | bytes 1179656 | tf_op jit(solution)/shard_map/ppermute | solution.py:22
  30.8 40.5 %collective-permute-start.10 = (bf16[512,512]{1,0:T(8,128)(2,1)}, bf16[512,512]{1,0:T(8,128)(2,1)S(1)}, u32[]{:S(2)}, u32[]{:S(2)}) collective-permute-start(bf16[512,512]{1,0:T(8,128)(2,1)} %get-tuple-element.167), channel_id=1, source_target_pairs={{0,16},{2,18},{4,20},{6,22},{8,24},{10,26},{12,28},{14,30},{16,0},... | collective-permute-start | bytes 1572872 | tf_op jit(solution)/shard_map/ppermute | solution.py:22
  70.8 36.7 %collective-permute-start.16 = (bf16[512,1024]{1,0:T(8,128)(2,1)S(1)}, bf16[512,1024]{1,0:T(8,128)(2,1)S(1)}, u32[]{:S(2)}, u32[]{:S(2)}) collective-permute-start(bf16[512,1024]{1,0:T(8,128)(2,1)S(1)} %get-tuple-element.68), channel_id=1, source_target_pairs={{0,8},{2,10},{4,12},{6,14},{8,0},{10,2},{12,4},{14,6},{16,24},{18,... | collective-permute-start | bytes 3145736 | tf_op jit(solution)/shard_map/ppermute | solution.py:22
  71.3 34.1 %collective-permute-start.11 = (bf16[512,512]{1,0:T(8,128)(2,1)S(1)}, bf16[512,512]{1,0:T(8,128)(2,1)}, u32[]{:S(2)}, u32[]{:S(2)}) collective-permute-start(bf16[512,512]{1,0:T(8,128)(2,1)S(1)} %get-tuple-element.65), channel_id=1, source_target_pairs={{0,16},{2,18},{4,20},{6,22},{8,24},{10,26},{12,28},{14,30},{16,0},... | collective-permute-start | bytes 1572872 | tf_op jit(solution)/shard_map/ppermute | solution.py:22
  107.5 24.6 %collective-permute-start.23 = (bf16[512,1024]{1,0:T(8,128)(2,1)S(1)}, bf16[512,1024]{1,0:T(8,128)(2,1)S(1)}, u32[]{:S(2)}, u32[]{:S(2)}) collective-permute-start(bf16[512,1024]{1,0:T(8,128)(2,1)S(1)} %get-tuple-element.78), channel_id=1, source_target_pairs={{0,8},{2,10},{4,12},{6,14},{8,0},{10,2},{12,4},{14,6},{16,24},{18,... | collective-permute-start | bytes 3145736 | tf_op jit(solution)/shard_map/ppermute | solution.py:22
  108.0 28.2 %collective-permute-start.24 = (bf16[512,1024]{1,0:T(8,128)(2,1)S(1)}, bf16[512,1024]{1,0:T(8,128)(2,1)S(1)}, u32[]{:S(2)}, u32[]{:S(2)}) collective-permute-start(bf16[512,1024]{1,0:T(8,128)(2,1)S(1)} %collective-permute-done.16), channel_id=1, source_target_pairs={{0,1},{1,0},{2,3},{3,2},{4,5},{5,4},{6,7},{7,6},{8,9},{9,8},{10,11... | collective-permute-start | bytes 3145736 | tf_op jit(solution)/shard_map/ppermute | solution.py:22
  132.2 23.7 %collective-permute-start.25 = (bf16[512,1024]{1,0:T(8,128)(2,1)S(1)}, bf16[512,1024]{1,0:T(8,128)(2,1)S(1)}, u32[]{:S(2)}, u32[]{:S(2)}) collective-permute-start(bf16[512,1024]{1,0:T(8,128)(2,1)S(1)} %collective-permute-done.23), channel_id=1, source_target_pairs={{0,1},{1,0},{2,3},{3,2},{4,5},{5,4},{6,7},{7,6},{8,9},{9,8},{10,11... | collective-permute-start | bytes 3145736 | tf_op jit(solution)/shard_map/ppermute | solution.py:22
  133.7 23.3 %collective-permute-start.13 = (bf16[512,384]{1,0:T(8,128)(2,1)S(1)}, bf16[512,384]{1,0:T(8,128)(2,1)}, u32[]{:S(2)}, u32[]{:S(2)}) collective-permute-start(bf16[512,384]{1,0:T(8,128)(2,1)S(1)} %maximum_select_fusion.3.refs_1_), channel_id=1, source_target_pairs={{0,8},{2,10},{4,12},{6,14},{8,0},{10,2},{12,4},{14,6},{16,24},{18,... | collective-permute-start | bytes 1179656 | tf_op jit(solution)/shard_map/ppermute | solution.py:22
  156.9 103.6 %collective-permute-start.26 = (bf16[512,4096]{1,0:T(8,128)(2,1)}, bf16[512,4096]{1,0:T(8,128)(2,1)}, u32[]{:S(2)}, u32[]{:S(2)}) collective-permute-start(bf16[512,4096]{1,0:T(8,128)(2,1)} %constant_dynamic-update-slice_fusion.12.first_ref), channel_id=1, source_target_pairs={{0,2},{2,0},{4,6},{6,4},{8,10},{10,8},{12,14},{14,12},{16,18},{18,... | collective-permute-start | bytes 12582920 | tf_op jit(solution)/shard_map/ppermute | solution.py:22
  159.7 38.7 %collective-permute-start.9 = (bf16[512,1024]{1,0:T(8,128)(2,1)S(1)}, bf16[512,1024]{1,0:T(8,128)(2,1)}, u32[]{:S(2)}, u32[]{:S(2)}) collective-permute-start(bf16[512,1024]{1,0:T(8,128)(2,1)S(1)} %collective-permute-done.7), channel_id=1, source_target_pairs={{0,4},{2,6},{4,0},{6,2},{8,12},{10,14},{12,8},{14,10},{16,20},{18,... | collective-permute-start | bytes 3145736 | tf_op jit(solution)/shard_map/ppermute | solution.py:22
  161.4 25.7 %collective-permute-start.20 = (bf16[512,512]{1,0:T(8,128)(2,1)S(1)}, bf16[512,512]{1,0:T(8,128)(2,1)}, u32[]{:S(2)}, u32[]{:S(2)}) collective-permute-start(bf16[512,512]{1,0:T(8,128)(2,1)S(1)} %get-tuple-element.74), channel_id=1, source_target_pairs={{0,16},{2,18},{4,20},{6,22},{8,24},{10,26},{12,28},{14,30},{16,0},... | collective-permute-start | bytes 1572872 | tf_op jit(solution)/shard_map/ppermute | solution.py:22
  165.2 60.5 %collective-permute-start.19 = (bf16[512,512]{1,0:T(8,128)(2,1)S(1)}, bf16[512,512]{1,0:T(8,128)(2,1)S(1)}, u32[]{:S(2)}, u32[]{:S(2)}) collective-permute-start(bf16[512,512]{1,0:T(8,128)(2,1)S(1)} %collective-permute-done.10), channel_id=1, source_target_pairs={{0,4},{2,6},{4,0},{6,2},{8,12},{10,14},{12,8},{14,10},{16,20},{18,... | collective-permute-start | bytes 1572872 | tf_op jit(solution)/shard_map/ppermute | solution.py:22
  166.5 83.6 %collective-permute-start.12 = (bf16[512,512]{1,0:T(8,128)(2,1)}, bf16[512,512]{1,0:T(8,128)(2,1)}, u32[]{:S(2)}, u32[]{:S(2)}) collective-permute-start(bf16[512,512]{1,0:T(8,128)(2,1)} %collective-permute-done.11), channel_id=1, source_target_pairs={{0,4},{2,6},{4,0},{6,2},{8,12},{10,14},{12,8},{14,10},{16,20},{18,... | collective-permute-start | bytes 1572872 | tf_op jit(solution)/shard_map/ppermute | solution.py:22
  222.6 24.0 %collective-permute-start.17 = (bf16[512,512]{1,0:T(8,128)(2,1)}, bf16[512,512]{1,0:T(8,128)(2,1)S(1)}, u32[]{:S(2)}, u32[]{:S(2)}) collective-permute-start(bf16[512,512]{1,0:T(8,128)(2,1)} %get-tuple-element.72), channel_id=1, source_target_pairs={{0,16},{2,18},{4,20},{6,22},{8,24},{10,26},{12,28},{14,30},{16,0},... | collective-permute-start | bytes 1572872 | tf_op jit(solution)/shard_map/ppermute | solution.py:22
  233.2 18.9 %collective-permute-start.21 = (bf16[512,512]{1,0:T(8,128)(2,1)}, bf16[512,512]{1,0:T(8,128)(2,1)S(1)}, u32[]{:S(2)}, u32[]{:S(2)}) collective-permute-start(bf16[512,512]{1,0:T(8,128)(2,1)} %collective-permute-done.20), channel_id=1, source_target_pairs={{0,4},{2,6},{4,0},{6,2},{8,12},{10,14},{12,8},{14,10},{16,20},{18,... | collective-permute-start | bytes 1572872 | tf_op jit(solution)/shard_map/ppermute | solution.py:22
  234.7 17.2 %collective-permute-start.37 = (f32[2,2,512]{2,1,0:T(2,128)S(1)}, f32[2,2,512]{2,1,0:T(2,128)S(1)}, u32[]{:S(2)}, u32[]{:S(2)}) collective-permute-start(f32[2,2,512]{2,1,0:T(2,128)S(1)} %pad_maximum_fusion.20), channel_id=1, source_target_pairs={{0,8},{2,10},{4,12},{6,14},{8,0},{10,2},{12,4},{14,6},{16,24},{18,... | collective-permute-start | bytes 24584 | tf_op jit(solution)/shard_map/ppermute | solution.py:22
  251.9 43.6 %collective-permute-start.39 = (f32[2,2,512]{2,1,0:T(2,128)S(1)}, f32[2,2,512]{2,1,0:T(2,128)S(1)}, u32[]{:S(2)}, u32[]{:S(2)}) collective-permute-start(f32[2,2,512]{2,1,0:T(2,128)S(1)} %multiply_add_fusion.6), channel_id=1, source_target_pairs={{0,2},{2,0},{4,6},{6,4},{8,10},{10,8},{12,14},{14,12},{16,18},{18,... | collective-permute-start | bytes 24584 | tf_op jit(solution)/shard_map/ppermute | solution.py:22
  289.8 28.4 %collective-permute-start.27 = (f32[512,384]{1,0:T(8,128)}, f32[512,384]{1,0:T(8,128)}, u32[]{:S(2)}, u32[]{:S(2)}) collective-permute-start(f32[512,384]{1,0:T(8,128)} %slice.386), channel_id=1, source_target_pairs={{0,2},{2,0},{4,6},{6,4},{8,10},{10,8},{12,14},{14,12},{16,18},{18,... | collective-permute-start | bytes 2359304 | tf_op jit(solution)/shard_map/ppermute | solution.py:22
  295.6 26.9 %collective-permute-start.38 = (bf16[1024,384]{1,0:T(8,128)(2,1)}, bf16[1024,384]{1,0:T(8,128)(2,1)}, u32[]{:S(2)}, u32[]{:S(2)}) collective-permute-start(bf16[1024,384]{1,0:T(8,128)(2,1)} %convert_element_type.96), channel_id=1, source_target_pairs={{0,8},{2,10},{4,12},{6,14},{8,0},{10,2},{12,4},{14,6},{16,24},{18,... | collective-permute-start | bytes 2359304 | tf_op jit(solution)/shard_map/ppermute | solution.py:22
  320.2 19.5 %collective-permute-start.28 = (f32[512,384]{1,0:T(8,128)S(1)}, f32[512,384]{1,0:T(8,128)S(1)}, u32[]{:S(2)}, u32[]{:S(2)}) collective-permute-start(f32[512,384]{1,0:T(8,128)S(1)} %slice_add_fusion), channel_id=1, source_target_pairs={{0,8},{2,10},{4,12},{6,14},{8,0},{10,2},{12,4},{14,6},{16,24},{18,... | collective-permute-start | bytes 2359304 | tf_op jit(solution)/shard_map/ppermute | solution.py:22
  323.6 17.8 %collective-permute-start.40 = (bf16[512,384]{1,0:T(8,128)(2,1)S(1)}, bf16[512,384]{1,0:T(8,128)(2,1)S(1)}, u32[]{:S(2)}, u32[]{:S(2)}) collective-permute-start(bf16[512,384]{1,0:T(8,128)(2,1)S(1)} %add_convert_fusion.1), channel_id=1, source_target_pairs={{0,2},{2,0},{4,6},{6,4},{8,10},{10,8},{12,14},{14,12},{16,18},{18,... | collective-permute-start | bytes 1179656 | tf_op jit(solution)/shard_map/ppermute | solution.py:22
  363.8 26.5 %collective-permute-start.31 = (bf16[512,384]{1,0:T(8,128)(2,1)S(1)}, bf16[512,384]{1,0:T(8,128)(2,1)S(1)}, u32[]{:S(2)}, u32[]{:S(2)}) collective-permute-start(bf16[512,384]{1,0:T(8,128)(2,1)S(1)} %maximum_select_fusion.4.refs_1_), channel_id=1, source_target_pairs={{0,2},{2,0},{4,6},{6,4},{8,10},{10,8},{12,14},{14,12},{16,18},{18,... | collective-permute-start | bytes 1179656 | tf_op jit(solution)/shard_map/ppermute | solution.py:22
  376.1 29.6 %collective-permute-start.33 = (bf16[512,384]{1,0:T(8,128)(2,1)S(1)}, bf16[512,384]{1,0:T(8,128)(2,1)S(1)}, u32[]{:S(2)}, u32[]{:S(2)}) collective-permute-start(bf16[512,384]{1,0:T(8,128)(2,1)S(1)} %collective-permute-done.32), channel_id=1, source_target_pairs={{0,2},{2,0},{4,6},{6,4},{8,10},{10,8},{12,14},{14,12},{16,18},{18,... | collective-permute-start | bytes 1179656 | tf_op jit(solution)/shard_map/ppermute | solution.py:22
  434.5 28.4 %collective-permute-start.45 = (bf16[1024,384]{1,0:T(8,128)(2,1)}, bf16[1024,384]{1,0:T(8,128)(2,1)}, u32[]{:S(2)}, u32[]{:S(2)}) collective-permute-start(bf16[1024,384]{1,0:T(8,128)(2,1)} %convert_element_type.103), channel_id=1, source_target_pairs={{0,8},{2,10},{4,12},{6,14},{8,0},{10,2},{12,4},{14,6},{16,24},{18,... | collective-permute-start | bytes 2359304 | tf_op jit(solution)/shard_map/ppermute | solution.py:22
  481.0 32.9 %collective-permute-start.79 = (bf16[2,2,48,3072]{3,2,1,0:T(8,128)(2,1)S(1)}, bf16[2,2,48,3072]{3,2,1,0:T(8,128)(2,1)S(1)}, u32[]{:S(2)}, u32[]{:S(2)}) collective-permute-start(bf16[2,2,48,3072]{3,2,1,0:T(8,128)(2,1)S(1)} %slice_bitcast_fusion.2), channel_id=1, source_target_pairs={{0,4},{2,6},{4,0},{6,2},{8,12},{10,14},{12,8},{14,10},{16,20},{18,... | collective-permute-start | bytes 3538952 | tf_op jit(solution)/shard_map/ppermute | solution.py:22
  502.1 47.4 %collective-permute-start.83 = (bf16[2,2,48,3072]{3,2,1,0:T(8,128)(2,1)S(1)}, bf16[2,2,48,3072]{3,2,1,0:T(8,128)(2,1)S(1)}, u32[]{:S(2)}, u32[]{:S(2)}) collective-permute-start(bf16[2,2,48,3072]{3,2,1,0:T(8,128)(2,1)S(1)} %slice_bitcast_fusion), channel_id=1, source_target_pairs={{0,4},{2,6},{4,0},{6,2},{8,12},{10,14},{12,8},{14,10},{16,20},{18,... | collective-permute-start | bytes 3538952 | tf_op jit(solution)/shard_map/ppermute | solution.py:22
  546.3 49.6 %collective-permute-start.80 = (bf16[2,48,3072]{2,1,0:T(8,128)(2,1)S(1)}, bf16[2,48,3072]{2,1,0:T(8,128)(2,1)S(1)}, u32[]{:S(2)}, u32[]{:S(2)}) collective-permute-start(bf16[2,48,3072]{2,1,0:T(8,128)(2,1)S(1)} %slice_bitcast_fusion.13), channel_id=1, source_target_pairs={{0,16},{2,18},{4,20},{6,22},{8,24},{10,26},{12,28},{14,30},{16,0},... | collective-permute-start | bytes 1769480 | tf_op jit(solution)/shard_map/ppermute | solution.py:22
  547.8 72.9 %collective-permute-start.55 = (bf16[2,2,512,256]{3,2,1,0:T(8,128)(2,1)S(1)}, bf16[2,2,512,256]{3,2,1,0:T(8,128)(2,1)S(1)}, u32[]{:S(2)}, u32[]{:S(2)}) collective-permute-start(bf16[2,2,512,256]{3,2,1,0:T(8,128)(2,1)S(1)} %slice_bitcast_fusion.10), channel_id=1, source_target_pairs={{0,4},{2,6},{4,0},{6,2},{8,12},{10,14},{12,8},{14,10},{16,20},{18,... | collective-permute-start | bytes 3145736 | tf_op jit(solution)/shard_map/ppermute | solution.py:22
  549.5 71.5 %collective-permute-start.59 = (bf16[2,2,512,256]{3,2,1,0:T(8,128)(2,1)S(1)}, bf16[2,2,512,256]{3,2,1,0:T(8,128)(2,1)S(1)}, u32[]{:S(2)}, u32[]{:S(2)}) collective-permute-start(bf16[2,2,512,256]{3,2,1,0:T(8,128)(2,1)S(1)} %slice_bitcast_fusion.8), channel_id=1, source_target_pairs={{0,4},{2,6},{4,0},{6,2},{8,12},{10,14},{12,8},{14,10},{16,20},{18,... | collective-permute-start | bytes 3145736 | tf_op jit(solution)/shard_map/ppermute | solution.py:22
  557.8 37.9 %collective-permute-start.64 = (bf16[256,384]{1,0:T(8,128)(2,1)S(1)}, bf16[256,384]{1,0:T(8,128)(2,1)S(1)}, u32[]{:S(2)}, u32[]{:S(2)}) collective-permute-start(bf16[256,384]{1,0:T(8,128)(2,1)S(1)} %constant_dynamic-slice_fusion.3), channel_id=1, source_target_pairs={{0,16},{2,18},{4,20},{6,22},{8,24},{10,26},{12,28},{14,30},{16,0},... | collective-permute-start | bytes 589832 | tf_op jit(solution)/shard_map/ppermute | solution.py:22
  568.2 44.4 %collective-permute-start.84 = (bf16[2,48,3072]{2,1,0:T(8,128)(2,1)S(1)}, bf16[2,48,3072]{2,1,0:T(8,128)(2,1)S(1)}, u32[]{:S(2)}, u32[]{:S(2)}) collective-permute-start(bf16[2,48,3072]{2,1,0:T(8,128)(2,1)S(1)} %slice_bitcast_fusion.12), channel_id=1, source_target_pairs={{0,16},{2,18},{4,20},{6,22},{8,24},{10,26},{12,28},{14,30},{16,0},... | collective-permute-start | bytes 1769480 | tf_op jit(solution)/shard_map/ppermute | solution.py:22
  595.8 20.9 %collective-permute-start.65 = (bf16[256,384]{1,0:T(8,128)(2,1)S(1)}, bf16[256,384]{1,0:T(8,128)(2,1)S(1)}, u32[]{:S(2)}, u32[]{:S(2)}) collective-permute-start(bf16[256,384]{1,0:T(8,128)(2,1)S(1)} %dynamic-slice_add_fusion.2), channel_id=1, source_target_pairs={{0,16},{2,18},{4,20},{6,22},{8,24},{10,26},{12,28},{14,30},{16,0},... | collective-permute-start | bytes 589832 | tf_op jit(solution)/shard_map/ppermute | solution.py:22
  596.0 22.4 %collective-permute-start.81 = (bf16[2,24,3072]{2,1,0:T(8,128)(2,1)S(1)}, bf16[2,24,3072]{2,1,0:T(8,128)(2,1)S(1)}, u32[]{:S(2)}, u32[]{:S(2)}) collective-permute-start(bf16[2,24,3072]{2,1,0:T(8,128)(2,1)S(1)} %get-tuple-element.175), channel_id=1, source_target_pairs={{0,2},{2,0},{4,6},{6,4},{8,10},{10,8},{12,14},{14,12},{16,18},{18,... | collective-permute-start | bytes 884744 | tf_op jit(solution)/shard_map/ppermute | solution.py:22
  618.5 18.9 %collective-permute-start.82 = (bf16[2,24,3072]{2,1,0:T(8,128)(2,1)S(1)}, bf16[2,24,3072]{2,1,0:T(8,128)(2,1)S(1)}, u32[]{:S(2)}, u32[]{:S(2)}) collective-permute-start(bf16[2,24,3072]{2,1,0:T(8,128)(2,1)S(1)} %get-tuple-element.173), channel_id=1, source_target_pairs={{0,8},{2,10},{4,12},{6,14},{8,0},{10,2},{12,4},{14,6},{16,24},{18,... | collective-permute-start | bytes 884744 | tf_op jit(solution)/shard_map/ppermute | solution.py:22
  618.6 25.1 %collective-permute-start.86 = (bf16[2,24,3072]{2,1,0:T(8,128)(2,1)S(1)}, bf16[2,24,3072]{2,1,0:T(8,128)(2,1)S(1)}, u32[]{:S(2)}, u32[]{:S(2)}) collective-permute-start(bf16[2,24,3072]{2,1,0:T(8,128)(2,1)S(1)} %get-tuple-element.169), channel_id=1, source_target_pairs={{0,8},{2,10},{4,12},{6,14},{8,0},{10,2},{12,4},{14,6},{16,24},{18,... | collective-permute-start | bytes 884744 | tf_op jit(solution)/shard_map/ppermute | solution.py:22
  620.9 38.4 %collective-permute-start.56 = (bf16[2,512,256]{2,1,0:T(8,128)(2,1)S(1)}, bf16[2,512,256]{2,1,0:T(8,128)(2,1)S(1)}, u32[]{:S(2)}, u32[]{:S(2)}) collective-permute-start(bf16[2,512,256]{2,1,0:T(8,128)(2,1)S(1)} %slice_bitcast_fusion.20), channel_id=1, source_target_pairs={{0,16},{2,18},{4,20},{6,22},{8,24},{10,26},{12,28},{14,30},{16,0},... | collective-permute-start | bytes 1572872 | tf_op jit(solution)/shard_map/ppermute | solution.py:22
  621.1 47.6 %collective-permute-start.60 = (bf16[2,512,256]{2,1,0:T(8,128)(2,1)S(1)}, bf16[2,512,256]{2,1,0:T(8,128)(2,1)S(1)}, u32[]{:S(2)}, u32[]{:S(2)}) collective-permute-start(bf16[2,512,256]{2,1,0:T(8,128)(2,1)S(1)} %slice_bitcast_fusion.18), channel_id=1, source_target_pairs={{0,16},{2,18},{4,20},{6,22},{8,24},{10,26},{12,28},{14,30},{16,0},... | collective-permute-start | bytes 1572872 | tf_op jit(solution)/shard_map/ppermute | solution.py:22
  628.3 90.2 %collective-permute-start.75 = (bf16[1024,384]{1,0:T(8,128)(2,1)S(1)}, bf16[1024,384]{1,0:T(8,128)(2,1)S(1)}, u32[]{:S(2)}, u32[]{:S(2)}) collective-permute-start(bf16[1024,384]{1,0:T(8,128)(2,1)S(1)} %maximum_select_fusion.2), channel_id=1, source_target_pairs={{0,8},{2,10},{4,12},{6,14},{8,0},{10,2},{12,4},{14,6},{16,24},{18,... | collective-permute-start | bytes 2359304 | tf_op jit(solution)/shard_map/ppermute | solution.py:22
  637.4 31.6 %collective-permute-start.67 = (bf16[2,2,512,256]{3,2,1,0:T(8,128)(2,1)S(1)}, bf16[2,2,512,256]{3,2,1,0:T(8,128)(2,1)S(1)}, u32[]{:S(2)}, u32[]{:S(2)}) collective-permute-start(bf16[2,2,512,256]{3,2,1,0:T(8,128)(2,1)S(1)} %slice_bitcast_fusion.6), channel_id=1, source_target_pairs={{0,4},{2,6},{4,0},{6,2},{8,12},{10,14},{12,8},{14,10},{16,20},{18,... | collective-permute-start | bytes 3145736 | tf_op jit(solution)/shard_map/ppermute | solution.py:22
  643.7 38.8 %collective-permute-start.71 = (bf16[2,2,512,256]{3,2,1,0:T(8,128)(2,1)S(1)}, bf16[2,2,512,256]{3,2,1,0:T(8,128)(2,1)S(1)}, u32[]{:S(2)}, u32[]{:S(2)}) collective-permute-start(bf16[2,2,512,256]{3,2,1,0:T(8,128)(2,1)S(1)} %slice_bitcast_fusion.4), channel_id=1, source_target_pairs={{0,4},{2,6},{4,0},{6,2},{8,12},{10,14},{12,8},{14,10},{16,20},{18,... | collective-permute-start | bytes 3145736 | tf_op jit(solution)/shard_map/ppermute | solution.py:22
  669.0 52.8 %collective-permute-start.58 = (bf16[2,256,256]{2,1,0:T(8,128)(2,1)S(1)}, bf16[2,256,256]{2,1,0:T(8,128)(2,1)S(1)}, u32[]{:S(2)}, u32[]{:S(2)}) collective-permute-start(bf16[2,256,256]{2,1,0:T(8,128)(2,1)S(1)} %get-tuple-element.181), channel_id=1, source_target_pairs={{0,8},{2,10},{4,12},{6,14},{8,0},{10,2},{12,4},{14,6},{16,24},{18,... | collective-permute-start | bytes 786440 | tf_op jit(solution)/shard_map/ppermute | solution.py:22
  669.2 38.2 %collective-permute-start.68 = (bf16[2,512,256]{2,1,0:T(8,128)(2,1)S(1)}, bf16[2,512,256]{2,1,0:T(8,128)(2,1)S(1)}, u32[]{:S(2)}, u32[]{:S(2)}) collective-permute-start(bf16[2,512,256]{2,1,0:T(8,128)(2,1)S(1)} %slice_bitcast_fusion.16), channel_id=1, source_target_pairs={{0,16},{2,18},{4,20},{6,22},{8,24},{10,26},{12,28},{14,30},{16,0},... | collective-permute-start | bytes 1572872 | tf_op jit(solution)/shard_map/ppermute | solution.py:22
  682.7 35.6 %collective-permute-start.72 = (bf16[2,512,256]{2,1,0:T(8,128)(2,1)S(1)}, bf16[2,512,256]{2,1,0:T(8,128)(2,1)S(1)}, u32[]{:S(2)}, u32[]{:S(2)}) collective-permute-start(bf16[2,512,256]{2,1,0:T(8,128)(2,1)S(1)} %slice_bitcast_fusion.14), channel_id=1, source_target_pairs={{0,16},{2,18},{4,20},{6,22},{8,24},{10,26},{12,28},{14,30},{16,0},... | collective-permute-start | bytes 1572872 | tf_op jit(solution)/shard_map/ppermute | solution.py:22
  683.2 38.6 %collective-permute-start.62 = (bf16[2,256,256]{2,1,0:T(8,128)(2,1)S(1)}, bf16[2,256,256]{2,1,0:T(8,128)(2,1)S(1)}, u32[]{:S(2)}, u32[]{:S(2)}) collective-permute-start(bf16[2,256,256]{2,1,0:T(8,128)(2,1)S(1)} %get-tuple-element.185), channel_id=1, source_target_pairs={{0,8},{2,10},{4,12},{6,14},{8,0},{10,2},{12,4},{14,6},{16,24},{18,... | collective-permute-start | bytes 786440 | tf_op jit(solution)/shard_map/ppermute | solution.py:22
  718.9 17.6 %collective-permute-start.76 = (bf16[2,1,1024,384]{3,2,0,1:T(8,128)(2,1)S(1)}, bf16[2,1,1024,384]{3,2,0,1:T(8,128)(2,1)S(1)}, u32[]{:S(2)}, u32[]{:S(2)}) collective-permute-start(bf16[2,1,1024,384]{3,2,0,1:T(8,128)(2,1)S(1)} %bitcast.258), channel_id=1, source_target_pairs={{0,2},{2,0},{4,6},{6,4},{8,10},{10,8},{12,14},{14,12},{16,18},{18,... | collective-permute-start | bytes 4718600 | tf_op jit(solution)/shard_map/ppermute | solution.py:22
  (114 other events, 1065.6 us)

commit v2 on v1

--- a/solution.py
+++ b/solution.py
@@ -78,6 +78,10 @@
 
 def after(value, *others):
     return lax.optimization_barrier((value,) + others)[0] if others else value
+
+
+def together(*values):
+    return lax.optimization_barrier(values)
 
 
 def permute_body(order_ref, first_ref, second_ref, out_ref):
@@ -162,7 +166,7 @@
         out_specs=pl.BlockSpec((high, wide), lambda i: (i, 0)),
         compiler_params=pltpu.CompilerParams(vmem_limit_bytes=32 * 1024 * 1024),
         cost_estimate=pl.CostEstimate(
-            flops=features * rows * wide,
+            flops=8 * features * rows * wide,
             bytes_accessed=2 * features * rows,
             transcendentals=0,
         ),
@@ -239,8 +243,8 @@
         ),
         compiler_params=pltpu.CompilerParams(vmem_limit_bytes=48 * 1024 * 1024),
         cost_estimate=pl.CostEstimate(
-            flops=rows * width * count // 4,
-            bytes_accessed=rows * count // 4,
+            flops=rows * width * count * (24 if center is None else 1) // 4,
+            bytes_accessed=rows * count * (8 if center is None else 1) // 4,
             transcendentals=rows * count // 8,
         ),
         name="softmax_pass",
@@ -363,7 +367,9 @@
     images = local * row_size // 128
     onehot = (image_of[:, None] == jnp.arange(images, dtype=jnp.int32)[None, :]).astype(f32)
     counts = jnp.sum(onehot, axis=0)
-    for bit in (ybit, zhi, zlo, core):
+    counts = counts + swap(counts, zlo)
+    counts_zlo = counts
+    for bit in (ybit, zhi, core):
         counts = counts + swap(counts, bit)
 
     def columns(index):
@@ -380,15 +386,9 @@
     from_core = after(swap(jnp.concatenate([near_c, far_c], 1), core), counts)
     mine = jnp.concatenate([near, from_core[:, :quarter]], 0)
     theirs = jnp.concatenate([far, from_core[:, quarter:]], 0)
-    low = swap(theirs, zlo)
-    own_h = [swap(cut(mine, 0), zhi)]
-    for c in range(1, chunks):
-        own_h.append(swap(after(cut(mine, c), own_h[-1]), zhi))
-    own_y = swap(mine, ybit)
-
     strip = features // proto_size
     order = (jnp.arange(row_size, dtype=jnp.int32) ^ row_index).astype(jnp.int32)
-    tokens_near = permute_columns(tokens, swap(tokens, core), order)
+    tokens_core = swap(tokens, core)
 
     def group_rows(value):
         value = collect(value, "proto", proto_bits, 0)
@@ -452,7 +452,8 @@
     teacher_own = (
         teach * lax.rsqrt(jnp.sum(teach * teach, axis=1, keepdims=True) + norm_eps)
     ).astype(bf16)
-    teacher_n = group_rows(teacher_own)
+    teacher_near = collect(teacher_own, "proto", proto_bits, 0)
+    teacher_core = swap(teacher_near, core)
     run = functools.partial(
         softmax_pass,
         left=proto_teacher,
@@ -462,40 +463,72 @@
         parts=4,
         tau=tau_teacher,
     )
-    first = run(after(teacher_n[0][0], counts, tokens_near))
-    low_y = swap(after(low, first[2]), ybit)
-    third = run(after(teacher_n[0][1], first[2], own_y))
     piece = lax.dynamic_slice_in_dim(tokens, proto_index * strip, strip, 1)
-    first_half = swap(after(piece[:, : strip // 2], low, third[2]), zlo)
-    own_hy = [swap(value, ybit) for value in own_h]
-    low_h = [swap(after(cut(low, 0), own_h[-1]), zhi)]
-    second_half = swap(after(piece[:, strip // 2 :], first_half, own_h[-1]), zlo)
-    turned_near = turn_rows(after(tokens_near, third[2]))
-    second = run(after(jnp.concatenate(teacher_n[1], 0), third[2], *own_h, low_y, first_half, turned_near))
-    far_t = swap(second[1].astype(bf16), zlo)
-    low_h += [swap(after(cut(low, c), second[2]), zhi) for c in range(1, chunks)]
-    low_hy = [swap(after(value, second[2]), ybit) for value in low_h]
-    strips = [[first_half, second_half]]
+    mine, theirs, teacher_near, teacher_core, tokens_core = together(
+        mine, theirs, teacher_near, teacher_core, tokens_core
+    )
+    low = swap(theirs, zlo)
+    own_y = swap(mine, ybit)
+    own_h = [swap(cut(mine, 0), zhi)]
+    teacher_far = swap(teacher_near, zlo)
+    low, own_y, own_h[0], teacher_far = together(low, own_y, own_h[0], teacher_far)
+
+    first = run(after(teacher_near, low))
+    first_half = swap(after(piece[:, : strip // 2], low), zlo)
+    low_y = swap(low, ybit)
+    own_h += [swap(after(cut(mine, c), low), zhi) for c in range(1, chunks)]
+    weight = 1.0 / (images * jnp.sum(onehot * counts[None, :], axis=1))
+    weight_far = swap(weight, zlo)
+    first_half, low_y, own_h[-1], weight_far, *first = together(
+        first_half, low_y, own_h[-1], weight_far, *first
+    )
+
+    third = run(after(teacher_core, first_half))
+    second_half = swap(after(piece[:, strip // 2 :], first_half), zlo)
+    own_hy = swap(after(jnp.concatenate(own_h, 1), first_half), ybit)
+    low_h = [swap(after(cut(low, 0), first_half), zhi)]
+    strips = [[first_half]]
     for bit in reversed(proto_bits):
         strips = strips + [[swap(value, bit, "proto") for value in pair] for pair in strips]
+    ends = [pair[0] for pair in strips[1:]]
+    far_core = swap(teacher_far, core)
+    second_half, own_hy, low_h[0], far_core, *rest = together(
+        second_half, own_hy, low_h[0], far_core, *ends, *third
+    )
+    ends, third = rest[: len(ends)], rest[len(ends) :]
+    strips = [[value] for value in [first_half] + ends]
+
+    second = run(after(jnp.concatenate([teacher_far, far_core], 0), second_half))
+    low_hy = [swap(after(low_h[0], second_half), ybit)]
+    low_h += [swap(after(cut(low, c), second_half), zhi) for c in range(1, chunks)]
+    ends = [second_half]
+    for bit in reversed(proto_bits):
+        ends = ends + [swap(value, bit, "proto") for value in ends]
+    tokens_near = permute_columns(after(tokens, second_half), tokens_core, order)
+    pair = swap(jnp.stack([weight, weight_far]), core)
+    low_hy[0], low_h[-1], tokens_near, pair, *rest = together(
+        low_hy[0], low_h[-1], tokens_near, pair, *ends, *second
+    )
+    weight = [[weight, pair[0]], [weight_far, pair[1]]]
+    ends, second = rest[: len(ends)], rest[len(ends) :]
+    strips = [pair + [value] for pair, value in zip(strips, ends)]
+    low_hy += [swap(value, ybit) for value in low_h[1:]]
+    far_t = swap(second[1].astype(bf16), zlo)
     tokens_far = jnp.concatenate([value for pair in strips for value in pair], 1)
     each = row_size // proto_size
     order_far = ((order // each) ^ proto_index) * each + order % each
-    tokens_far = permute_columns(tokens_far, swap(tokens_far, core), order_far)
+    far_cores = swap(tokens_far, core)
+    turned_near = turn_rows(tokens_near)
+    tokens_far = permute_columns(tokens_far, far_cores, order_far)
     et, near_t, lse_t = gather_passes(first, second, third)
     mean_t, _, lse_t, _ = merge(near_t, far_t, lse_t)
-
-    weight = 1.0 / (images * jnp.sum(onehot * counts[None, :], axis=1))
-    weight_far = swap(weight, zlo)
-    pair = swap(jnp.stack([weight, weight_far]), core)
-    weight = [[weight, pair[0]], [weight_far, pair[1]]]
 
     w_out_part = lax.dynamic_slice_in_dim(w_out, part * quarter, quarter, 0)
     slopes, hiddens = [[], []], [[], []]
     bott = [jnp.zeros((2 * local, w_out.shape[1]), f32)] * 2
     for c in range(chunks):
         early = [cut(value, c) for value in (mine, own_y, low, low_y)]
-        early = jnp.concatenate(early + [own_h[c], own_hy[c]], 0)
+        early = jnp.concatenate(early + [own_h[c], cut(own_hy, c)], 0)
         late = jnp.concatenate([low_h[c], low_hy[c]], 0)
         w_cut = w_out_part[c * chunk : (c + 1) * chunk]
         for z, rows in enumerate((tokens_near, tokens_far)):
@@ -504,11 +537,12 @@
             slopes[z].append(slope)
             hiddens[z].append(hidden)
 
-    bott = [value[:local] + swap(value[local:], core) for value in bott]
-    bott = bott[0] + swap(bott[1], zlo)
+    bott = [value[:local] + swap(after(value[local:], mean_t, lse_t), core) for value in bott]
+    bott, turned_near = together(bott[0] + swap(bott[1], zlo), turned_near)
     for bit in proto_bits:
         keep, given = halves(bott, bit, "proto", 0)
         bott = keep + swap(given, bit, "proto")
+    bott, turned_far = together(bott, turn_rows(tokens_far))
     recip = lax.rsqrt(jnp.sum(bott * bott, axis=1, keepdims=True) + norm_eps)
     unit = bott * recip
     student_own = unit.astype(bf16)
@@ -522,26 +556,24 @@
         parts=4,
         tau=tau_student,
     )
-    turned_far = turn_rows(tokens_far)
-    first = run(after(student_blocks[0][0], turned_far))
-    second = run(after(jnp.concatenate(student_blocks[1], 0), first[2]))
+    first = run(student_blocks[0][0])
+    far_rows, *first = together(jnp.concatenate(student_blocks[1], 0), *first)
+    second = run(far_rows)
+    student_blocks[0][1], *second = together(student_blocks[0][1], *second)
     far_s = swap(second[1].astype(bf16), zlo)
-    third = run(after(student_blocks[0][1], second[2]))
+    third = run(student_blocks[0][1])
+    far_s, *third = together(far_s, *third)
     es, near_s, lse_s = gather_passes(first, second, third)
     mean_s, own_lse, lse_s, marks = merge(near_s, far_s, lse_s)
 
     weight_own = own_rows(weight[0][0])
     cross = own_lse / log2e - jnp.sum(student_own.astype(f32) * mean_t, axis=1) / tau_student
     loss = jnp.sum(weight_own * cross).reshape((1,))
-    loss = loss + swap(loss, ybit)
-    loss_y = loss
     loss = loss + swap(loss, zhi)
 
     coef = loss_scale / tau_student
     dnorm = (coef * weight_own)[:, None] * (mean_s - mean_t)
     dbott_own = (recip * (dnorm - unit * jnp.sum(unit * dnorm, axis=1, keepdims=True))).astype(bf16)
-    dbott = group_rows(dbott_own)
-    dbott = [jnp.concatenate(pair, 0) for pair in dbott]
 
     student_n = jnp.concatenate(
         [student_blocks[0][0], student_blocks[1][0], student_blocks[1][1], student_blocks[0][1]], 0
@@ -570,16 +602,18 @@
     count = es[0][0].shape[1]
     blocks = [(es[i][0], scale_s[i], et[i][0], scale_t[i]) for i in range(3)]
 
-    def fold(value, ready=(), before=()):
-        columns = value.shape[1]
-        value = value.reshape((2, 2, 2, -1, columns))
+    def fold_y(value, *before):
+        value = value.reshape((2, 2, 2, -1, value.shape[1]))
         sent = swap(after(value[:, :, 1], *before), ybit)
-        value = after(value[:, :, 0] + sent, *ready)
+        return value[:, :, 0] + sent, sent
+
+    def fold(value):
+        columns = value.shape[-1]
         value = value[0] + swap(value[1], zhi)
         value = value.reshape((2, 2, -1, columns))
         value = jnp.stack([value[:, 0], swap(value[:, 1], core)], 1)
         value = jnp.stack([value[0], swap(value[1], zlo)])
-        return value.reshape((4, -1, columns)), sent
+        return value.reshape((4, -1, columns))
 
     def spread(pieces):
         whole = jnp.concatenate(pieces, 2)
@@ -591,47 +625,52 @@
     proto_pieces, sent = [], []
     for i in range(pieces):
         value = proto_pass(after(turned, marks[i]), blocks, i, pieces)
-        value, got = fold(value, tuple(dbott), (loss_y,))
+        value, got = fold_y(value)
         proto_pieces.append(value)
         sent.append(got)
+    dbott = collect(dbott_own, "proto", proto_bits, 0)
+    dbott, loss, proto_pieces[0] = together(dbott, loss, proto_pieces[0])
+    dbott_far = swap(dbott, zlo)
+    dbott = [
+        jnp.concatenate([dbott, swap(dbott, core)], 0),
+        jnp.concatenate([dbott_far, swap(dbott_far, core)], 0),
+    ]
+    proto_pieces[0] = fold(proto_pieces[0])
 
     hidden = [jnp.concatenate(pair, 1) for pair in hiddens]
     w_out_grad = (inner(hidden[0], dbott[0]) + inner(hidden[1], dbott[1])).astype(bf16)
     product = w_out_grad
-    loss = after(loss, product)
-    for bit in (core, zlo):
-        loss = loss + swap(loss, bit)
+    parts = 2
+    back = [
+        outer_last(dbott[z], w_out_part) * jnp.concatenate(slopes[z], 1).astype(f32)
+        for z in (0, 1)
+    ]
+    back = [value.astype(bf16) for value in back]
+    *back, product, proto_pieces[-1] = together(*back, product, proto_pieces[-1])
+    proto_pieces = proto_pieces[:1] + [fold(value) for value in proto_pieces[1:]]
+    keep, given = halves(product, ybit, "row", 0)
+    w_out_grad = keep + swap(given, ybit)
+    sums = []
+    for i in range(parts):
+        grad = grad_pass(turned_near, turned_far, *back, i, parts)
+        grad, back[0] = together(grad, back[0])
+        sums += [fold_y(half)[0] for half in jnp.split(grad, 2, axis=1)]
+    keep, given = halves(w_out_grad, zhi, "row", 0)
+    w_out_grad = keep + swap(given, zhi)
+    w_out_grad = in_order(w_out_grad, swap(w_out_grad, zhi), zhi, "row", 0)
+    w_out_grad, loss, sums[0] = together(w_out_grad, loss, sums[0])
     for bit in proto_bits:
         loss = loss + swap(loss, bit, "proto")
-    loss = loss[0]
-    for bit in (ybit, zhi):
-        keep, given = halves(w_out_grad, bit, "row", 0)
-        w_out_grad = keep + swap(given, bit)
-    for bit in (zhi, ybit):
-        w_out_grad = in_order(w_out_grad, swap(w_out_grad, bit), bit, "row", 0)
-    summed = w_out_grad
+    loss = loss + swap(loss, core)
+    loss = loss + swap(loss, zlo)
+    w_out_grad, loss, sums[-1] = together(w_out_grad, loss, sums[-1])
+    w_out_grad = in_order(w_out_grad, swap(w_out_grad, ybit), ybit, "row", 0)
     w_out_grad = in_order(w_out_grad, swap(w_out_grad, zlo), zlo, "row", 0)
+    w_in_pieces = [fold(value) for value in sums]
     w_out_grad = w_out_grad.reshape((2, 1, quarter, -1))
     w_out_grad = in_order(w_out_grad, swap(w_out_grad, core), core, "row", 1)
     w_out_grad = w_out_grad.reshape((4 * quarter, -1))
-
-    w_in_pieces = []
-    parts = 4 if quarter % 1024 == 0 else 2
-    back = [
-        outer_last(after(dbott[z], product), w_out_part)
-        * jnp.concatenate(slopes[z], 1).astype(f32)
-        for z in (0, 1)
-    ]
-    back = lax.optimization_barrier([value.astype(bf16) for value in back])
-    grads = []
-    for i in range(parts // 2):
-        grad = grad_pass(turned_near, turned_far, *back, i, parts // 2)
-        grads += jnp.split(grad, 2, axis=1)
-    for i, grad in enumerate(grads):
-        earlier = (sent[-2], summed) if i >= 2 else ()
-        value, got = fold(grad, before=earlier)
-        w_in_pieces.append(value)
-        sent.append(got)
+    loss = (loss + swap(loss, ybit))[0]
     return (loss, spread(w_in_pieces), w_out_grad.astype(f32), spread(proto_pieces))
 
 

time: 753 us -> 678 us (0.900)
  waiting for transfers between devices: 326 us -> 263 us
  local copies, waits for them, and re-layouts: 82.2 us -> 59 us
  starting transfers between devices: 82.8 us -> 98.8 us
  matrix products: 25.6 us -> 33.2 us
    ppermute x87 -> x86, waiting for transfers between devices: 326 us -> 263 us  [swap(): return lax.ppermute(value, axis, [(i, i ^ bit) for i in range(size)])]
    ppermute x87 -> x86, starting transfers between devices: 82.8 us -> 98.8 us  [swap(): return lax.ppermute(value, axis, [(i, i ^ bit) for i in range(size)])]
    unnamed x166 -> x163, local copies, waits for them, and re-layouts: 51.4 us -> 35.7 us
    dot_general x4, matrix products: 18.1 us -> 26 us  [dot(): return jnp.dot(left, right, preferred_element_type=f32)]
  transfers between devices with their start and end apart: 87 -> 86, of which waited for: 40 -> 40; matrix products, arithmetic and copies ran while one was open for 12% -> 11% of each run, Pallas kernels for 22% -> 25%
where the time goes in v2:
time: 678 us; the launch traced here: 674 us
  waiting for transfers between devices  263 us (39%)
  Pallas kernels  185 us (27%)
  starting transfers between devices  98.8 us (15%)
  local copies, waits for them, and re-layouts  59 us (9%)
  matrix products  33.2 us (5%)
  other arithmetic  26.5 us (4%)
  between operations  8.17 us (1%)
    ppermute x86, waiting for transfers between devices, swap(): return lax.ppermute(value, axis, [(i, i ^ bit) for i in range(size)])  263 us
    pallas_call x6, Pallas kernels, softmax_pass(): pl.pallas_call(functools.partial(softmax_body, log2e / tau, tile_of(count...  99.5 us
    ppermute x86, starting transfers between devices, swap(): return lax.ppermute(value, axis, [(i, i ^ bit) for i in range(size)])  98.8 us
    unnamed x163, local copies, waits for them, and re-layouts  35.7 us
    dot_general x4, matrix products, dot(): return jnp.dot(left, right, preferred_element_type=f32)  26 us
    pallas_call x2, Pallas kernels, proto_pass(): pl.pallas_call(functools.partial(proto_body, len(blocks)), out_shape=jax....  25.6 us
    pallas_call x2, Pallas kernels, grad_pass(): pl.pallas_call(grad_body, out_shape=jax.ShapeDtypeStruct((features, wide)...  23 us
    pallas_call x4, Pallas kernels, head_pass(): pl.pallas_call(head_body, out_shape=(jax.ShapeDtypeStruct((count, wide),...  16.7 us
  transfers between devices with their start and end apart: 86, of which 40 were waited for; matrix products, arithmetic and copies ran while one was open for 11% of the time, Pallas kernels for 25%

profile of v2, /device:TPU:0, one launch (start us, length us, event | category | flops | bytes accessed | tf_op | source)
XLA Modules:
  0.0 673.7 jit_solution(618969689262722797)
XLA Ops:
  32.2 35.1 %collective-permute-done.11 = bf16[512,384]{1,0:T(8,128)(2,1)} collective-permute-done((bf16[512,384]{1,0:T(8,128)(2,1)S(1)}, bf16[512,384]{1,0:T(8,128)(2,1)}, u32[]{:S(2)}, u32[]{:S(2)}) %collective-permute-start.11) | collective-permute-done | bytes 393248 | tf_op jit(solution)/shard_map/ppermute | solution.py:22
  73.7 13.4 %softmax_pass.6 = (bf16[512,6144]{1,0:T(8,128)(2,1)}, f32[512,384]{1,0:T(8,128)S(1)}, f32[512,128]{1,0:T(8,128)S(1)}) custom-call(s32[1]{0:T(128)} %bitcast.refs_0_, bf16[512,384]{1,0:T(8,128)(2,1)S(1)} %maximum_select_fusion.3.refs_1_, bf16[384,24576]{1,0:T(8,128)(2,1)} %refs_2_.8, f32[1,24576]{1,0:T(1,128)S(1)} %bitcast.233, bf16[384,24576]{1,0:T(8,128)(2,1)} %refs_3_.5), custom_call_target="tpu_custom_call" | custom-call | flops 301989888 | bytes 786432 | tf_op jit(solution)/shard_map/softmax_pass/pallas_call | solution.py:224
  88.0 15.2 %collective-permute-done.15 = f32[512]{0:T(512)S(1)} collective-permute-done((f32[512]{0:T(512)S(1)}, f32[512]{0:T(512)S(1)}, u32[]{:S(2)}, u32[]{:S(2)}) %collective-permute-start.15) | collective-permute-done | bytes 2080 | tf_op jit(solution)/shard_map/ppermute | solution.py:22
  116.9 13.3 %softmax_pass.7 = (bf16[512,6144]{1,0:T(8,128)(2,1)}, f32[512,384]{1,0:T(8,128)S(1)}, f32[512,128]{1,0:T(8,128)S(1)}) custom-call(s32[1]{0:T(128)} %bitcast.refs_0_, bf16[512,384]{1,0:T(8,128)(2,1)S(1)} %collective-permute-done.6.refs_1_, bf16[384,24576]{1,0:T(8,128)(2,1)} %refs_2_.8, f32[1,24576]{1,0:T(1,128)S(1)} %bitcast.234, bf16[384,24576]{1,0:T(8,128)(2,1)} %refs_3_.5), custom_call_target="tpu_custom_call" | custom-call | flops 301989888 | bytes 786432 | tf_op jit(solution)/shard_map/softmax_pass/pallas_call | solution.py:224
  131.1 10.4 %collective-permute-done.18 = bf16[512,512]{1,0:T(8,128)(2,1)} collective-permute-done((bf16[512,512]{1,0:T(8,128)(2,1)S(1)}, bf16[512,512]{1,0:T(8,128)(2,1)}, u32[]{:S(2)}, u32[]{:S(2)}) %collective-permute-start.18) | collective-permute-done | bytes 524320 | tf_op jit(solution)/shard_map/ppermute | solution.py:22
  151.8 23.0 %softmax_pass.8 = (bf16[1024,6144]{1,0:T(8,128)(2,1)}, f32[1024,384]{1,0:T(8,128)S(1)}, f32[1024,128]{1,0:T(8,128)S(1)}) custom-call(s32[1]{0:T(128)} %bitcast.refs_0_, bf16[1024,384]{1,0:T(8,128)(2,1)S(1)} %pad_maximum_fusion.5.refs_1_, bf16[384,24576]{1,0:T(8,128)(2,1)} %refs_2_.8, f32[1,24576]{1,0:T(1,128)S(1)} %bitcast.235, bf16[384,24576]{1,0:T(8,128)(2,1)} %refs_3_.5), custom_call_target="tpu_custom_call" | custom-call | flops 603979776 | bytes 1572864 | tf_op jit(solution)/shard_map/softmax_pass/pallas_call | solution.py:224
  175.7 6.1 permute_columns.2.rows_ref.in_ref
  181.8 3.2 copy-done
  200.4 6.8 %fusion.4.early_ref = f32[1024,512]{1,0:T(8,128)S(1)} fusion(bf16[3072,512]{1,0:T(8,128)(2,1)} %get-tuple-element.272, bf16[1024,4096]{1,0:T(8,128)(2,1)} %copy-done), kind=kOutput, calls=%fused_computation.4 | convolution fusion | flops 3221225472 | bytes 11534336 | tf_op jit(solution)/shard_map/dot_general | solution.py:76
  207.4 4.1 head_pass.4
  224.7 4.7 collective-permute-done.31
  230.2 6.8 %permute_columns.3.rows_ref.in_ref = bf16[1024,4096]{1,0:T(8,128)(2,1)S(1)} custom-call(s32[16]{0:T(128)S(1)} %fusion.129.order_ref, bf16[512,4096]{1,0:T(8,128)(2,1)} %constant_dynamic-update-slice_fusion.10.first_ref, bf16[512,4096]{1,0:T(8,128)(2,1)} %collective-permute-done.33.second_ref), custom_call_target="tpu_custom_call" | custom-call | bytes 8388608 | tf_op jit(solution)/shard_map/permute_columns/pallas_call | solution.py:112
  237.0 7.7 %fusion.early_ref = f32[1024,512]{1,0:T(8,128)S(1)} fusion(bf16[3072,512]{1,0:T(8,128)(2,1)} %get-tuple-element.272, bf16[1024,4096]{1,0:T(8,128)(2,1)S(1)} %permute_columns.3.rows_ref.in_ref), kind=kOutput, calls=%fused_computation | convolution fusion | flops 3221225472 | bytes 11534336 | tf_op jit(solution)/shard_map/dot_general | solution.py:76
  244.8 4.5 head_pass.6
  251.3 5.4 fusion.2.early_ref
  256.8 3.4 copy-done.2
  260.1 4.0 head_pass.7
  264.4 6.0 fusion.6.early_ref
  270.4 4.1 head_pass.5
  276.9 3.5 turn_rows.2.near_ref
  280.4 14.6 %collective-permute-done.35 = f32[512,384]{1,0:T(8,128)S(1)} collective-permute-done((f32[512,384]{1,0:T(8,128)S(1)}, f32[512,384]{1,0:T(8,128)S(1)}, u32[]{:S(2)}, u32[]{:S(2)}) %collective-permute-start.35) | collective-permute-done | bytes 786464 | tf_op jit(solution)/shard_map/ppermute | solution.py:22
  296.4 3.5 turn_rows.3.far_ref
  299.9 3.3 copy-done.5
  306.6 4.5 collective-permute-done.37
  313.6 5.5 collective-permute-done.38
  319.1 13.5 %softmax_pass.9 = (bf16[512,6144]{1,0:T(8,128)(2,1)}, f32[512,384]{1,0:T(8,128)S(1)}, f32[512,128]{1,0:T(8,128)S(1)}) custom-call(s32[1]{0:T(128)} %bitcast.refs_0_, bf16[512,384]{1,0:T(8,128)(2,1)S(1)} %maximum_select_fusion.4.refs_1_, bf16[384,24576]{1,0:T(8,128)(2,1)} %refs_3_.5, bf16[384,24576]{1,0:T(8,128)(2,1)} %refs_3_.5), custom_call_target="tpu_custom_call" | custom-call | flops 7247757312 | bytes 6291456 | tf_op jit(solution)/shard_map/softmax_pass/pallas_call | solution.py:224
  334.3 22.8 %softmax_pass.10 = (bf16[1024,6144]{1,0:T(8,128)(2,1)}, f32[1024,384]{1,0:T(8,128)S(1)}, f32[1024,128]{1,0:T(8,128)S(1)}) custom-call(s32[1]{0:T(128)} %bitcast.refs_0_, bf16[1024,384]{1,0:T(8,128)(2,1)S(1)} %pad_maximum_fusion.6.refs_1_, bf16[384,24576]{1,0:T(8,128)(2,1)} %refs_3_.5, bf16[384,24576]{1,0:T(8,128)(2,1)} %refs_3_.5), custom_call_target="tpu_custom_call" | custom-call | flops 14495514624 | bytes 12582912 | tf_op jit(solution)/shard_map/softmax_pass/pallas_call | solution.py:224
  358.8 13.6 %softmax_pass.11 = (bf16[512,6144]{1,0:T(8,128)(2,1)}, f32[512,384]{1,0:T(8,128)S(1)}, f32[512,128]{1,0:T(8,128)S(1)}) custom-call(s32[1]{0:T(128)} %bitcast.refs_0_, bf16[512,384]{1,0:T(8,128)(2,1)S(1)} %collective-permute-done.40.refs_1_, bf16[384,24576]{1,0:T(8,128)(2,1)} %refs_3_.5, bf16[384,24576]{1,0:T(8,128)(2,1)} %refs_3_.5), custom_call_target="tpu_custom_call" | custom-call | flops 7247757312 | bytes 6291456 | tf_op jit(solution)/shard_map/softmax_pass/pallas_call | solution.py:224
  373.2 4.4 collective-permute-done.41
  392.0 12.7 %proto_pass.2 = bf16[384,3072]{1,0:T(8,128)(2,1)S(1)} custom-call(bf16[384,2048]{1,0:T(8,128)(2,1)S(1)} %convolution_convert_fusion.n_ref, bf16[512,6144]{1,0:T(8,128)(2,1)} %get-tuple-element.198.refs_0_, f32[512,128]{1,0:T(8,128)S(1)} %broadcast_in_dim.15.refs_1_, bf16[512,6144]{1,0:T(8,128)(2,1)} %get-tuple-element.200.refs_2_, ...), custom_call_target="tpu_custom_call" | custom-call | flops 9663676416 | bytes 25165824 | tf_op jit(solution)/shard_map/proto_pass/pallas_call | solution.py:339
  406.9 12.9 %proto_pass.3 = bf16[384,3072]{1,0:T(8,128)(2,1)S(1)} custom-call(bf16[384,2048]{1,0:T(8,128)(2,1)S(1)} %convolution_convert_fusion.n_ref, bf16[512,6144]{1,0:T(8,128)(2,1)} %get-tuple-element.198.refs_0_, f32[512,128]{1,0:T(8,128)S(1)} %broadcast_in_dim.15.refs_1_, bf16[512,6144]{1,0:T(8,128)(2,1)} %get-tuple-element.200.refs_2_, ...), custom_call_target="tpu_custom_call" | custom-call | flops 9663676416 | bytes 25165824 | tf_op jit(solution)/shard_map/proto_pass/pallas_call | solution.py:339
  425.2 3.4 collective-permute-done.48
  429.9 3.8 collective-permute-done.49
  436.3 21.8 %collective-permute-done.53 = bf16[2,2,48,3072]{3,2,1,0:T(8,128)(2,1)S(1)} collective-permute-done((bf16[2,2,48,3072]{3,2,1,0:T(8,128)(2,1)S(1)}, bf16[2,2,48,3072]{3,2,1,0:T(8,128)(2,1)S(1)}, u32[]{:S(2)}, u32[]{:S(2)}) %collective-permute-start.53) | collective-permute-done | bytes 1179680 | tf_op jit(solution)/shard_map/ppermute | solution.py:22
  461.3 3.1 collective-permute-done.80
  469.0 11.4 %grad_pass.2 = bf16[4096,512]{1,0:T(8,128)(2,1)S(1)} custom-call(bf16[4096,1024]{1,0:T(8,128)(2,1)S(1)} %bitcast.232, bf16[4096,1024]{1,0:T(8,128)(2,1)} %copy-done.5, bf16[1024,1024]{1,0:T(8,128)(2,1)S(1)} %multiply_convert_fusion.1.dnear_ref, bf16[1024,1024]{1,0:T(8,128)(2,1)S(1)} %multiply_convert_fusion.dfar_ref), custom_call_target="tpu_custom_call" | custom-call | flops 17179869184 | bytes 8388608 | tf_op jit(solution)/shard_map/grad_pass/pallas_call | solution.py:161
  480.4 11.7 %grad_pass.3 = bf16[4096,512]{1,0:T(8,128)(2,1)S(1)} custom-call(bf16[4096,1024]{1,0:T(8,128)(2,1)S(1)} %bitcast.232, bf16[4096,1024]{1,0:T(8,128)(2,1)} %copy-done.5, bf16[1024,1024]{1,0:T(8,128)(2,1)S(1)} %multiply_convert_fusion.1.dnear_ref, bf16[1024,1024]{1,0:T(8,128)(2,1)S(1)} %multiply_convert_fusion.dfar_ref), custom_call_target="tpu_custom_call" | custom-call | flops 17179869184 | bytes 8388608 | tf_op jit(solution)/shard_map/grad_pass/pallas_call | solution.py:161
  499.2 8.4 %collective-permute-done.55 = bf16[256,384]{1,0:T(8,128)(2,1)S(1)} collective-permute-done((bf16[256,384]{1,0:T(8,128)(2,1)S(1)}, bf16[256,384]{1,0:T(8,128)(2,1)S(1)}, u32[]{:S(2)}, u32[]{:S(2)}) %collective-permute-start.55) | collective-permute-done | bytes 196640 | tf_op jit(solution)/shard_map/ppermute | solution.py:22
  510.0 9.3 %collective-permute-done.82 = bf16[2,24,3072]{2,1,0:T(8,128)(2,1)S(1)} collective-permute-done((bf16[2,24,3072]{2,1,0:T(8,128)(2,1)S(1)}, bf16[2,24,3072]{2,1,0:T(8,128)(2,1)S(1)}, u32[]{:S(2)}, u32[]{:S(2)}) %collective-permute-start.82) | collective-permute-done | bytes 294944 | tf_op jit(solution)/shard_map/ppermute | solution.py:22
  523.9 17.4 %collective-permute-done.57 = bf16[2,2,512,256]{3,2,1,0:T(8,128)(2,1)S(1)} collective-permute-done((bf16[2,2,512,256]{3,2,1,0:T(8,128)(2,1)S(1)}, bf16[2,2,512,256]{3,2,1,0:T(8,128)(2,1)S(1)}, u32[]{:S(2)}, u32[]{:S(2)}) %collective-permute-start.57) | collective-permute-done | bytes 1048608 | tf_op jit(solution)/shard_map/ppermute | solution.py:22
  544.1 19.8 %collective-permute-done.70 = bf16[2,2,512,256]{3,2,1,0:T(8,128)(2,1)S(1)} collective-permute-done((bf16[2,2,512,256]{3,2,1,0:T(8,128)(2,1)S(1)}, bf16[2,2,512,256]{3,2,1,0:T(8,128)(2,1)S(1)}, u32[]{:S(2)}, u32[]{:S(2)}) %collective-permute-start.70) | collective-permute-done | bytes 1048608 | tf_op jit(solution)/shard_map/ppermute | solution.py:22
  566.3 19.6 %collective-permute-done.61 = bf16[2,2,512,256]{3,2,1,0:T(8,128)(2,1)S(1)} collective-permute-done((bf16[2,2,512,256]{3,2,1,0:T(8,128)(2,1)S(1)}, bf16[2,2,512,256]{3,2,1,0:T(8,128)(2,1)S(1)}, u32[]{:S(2)}, u32[]{:S(2)}) %collective-permute-start.61) | collective-permute-done | bytes 1048608 | tf_op jit(solution)/shard_map/ppermute | solution.py:22
  590.2 7.8 %collective-permute-start.60 = (f32[1]{0:T(128)}, f32[1]{0:T(128)}, u32[]{:S(2)}, u32[]{:S(2)}) collective-permute-start(f32[1]{0:T(128)} %add.354), channel_id=1, source_target_pairs={{0,8},{2,10},{4,12},{6,14},{8,0},{10,2},{12,4},{14,6},{16,24},{18,... | collective-permute-start | bytes 20 | tf_op jit(solution)/shard_map/ppermute | solution.py:22
  614.2 8.5 %collective-permute-done.71 = bf16[2,512,256]{2,1,0:T(8,128)(2,1)S(1)} collective-permute-done((bf16[2,512,256]{2,1,0:T(8,128)(2,1)S(1)}, bf16[2,512,256]{2,1,0:T(8,128)(2,1)S(1)}, u32[]{:S(2)}, u32[]{:S(2)}) %collective-permute-start.71) | collective-permute-done | bytes 524320 | tf_op jit(solution)/shard_map/ppermute | solution.py:22
  622.8 11.0 %collective-permute-done.74 = bf16[2,512,256]{2,1,0:T(8,128)(2,1)S(1)} collective-permute-done((bf16[2,512,256]{2,1,0:T(8,128)(2,1)S(1)}, bf16[2,512,256]{2,1,0:T(8,128)(2,1)S(1)}, u32[]{:S(2)}, u32[]{:S(2)}) %collective-permute-start.74) | collective-permute-done | bytes 524320 | tf_op jit(solution)/shard_map/ppermute | solution.py:22
  636.3 10.7 %collective-permute-done.78 = bf16[1024,384]{1,0:T(8,128)(2,1)S(1)} collective-permute-done((bf16[1024,384]{1,0:T(8,128)(2,1)S(1)}, bf16[1024,384]{1,0:T(8,128)(2,1)S(1)}, u32[]{:S(2)}, u32[]{:S(2)}) %collective-permute-start.78) | collective-permute-done | bytes 786464 | tf_op jit(solution)/shard_map/ppermute | solution.py:22
  651.8 5.6 collective-permute-done.65
  657.4 5.0 collective-permute-done.73
  (463 shorter events, 195.6 us)
Async XLA Ops:
  0.6 21.4 %collective-permute-start.7 = (bf16[512,4096]{1,0:T(8,128)(2,1)}, bf16[512,4096]{1,0:T(8,128)(2,1)}, u32[]{:S(2)}, u32[]{:S(2)}) collective-permute-start(bf16[512,4096]{1,0:T(8,128)(2,1)} %first_ref), channel_id=1, source_target_pairs={{0,2},{2,0},{4,6},{6,4},{8,10},{10,8},{12,14},{14,12},{16,18},{18,... | collective-permute-start | bytes 12582920 | tf_op jit(solution)/shard_map/ppermute | solution.py:22
  22.1 45.3 %collective-permute-start.8 = (bf16[512,1024]{1,0:T(8,128)(2,1)}, bf16[512,1024]{1,0:T(8,128)(2,1)}, u32[]{:S(2)}, u32[]{:S(2)}) collective-permute-start(bf16[512,1024]{1,0:T(8,128)(2,1)} %get-tuple-element.122), channel_id=1, source_target_pairs={{0,8},{2,10},{4,12},{6,14},{8,0},{10,2},{12,4},{14,6},{16,24},{18,... | collective-permute-start | bytes 3145736 | tf_op jit(solution)/shard_map/ppermute | solution.py:22
  23.6 43.7 %collective-permute-start.9 = (bf16[512,1024]{1,0:T(8,128)(2,1)S(1)}, bf16[512,1024]{1,0:T(8,128)(2,1)}, u32[]{:S(2)}, u32[]{:S(2)}) collective-permute-start(bf16[512,1024]{1,0:T(8,128)(2,1)S(1)} %get-tuple-element.123), channel_id=1, source_target_pairs={{0,4},{2,6},{4,0},{6,2},{8,12},{10,14},{12,8},{14,10},{16,20},{18,... | collective-permute-start | bytes 3145736 | tf_op jit(solution)/shard_map/ppermute | solution.py:22
  26.4 40.9 %collective-permute-start.10 = (bf16[512,512]{1,0:T(8,128)(2,1)S(1)}, bf16[512,512]{1,0:T(8,128)(2,1)S(1)}, u32[]{:S(2)}, u32[]{:S(2)}) collective-permute-start(bf16[512,512]{1,0:T(8,128)(2,1)S(1)} %get-tuple-element.285), channel_id=1, source_target_pairs={{0,16},{2,18},{4,20},{6,22},{8,24},{10,26},{12,28},{14,30},{16,0},... | collective-permute-start | bytes 1572872 | tf_op jit(solution)/shard_map/ppermute | solution.py:22
  29.0 38.3 %collective-permute-start.11 = (bf16[512,384]{1,0:T(8,128)(2,1)S(1)}, bf16[512,384]{1,0:T(8,128)(2,1)}, u32[]{:S(2)}, u32[]{:S(2)}) collective-permute-start(bf16[512,384]{1,0:T(8,128)(2,1)S(1)} %maximum_select_fusion.3.refs_1_), channel_id=1, source_target_pairs={{0,8},{2,10},{4,12},{6,14},{8,0},{10,2},{12,4},{14,6},{16,24},{18,... | collective-permute-start | bytes 1179656 | tf_op jit(solution)/shard_map/ppermute | solution.py:22
  67.3 35.9 %collective-permute-start.12 = (bf16[512,1024]{1,0:T(8,128)(2,1)S(1)}, bf16[512,1024]{1,0:T(8,128)(2,1)}, u32[]{:S(2)}, u32[]{:S(2)}) collective-permute-start(bf16[512,1024]{1,0:T(8,128)(2,1)S(1)} %get-tuple-element.126), channel_id=1, source_target_pairs={{0,8},{2,10},{4,12},{6,14},{8,0},{10,2},{12,4},{14,6},{16,24},{18,... | collective-permute-start | bytes 3145736 | tf_op jit(solution)/shard_map/ppermute | solution.py:22
  69.0 34.2 %collective-permute-start.13 = (bf16[512,1024]{1,0:T(8,128)(2,1)}, bf16[512,1024]{1,0:T(8,128)(2,1)S(1)}, u32[]{:S(2)}, u32[]{:S(2)}) collective-permute-start(bf16[512,1024]{1,0:T(8,128)(2,1)} %collective-permute-done.8), channel_id=1, source_target_pairs={{0,4},{2,6},{4,0},{6,2},{8,12},{10,14},{12,8},{14,10},{16,20},{18,... | collective-permute-start | bytes 3145736 | tf_op jit(solution)/shard_map/ppermute | solution.py:22
  70.5 32.7 %collective-permute-start.14 = (bf16[512,512]{1,0:T(8,128)(2,1)S(1)}, bf16[512,512]{1,0:T(8,128)(2,1)S(1)}, u32[]{:S(2)}, u32[]{:S(2)}) collective-permute-start(bf16[512,512]{1,0:T(8,128)(2,1)S(1)} %copy-done.45), channel_id=1, source_target_pairs={{0,16},{2,18},{4,20},{6,22},{8,24},{10,26},{12,28},{14,30},{16,0},... | collective-permute-start | bytes 1572872 | tf_op jit(solution)/shard_map/ppermute | solution.py:22
  73.2 30.0 %collective-permute-start.15 = (f32[512]{0:T(512)S(1)}, f32[512]{0:T(512)S(1)}, u32[]{:S(2)}, u32[]{:S(2)}) collective-permute-start(f32[512]{0:T(512)S(1)} %multiply_divide_fusion), channel_id=1, source_target_pairs={{0,8},{2,10},{4,12},{6,14},{8,0},{10,2},{12,4},{14,6},{16,24},{18,... | collective-permute-start | bytes 6152 | tf_op jit(solution)/shard_map/ppermute | solution.py:22
  103.2 39.1 %collective-permute-start.20 = (bf16[512,1024]{1,0:T(8,128)(2,1)}, bf16[512,1024]{1,0:T(8,128)(2,1)}, u32[]{:S(2)}, u32[]{:S(2)}) collective-permute-start(bf16[512,1024]{1,0:T(8,128)(2,1)} %collective-permute-done.12), channel_id=1, source_target_pairs={{0,1},{1,0},{2,3},{3,2},{4,5},{5,4},{6,7},{7,6},{8,9},{9,8},{10,11... | collective-permute-start | bytes 3145736 | tf_op jit(solution)/shard_map/ppermute | solution.py:22
  105.3 36.2 %collective-permute-start.17 = (bf16[512,1024]{1,0:T(8,128)(2,1)}, bf16[512,1024]{1,0:T(8,128)(2,1)S(1)}, u32[]{:S(2)}, u32[]{:S(2)}) collective-permute-start(bf16[512,1024]{1,0:T(8,128)(2,1)} %pad_maximum_fusion.4), channel_id=1, source_target_pairs={{0,4},{2,6},{4,0},{6,2},{8,12},{10,14},{12,8},{14,10},{16,20},{18,... | collective-permute-start | bytes 3145736 | tf_op jit(solution)/shard_map/ppermute | solution.py:22
  106.9 35.5 %collective-permute-start.16 = (bf16[512,1024]{1,0:T(8,128)(2,1)}, bf16[512,1024]{1,0:T(8,128)(2,1)}, u32[]{:S(2)}, u32[]{:S(2)}) collective-permute-start(bf16[512,1024]{1,0:T(8,128)(2,1)} %get-tuple-element.133), channel_id=1, source_target_pairs={{0,8},{2,10},{4,12},{6,14},{8,0},{10,2},{12,4},{14,6},{16,24},{18,... | collective-permute-start | bytes 3145736 | tf_op jit(solution)/shard_map/ppermute | solution.py:22
  114.0 27.5 %collective-permute-start.18 = (bf16[512,512]{1,0:T(8,128)(2,1)S(1)}, bf16[512,512]{1,0:T(8,128)(2,1)}, u32[]{:S(2)}, u32[]{:S(2)}) collective-permute-start(bf16[512,512]{1,0:T(8,128)(2,1)S(1)} %get-tuple-element.137), channel_id=1, source_target_pairs={{0,16},{2,18},{4,20},{6,22},{8,24},{10,26},{12,28},{14,30},{16,0},... | collective-permute-start | bytes 1572872 | tf_op jit(solution)/shard_map/ppermute | solution.py:22
  142.4 42.7 %collective-permute-start.24 = (bf16[512,1024]{1,0:T(8,128)(2,1)}, bf16[512,1024]{1,0:T(8,128)(2,1)S(1)}, u32[]{:S(2)}, u32[]{:S(2)}) collective-permute-start(bf16[512,1024]{1,0:T(8,128)(2,1)} %collective-permute-done.16), channel_id=1, source_target_pairs={{0,1},{1,0},{2,3},{3,2},{4,5},{5,4},{6,7},{7,6},{8,9},{9,8},{10,11... | collective-permute-start | bytes 3145736 | tf_op jit(solution)/shard_map/ppermute | solution.py:22
  145.1 39.9 %collective-permute-start.22 = (bf16[512,512]{1,0:T(8,128)(2,1)}, bf16[512,512]{1,0:T(8,128)(2,1)S(1)}, u32[]{:S(2)}, u32[]{:S(2)}) collective-permute-start(bf16[512,512]{1,0:T(8,128)(2,1)} %get-tuple-element.147), channel_id=1, source_target_pairs={{0,16},{2,18},{4,20},{6,22},{8,24},{10,26},{12,28},{14,30},{16,0},... | collective-permute-start | bytes 1572872 | tf_op jit(solution)/shard_map/ppermute | solution.py:22
  147.8 37.2 %collective-permute-start.21 = (bf16[512,512]{1,0:T(8,128)(2,1)}, bf16[512,512]{1,0:T(8,128)(2,1)S(1)}, u32[]{:S(2)}, u32[]{:S(2)}) collective-permute-start(bf16[512,512]{1,0:T(8,128)(2,1)} %collective-permute-done.18), channel_id=1, source_target_pairs={{0,4},{2,6},{4,0},{6,2},{8,12},{10,14},{12,8},{14,10},{16,20},{18,... | collective-permute-start | bytes 1572872 | tf_op jit(solution)/shard_map/ppermute | solution.py:22
  148.3 36.7 %collective-permute-start.23 = (f32[2,512]{1,0:T(2,128)S(1)}, f32[2,512]{1,0:T(2,128)S(1)}, u32[]{:S(2)}, u32[]{:S(2)}) collective-permute-start(f32[2,512]{1,0:T(2,128)S(1)} %pad_maximum_fusion.21), channel_id=1, source_target_pairs={{0,2},{2,0},{4,6},{6,4},{8,10},{10,8},{12,14},{14,12},{16,18},{18,... | collective-permute-start | bytes 12296 | tf_op jit(solution)/shard_map/ppermute | solution.py:22
  191.1 39.1 %collective-permute-start.33 = (bf16[512,4096]{1,0:T(8,128)(2,1)}, bf16[512,4096]{1,0:T(8,128)(2,1)}, u32[]{:S(2)}, u32[]{:S(2)}) collective-permute-start(bf16[512,4096]{1,0:T(8,128)(2,1)} %constant_dynamic-update-slice_fusion.10.first_ref), channel_id=1, source_target_pairs={{0,2},{2,0},{4,6},{6,4},{8,10},{10,8},{12,14},{14,12},{16,18},{18,... | collective-permute-start | bytes 12582920 | tf_op jit(solution)/shard_map/ppermute | solution.py:22
  194.7 19.9 %collective-permute-start.26 = (f32[2,2,512]{2,1,0:T(2,128)S(1)}, f32[2,2,512]{2,1,0:T(2,128)S(1)}, u32[]{:S(2)}, u32[]{:S(2)}) collective-permute-start(f32[2,2,512]{2,1,0:T(2,128)S(1)} %pad_maximum_fusion.19), channel_id=1, source_target_pairs={{0,8},{2,10},{4,12},{6,14},{8,0},{10,2},{12,4},{14,6},{16,24},{18,... | collective-permute-start | bytes 24584 | tf_op jit(solution)/shard_map/ppermute | solution.py:22
  195.5 28.0 %collective-permute-start.25 = (bf16[512,512]{1,0:T(8,128)(2,1)}, bf16[512,512]{1,0:T(8,128)(2,1)}, u32[]{:S(2)}, u32[]{:S(2)}) collective-permute-start(bf16[512,512]{1,0:T(8,128)(2,1)} %copy-done.42), channel_id=1, source_target_pairs={{0,4},{2,6},{4,0},{6,2},{8,12},{10,14},{12,8},{14,10},{16,20},{18,... | collective-permute-start | bytes 1572872 | tf_op jit(solution)/shard_map/ppermute | solution.py:22
  198.3 19.2 %collective-permute-start.27 = (bf16[1024,384]{1,0:T(8,128)(2,1)}, bf16[1024,384]{1,0:T(8,128)(2,1)}, u32[]{:S(2)}, u32[]{:S(2)}) collective-permute-start(bf16[1024,384]{1,0:T(8,128)(2,1)} %convert_element_type.94), channel_id=1, source_target_pairs={{0,8},{2,10},{4,12},{6,14},{8,0},{10,2},{12,4},{14,6},{16,24},{18,... | collective-permute-start | bytes 2359304 | tf_op jit(solution)/shard_map/ppermute | solution.py:22
  275.8 19.2 %collective-permute-start.35 = (f32[512,384]{1,0:T(8,128)S(1)}, f32[512,384]{1,0:T(8,128)S(1)}, u32[]{:S(2)}, u32[]{:S(2)}) collective-permute-start(f32[512,384]{1,0:T(8,128)S(1)} %slice_add_fusion), channel_id=1, source_target_pairs={{0,8},{2,10},{4,12},{6,14},{8,0},{10,2},{12,4},{14,6},{16,24},{18,... | collective-permute-start | bytes 2359304 | tf_op jit(solution)/shard_map/ppermute | solution.py:22
  313.6 44.3 %collective-permute-start.40 = (bf16[512,384]{1,0:T(8,128)(2,1)S(1)}, bf16[512,384]{1,0:T(8,128)(2,1)S(1)}, u32[]{:S(2)}, u32[]{:S(2)}) collective-permute-start(bf16[512,384]{1,0:T(8,128)(2,1)S(1)} %maximum_select_fusion.4.refs_1_), channel_id=1, source_target_pairs={{0,2},{2,0},{4,6},{6,4},{8,10},{10,8},{12,14},{14,12},{16,18},{18,... | collective-permute-start | bytes 1179656 | tf_op jit(solution)/shard_map/ppermute | solution.py:22
  358.1 19.6 %collective-permute-start.41 = (bf16[1024,384]{1,0:T(8,128)(2,1)S(1)}, bf16[1024,384]{1,0:T(8,128)(2,1)S(1)}, u32[]{:S(2)}, u32[]{:S(2)}) collective-permute-start(bf16[1024,384]{1,0:T(8,128)(2,1)S(1)} %convert_element_type.102), channel_id=1, source_target_pairs={{0,8},{2,10},{4,12},{6,14},{8,0},{10,2},{12,4},{14,6},{16,24},{18,... | collective-permute-start | bytes 2359304 | tf_op jit(solution)/shard_map/ppermute | solution.py:22
  404.8 28.9 %collective-permute-start.49 = (bf16[2,2,48,3072]{3,2,1,0:T(8,128)(2,1)S(1)}, bf16[2,2,48,3072]{3,2,1,0:T(8,128)(2,1)S(1)}, u32[]{:S(2)}, u32[]{:S(2)}) collective-permute-start(bf16[2,2,48,3072]{3,2,1,0:T(8,128)(2,1)S(1)} %slice_bitcast_fusion.2), channel_id=1, source_target_pairs={{0,4},{2,6},{4,0},{6,2},{8,12},{10,14},{12,8},{14,10},{16,20},{18,... | collective-permute-start | bytes 3538952 | tf_op jit(solution)/shard_map/ppermute | solution.py:22
  421.5 36.6 %collective-permute-start.53 = (bf16[2,2,48,3072]{3,2,1,0:T(8,128)(2,1)S(1)}, bf16[2,2,48,3072]{3,2,1,0:T(8,128)(2,1)S(1)}, u32[]{:S(2)}, u32[]{:S(2)}) collective-permute-start(bf16[2,2,48,3072]{3,2,1,0:T(8,128)(2,1)S(1)} %slice_bitcast_fusion), channel_id=1, source_target_pairs={{0,4},{2,6},{4,0},{6,2},{8,12},{10,14},{12,8},{14,10},{16,20},{18,... | collective-permute-start | bytes 3538952 | tf_op jit(solution)/shard_map/ppermute | solution.py:22
  433.8 24.4 %collective-permute-start.51 = (bf16[512,384]{1,0:T(8,128)(2,1)S(1)}, bf16[512,384]{1,0:T(8,128)(2,1)S(1)}, u32[]{:S(2)}, u32[]{:S(2)}) collective-permute-start(bf16[512,384]{1,0:T(8,128)(2,1)S(1)} %maximum_select_fusion.5), channel_id=1, source_target_pairs={{0,8},{2,10},{4,12},{6,14},{8,0},{10,2},{12,4},{14,6},{16,24},{18,... | collective-permute-start | bytes 1179656 | tf_op jit(solution)/shard_map/ppermute | solution.py:22
  435.0 23.4 %collective-permute-start.50 = (bf16[512,384]{1,0:T(8,128)(2,1)S(1)}, bf16[512,384]{1,0:T(8,128)(2,1)S(1)}, u32[]{:S(2)}, u32[]{:S(2)}) collective-permute-start(bf16[512,384]{1,0:T(8,128)(2,1)S(1)} %maximum_select_fusion.5), channel_id=1, source_target_pairs={{0,2},{2,0},{4,6},{6,4},{8,10},{10,8},{12,14},{14,12},{16,18},{18,... | collective-permute-start | bytes 1179656 | tf_op jit(solution)/shard_map/ppermute | solution.py:22
  435.1 29.4 %collective-permute-start.80 = (bf16[2,48,3072]{2,1,0:T(8,128)(2,1)S(1)}, bf16[2,48,3072]{2,1,0:T(8,128)(2,1)S(1)}, u32[]{:S(2)}, u32[]{:S(2)}) collective-permute-start(bf16[2,48,3072]{2,1,0:T(8,128)(2,1)S(1)} %slice_bitcast_fusion.13), channel_id=1, source_target_pairs={{0,16},{2,18},{4,20},{6,22},{8,24},{10,26},{12,28},{14,30},{16,0},... | collective-permute-start | bytes 1769480 | tf_op jit(solution)/shard_map/ppermute | solution.py:22
  464.6 31.6 %collective-permute-start.81 = (bf16[2,24,3072]{2,1,0:T(8,128)(2,1)S(1)}, bf16[2,24,3072]{2,1,0:T(8,128)(2,1)S(1)}, u32[]{:S(2)}, u32[]{:S(2)}) collective-permute-start(bf16[2,24,3072]{2,1,0:T(8,128)(2,1)S(1)} %get-tuple-element.295), channel_id=1, source_target_pairs={{0,2},{2,0},{4,6},{6,4},{8,10},{10,8},{12,14},{14,12},{16,18},{18,... | collective-permute-start | bytes 884744 | tf_op jit(solution)/shard_map/ppermute | solution.py:22
  467.7 27.3 %collective-permute-start.54 = (bf16[512,384]{1,0:T(8,128)(2,1)S(1)}, bf16[512,384]{1,0:T(8,128)(2,1)S(1)}, u32[]{:S(2)}, u32[]{:S(2)}) collective-permute-start(bf16[512,384]{1,0:T(8,128)(2,1)S(1)} %constant_dynamic-slice_fusion.4), channel_id=1, source_target_pairs={{0,4},{2,6},{4,0},{6,2},{8,12},{10,14},{12,8},{14,10},{16,20},{18,... | collective-permute-start | bytes 1179656 | tf_op jit(solution)/shard_map/ppermute | solution.py:22
  468.3 39.3 %collective-permute-start.83 = (bf16[2,48,3072]{2,1,0:T(8,128)(2,1)S(1)}, bf16[2,48,3072]{2,1,0:T(8,128)(2,1)S(1)}, u32[]{:S(2)}, u32[]{:S(2)}) collective-permute-start(bf16[2,48,3072]{2,1,0:T(8,128)(2,1)S(1)} %slice_bitcast_fusion.12), channel_id=1, source_target_pairs={{0,16},{2,18},{4,20},{6,22},{8,24},{10,26},{12,28},{14,30},{16,0},... | collective-permute-start | bytes 1769480 | tf_op jit(solution)/shard_map/ppermute | solution.py:22
  492.8 29.3 %collective-permute-start.66 = (bf16[2,2,512,256]{3,2,1,0:T(8,128)(2,1)S(1)}, bf16[2,2,512,256]{3,2,1,0:T(8,128)(2,1)S(1)}, u32[]{:S(2)}, u32[]{:S(2)}) collective-permute-start(bf16[2,2,512,256]{3,2,1,0:T(8,128)(2,1)S(1)} %slice_bitcast_fusion.6), channel_id=1, source_target_pairs={{0,4},{2,6},{4,0},{6,2},{8,12},{10,14},{12,8},{14,10},{16,20},{18,... | collective-permute-start | bytes 3145736 | tf_op jit(solution)/shard_map/ppermute | solution.py:22
  493.8 47.5 %collective-permute-start.57 = (bf16[2,2,512,256]{3,2,1,0:T(8,128)(2,1)S(1)}, bf16[2,2,512,256]{3,2,1,0:T(8,128)(2,1)S(1)}, u32[]{:S(2)}, u32[]{:S(2)}) collective-permute-start(bf16[2,2,512,256]{3,2,1,0:T(8,128)(2,1)S(1)} %slice_bitcast_fusion.10), channel_id=1, source_target_pairs={{0,4},{2,6},{4,0},{6,2},{8,12},{10,14},{12,8},{14,10},{16,20},{18,... | collective-permute-start | bytes 3145736 | tf_op jit(solution)/shard_map/ppermute | solution.py:22
  495.0 68.8 %collective-permute-start.70 = (bf16[2,2,512,256]{3,2,1,0:T(8,128)(2,1)S(1)}, bf16[2,2,512,256]{3,2,1,0:T(8,128)(2,1)S(1)}, u32[]{:S(2)}, u32[]{:S(2)}) collective-permute-start(bf16[2,2,512,256]{3,2,1,0:T(8,128)(2,1)S(1)} %slice_bitcast_fusion.4), channel_id=1, source_target_pairs={{0,4},{2,6},{4,0},{6,2},{8,12},{10,14},{12,8},{14,10},{16,20},{18,... | collective-permute-start | bytes 3145736 | tf_op jit(solution)/shard_map/ppermute | solution.py:22
  519.3 66.6 %collective-permute-start.61 = (bf16[2,2,512,256]{3,2,1,0:T(8,128)(2,1)S(1)}, bf16[2,2,512,256]{3,2,1,0:T(8,128)(2,1)S(1)}, u32[]{:S(2)}, u32[]{:S(2)}) collective-permute-start(bf16[2,2,512,256]{3,2,1,0:T(8,128)(2,1)S(1)} %slice_bitcast_fusion.8), channel_id=1, source_target_pairs={{0,4},{2,6},{4,0},{6,2},{8,12},{10,14},{12,8},{14,10},{16,20},{18,... | collective-permute-start | bytes 3145736 | tf_op jit(solution)/shard_map/ppermute | solution.py:22
  522.0 82.5 %collective-permute-start.85 = (bf16[2,24,3072]{2,1,0:T(8,128)(2,1)S(1)}, bf16[2,24,3072]{2,1,0:T(8,128)(2,1)S(1)}, u32[]{:S(2)}, u32[]{:S(2)}) collective-permute-start(bf16[2,24,3072]{2,1,0:T(8,128)(2,1)S(1)} %get-tuple-element.289), channel_id=1, source_target_pairs={{0,8},{2,10},{4,12},{6,14},{8,0},{10,2},{12,4},{14,6},{16,24},{18,... | collective-permute-start | bytes 884744 | tf_op jit(solution)/shard_map/ppermute | solution.py:22
  522.3 91.0 %collective-permute-start.67 = (bf16[2,512,256]{2,1,0:T(8,128)(2,1)S(1)}, bf16[2,512,256]{2,1,0:T(8,128)(2,1)S(1)}, u32[]{:S(2)}, u32[]{:S(2)}) collective-permute-start(bf16[2,512,256]{2,1,0:T(8,128)(2,1)S(1)} %slice_bitcast_fusion.16), channel_id=1, source_target_pairs={{0,16},{2,18},{4,20},{6,22},{8,24},{10,26},{12,28},{14,30},{16,0},... | collective-permute-start | bytes 1572872 | tf_op jit(solution)/shard_map/ppermute | solution.py:22
  541.5 46.2 %collective-permute-start.58 = (f32[1]{0:T(128)}, f32[1]{0:T(128)}, u32[]{:S(2)}, u32[]{:S(2)}) collective-permute-start(f32[1]{0:T(128)} %add.339), channel_id=1, source_target_pairs={{0,1},{1,0},{2,3},{3,2},{4,5},{5,4},{6,7},{7,6},{8,9},{9,8},{10,11... | collective-permute-start | bytes 20 | tf_op jit(solution)/shard_map/ppermute | solution.py:22
  563.8 49.7 %collective-permute-start.63 = (bf16[2,512,256]{2,1,0:T(8,128)(2,1)S(1)}, bf16[2,512,256]{2,1,0:T(8,128)(2,1)S(1)}, u32[]{:S(2)}, u32[]{:S(2)}) collective-permute-start(bf16[2,512,256]{2,1,0:T(8,128)(2,1)S(1)} %slice_bitcast_fusion.19), channel_id=1, source_target_pairs={{0,16},{2,18},{4,20},{6,22},{8,24},{10,26},{12,28},{14,30},{16,0},... | collective-permute-start | bytes 1572872 | tf_op jit(solution)/shard_map/ppermute | solution.py:22
  585.9 36.8 %collective-permute-start.71 = (bf16[2,512,256]{2,1,0:T(8,128)(2,1)S(1)}, bf16[2,512,256]{2,1,0:T(8,128)(2,1)S(1)}, u32[]{:S(2)}, u32[]{:S(2)}) collective-permute-start(bf16[2,512,256]{2,1,0:T(8,128)(2,1)S(1)} %slice_bitcast_fusion.14), channel_id=1, source_target_pairs={{0,16},{2,18},{4,20},{6,22},{8,24},{10,26},{12,28},{14,30},{16,0},... | collective-permute-start | bytes 1572872 | tf_op jit(solution)/shard_map/ppermute | solution.py:22
  604.5 29.3 %collective-permute-start.74 = (bf16[2,512,256]{2,1,0:T(8,128)(2,1)S(1)}, bf16[2,512,256]{2,1,0:T(8,128)(2,1)S(1)}, u32[]{:S(2)}, u32[]{:S(2)}) collective-permute-start(bf16[2,512,256]{2,1,0:T(8,128)(2,1)S(1)} %slice_bitcast_fusion.18), channel_id=1, source_target_pairs={{0,16},{2,18},{4,20},{6,22},{8,24},{10,26},{12,28},{14,30},{16,0},... | collective-permute-start | bytes 1572872 | tf_op jit(solution)/shard_map/ppermute | solution.py:22
  610.8 36.1 %collective-permute-start.78 = (bf16[1024,384]{1,0:T(8,128)(2,1)S(1)}, bf16[1024,384]{1,0:T(8,128)(2,1)S(1)}, u32[]{:S(2)}, u32[]{:S(2)}) collective-permute-start(bf16[1024,384]{1,0:T(8,128)(2,1)S(1)} %maximum_select_fusion.2), channel_id=1, source_target_pairs={{0,8},{2,10},{4,12},{6,14},{8,0},{10,2},{12,4},{14,6},{16,24},{18,... | collective-permute-start | bytes 2359304 | tf_op jit(solution)/shard_map/ppermute | solution.py:22
  613.4 20.6 %collective-permute-start.68 = (bf16[2,256,256]{2,1,0:T(8,128)(2,1)S(1)}, bf16[2,256,256]{2,1,0:T(8,128)(2,1)S(1)}, u32[]{:S(2)}, u32[]{:S(2)}) collective-permute-start(bf16[2,256,256]{2,1,0:T(8,128)(2,1)S(1)} %get-tuple-element.303), channel_id=1, source_target_pairs={{0,2},{2,0},{4,6},{6,4},{8,10},{10,8},{12,14},{14,12},{16,18},{18,... | collective-permute-start | bytes 786440 | tf_op jit(solution)/shard_map/ppermute | solution.py:22
  613.6 20.5 %collective-permute-start.64 = (bf16[2,256,256]{2,1,0:T(8,128)(2,1)S(1)}, bf16[2,256,256]{2,1,0:T(8,128)(2,1)S(1)}, u32[]{:S(2)}, u32[]{:S(2)}) collective-permute-start(bf16[2,256,256]{2,1,0:T(8,128)(2,1)S(1)} %get-tuple-element.299), channel_id=1, source_target_pairs={{0,2},{2,0},{4,6},{6,4},{8,10},{10,8},{12,14},{14,12},{16,18},{18,... | collective-permute-start | bytes 786440 | tf_op jit(solution)/shard_map/ppermute | solution.py:22
  622.7 24.7 %collective-permute-start.72 = (bf16[2,256,256]{2,1,0:T(8,128)(2,1)S(1)}, bf16[2,256,256]{2,1,0:T(8,128)(2,1)S(1)}, u32[]{:S(2)}, u32[]{:S(2)}) collective-permute-start(bf16[2,256,256]{2,1,0:T(8,128)(2,1)S(1)} %get-tuple-element.307), channel_id=1, source_target_pairs={{0,2},{2,0},{4,6},{6,4},{8,10},{10,8},{12,14},{14,12},{16,18},{18,... | collective-permute-start | bytes 786440 | tf_op jit(solution)/shard_map/ppermute | solution.py:22
  634.2 23.2 %collective-permute-start.65 = (bf16[2,256,256]{2,1,0:T(8,128)(2,1)S(1)}, bf16[2,256,256]{2,1,0:T(8,128)(2,1)S(1)}, u32[]{:S(2)}, u32[]{:S(2)}) collective-permute-start(bf16[2,256,256]{2,1,0:T(8,128)(2,1)S(1)} %get-tuple-element.297), channel_id=1, source_target_pairs={{0,8},{2,10},{4,12},{6,14},{8,0},{10,2},{12,4},{14,6},{16,24},{18,... | collective-permute-start | bytes 786440 | tf_op jit(solution)/shard_map/ppermute | solution.py:22
  647.4 21.0 %collective-permute-start.79 = (bf16[2,1,1024,384]{3,2,0,1:T(8,128)(2,1)S(1)}, bf16[2,1,1024,384]{3,2,0,1:T(8,128)(2,1)S(1)}, u32[]{:S(2)}, u32[]{:S(2)}) collective-permute-start(bf16[2,1,1024,384]{3,2,0,1:T(8,128)(2,1)S(1)} %bitcast.245), channel_id=1, source_target_pairs={{0,2},{2,0},{4,6},{6,4},{8,10},{10,8},{12,14},{14,12},{16,18},{18,... | collective-permute-start | bytes 4718600 | tf_op jit(solution)/shard_map/ppermute | solution.py:22
  (110 other events, 1425.6 us)

commit v3 on v2

--- a/solution.py
+++ b/solution.py
@@ -607,9 +607,11 @@
         sent = swap(after(value[:, :, 1], *before), ybit)
         return value[:, :, 0] + sent, sent
 
+    def fold_h(value):
+        return value[0] + swap(value[1], zhi)
+
     def fold(value):
         columns = value.shape[-1]
-        value = value[0] + swap(value[1], zhi)
         value = value.reshape((2, 2, -1, columns))
         value = jnp.stack([value[:, 0], swap(value[:, 1], core)], 1)
         value = jnp.stack([value[0], swap(value[1], zlo)])
@@ -635,7 +637,7 @@
         jnp.concatenate([dbott, swap(dbott, core)], 0),
         jnp.concatenate([dbott_far, swap(dbott_far, core)], 0),
     ]
-    proto_pieces[0] = fold(proto_pieces[0])
+    proto_pieces[0] = fold(fold_h(proto_pieces[0]))
 
     hidden = [jnp.concatenate(pair, 1) for pair in hiddens]
     w_out_grad = (inner(hidden[0], dbott[0]) + inner(hidden[1], dbott[1])).astype(bf16)
@@ -647,7 +649,7 @@
     ]
     back = [value.astype(bf16) for value in back]
     *back, product, proto_pieces[-1] = together(*back, product, proto_pieces[-1])
-    proto_pieces = proto_pieces[:1] + [fold(value) for value in proto_pieces[1:]]
+    proto_pieces = proto_pieces[:1] + [fold(fold_h(value)) for value in proto_pieces[1:]]
     keep, given = halves(product, ybit, "row", 0)
     w_out_grad = keep + swap(given, ybit)
     sums = []
@@ -658,19 +660,24 @@
     keep, given = halves(w_out_grad, zhi, "row", 0)
     w_out_grad = keep + swap(given, zhi)
     w_out_grad = in_order(w_out_grad, swap(w_out_grad, zhi), zhi, "row", 0)
-    w_out_grad, loss, sums[0] = together(w_out_grad, loss, sums[0])
+    w_out_grad, sums[0] = together(w_out_grad, sums[0])
+    w_out_grad, sums[-1] = together(w_out_grad, sums[-1])
+    w_out_grad = in_order(w_out_grad, swap(w_out_grad, ybit), ybit, "row", 0)
+    w_out_grad = in_order(w_out_grad, swap(w_out_grad, zlo), zlo, "row", 0)
+    sums = [fold_h(value) for value in sums]
+    loss, sums[0] = together(loss, sums[0])
+    loss = loss + swap(loss, ybit)
     for bit in proto_bits:
         loss = loss + swap(loss, bit, "proto")
-    loss = loss + swap(loss, core)
-    loss = loss + swap(loss, zlo)
-    w_out_grad, loss, sums[-1] = together(w_out_grad, loss, sums[-1])
-    w_out_grad = in_order(w_out_grad, swap(w_out_grad, ybit), ybit, "row", 0)
-    w_out_grad = in_order(w_out_grad, swap(w_out_grad, zlo), zlo, "row", 0)
-    w_in_pieces = [fold(value) for value in sums]
+    for bit in (core, zlo):
+        loss = loss + swap(loss, bit)
+    early = [fold(value) for value in sums[:-2]]
+    loss, sums[-2], *early = together(loss, sums[-2], *early)
+    loss = loss[0]
+    w_in_pieces = early + [fold(value) for value in sums[-2:]]
     w_out_grad = w_out_grad.reshape((2, 1, quarter, -1))
     w_out_grad = in_order(w_out_grad, swap(w_out_grad, core), core, "row", 1)
     w_out_grad = w_out_grad.reshape((4 * quarter, -1))
-    loss = (loss + swap(loss, ybit))[0]
     return (loss, spread(w_in_pieces), w_out_grad.astype(f32), spread(proto_pieces))
 
 

time: 678 us -> 673 us (level)
  starting transfers between devices: 98.8 us -> 89.4 us
    ppermute x86, starting transfers between devices: 98.8 us -> 89.4 us  [swap(): return lax.ppermute(value, axis, [(i, i ^ bit) for i in range(size)])]
where the time goes in v3:
time: 673 us; the launch traced here: 669 us
  waiting for transfers between devices  268 us (40%)
  Pallas kernels  185 us (27%)
  starting transfers between devices  89.4 us (13%)
  local copies, waits for them, and re-layouts  59 us (9%)
  matrix products  33.2 us (5%)
  other arithmetic  26.5 us (4%)
  between operations  8.14 us (1%)
    ppermute x86, waiting for transfers between devices, swap(): return lax.ppermute(value, axis, [(i, i ^ bit) for i in range(size)])  268 us
    pallas_call x6, Pallas kernels, softmax_pass(): pl.pallas_call(functools.partial(softmax_body, log2e / tau, tile_of(count...  99.5 us
    ppermute x86, starting transfers between devices, swap(): return lax.ppermute(value, axis, [(i, i ^ bit) for i in range(size)])  89.4 us
    unnamed x163, local copies, waits for them, and re-layouts  35.7 us
    dot_general x4, matrix products, dot(): return jnp.dot(left, right, preferred_element_type=f32)  26 us
    pallas_call x2, Pallas kernels, proto_pass(): pl.pallas_call(functools.partial(proto_body, len(blocks)), out_shape=jax....  25.6 us
    pallas_call x2, Pallas kernels, grad_pass(): pl.pallas_call(grad_body, out_shape=jax.ShapeDtypeStruct((features, wide)...  23 us
    pallas_call x4, Pallas kernels, head_pass(): pl.pallas_call(head_body, out_shape=(jax.ShapeDtypeStruct((count, wide),...  16.7 us
  transfers between devices with their start and end apart: 86, of which 40 were waited for; matrix products, arithmetic and copies ran while one was open for 11% of the time, Pallas kernels for 25%

profile of v3, /device:TPU:0, one launch (start us, length us, event | category | flops | bytes accessed | tf_op | source)
XLA Modules:
  0.0 669.3 jit_solution(5512210481146209573)
XLA Ops:
  32.2 35.1 %collective-permute-done.11 = bf16[512,384]{1,0:T(8,128)(2,1)} collective-permute-done((bf16[512,384]{1,0:T(8,128)(2,1)S(1)}, bf16[512,384]{1,0:T(8,128)(2,1)}, u32[]{:S(2)}, u32[]{:S(2)}) %collective-permute-start.11) | collective-permute-done | bytes 393248 | tf_op jit(solution)/shard_map/ppermute | solution.py:22
  73.7 13.4 %softmax_pass.6 = (bf16[512,6144]{1,0:T(8,128)(2,1)}, f32[512,384]{1,0:T(8,128)S(1)}, f32[512,128]{1,0:T(8,128)S(1)}) custom-call(s32[1]{0:T(128)} %bitcast.refs_0_, bf16[512,384]{1,0:T(8,128)(2,1)S(1)} %maximum_select_fusion.3.refs_1_, bf16[384,24576]{1,0:T(8,128)(2,1)} %refs_2_.8, f32[1,24576]{1,0:T(1,128)S(1)} %bitcast.233, bf16[384,24576]{1,0:T(8,128)(2,1)} %refs_3_.5), custom_call_target="tpu_custom_call" | custom-call | flops 301989888 | bytes 786432 | tf_op jit(solution)/shard_map/softmax_pass/pallas_call | solution.py:224
  88.0 15.2 %collective-permute-done.15 = f32[512]{0:T(512)S(1)} collective-permute-done((f32[512]{0:T(512)S(1)}, f32[512]{0:T(512)S(1)}, u32[]{:S(2)}, u32[]{:S(2)}) %collective-permute-start.15) | collective-permute-done | bytes 2080 | tf_op jit(solution)/shard_map/ppermute | solution.py:22
  116.9 13.3 %softmax_pass.7 = (bf16[512,6144]{1,0:T(8,128)(2,1)}, f32[512,384]{1,0:T(8,128)S(1)}, f32[512,128]{1,0:T(8,128)S(1)}) custom-call(s32[1]{0:T(128)} %bitcast.refs_0_, bf16[512,384]{1,0:T(8,128)(2,1)S(1)} %collective-permute-done.6.refs_1_, bf16[384,24576]{1,0:T(8,128)(2,1)} %refs_2_.8, f32[1,24576]{1,0:T(1,128)S(1)} %bitcast.234, bf16[384,24576]{1,0:T(8,128)(2,1)} %refs_3_.5), custom_call_target="tpu_custom_call" | custom-call | flops 301989888 | bytes 786432 | tf_op jit(solution)/shard_map/softmax_pass/pallas_call | solution.py:224
  131.1 10.4 %collective-permute-done.18 = bf16[512,512]{1,0:T(8,128)(2,1)} collective-permute-done((bf16[512,512]{1,0:T(8,128)(2,1)S(1)}, bf16[512,512]{1,0:T(8,128)(2,1)}, u32[]{:S(2)}, u32[]{:S(2)}) %collective-permute-start.18) | collective-permute-done | bytes 524320 | tf_op jit(solution)/shard_map/ppermute | solution.py:22
  151.8 23.0 %softmax_pass.8 = (bf16[1024,6144]{1,0:T(8,128)(2,1)}, f32[1024,384]{1,0:T(8,128)S(1)}, f32[1024,128]{1,0:T(8,128)S(1)}) custom-call(s32[1]{0:T(128)} %bitcast.refs_0_, bf16[1024,384]{1,0:T(8,128)(2,1)S(1)} %pad_maximum_fusion.5.refs_1_, bf16[384,24576]{1,0:T(8,128)(2,1)} %refs_2_.8, f32[1,24576]{1,0:T(1,128)S(1)} %bitcast.235, bf16[384,24576]{1,0:T(8,128)(2,1)} %refs_3_.5), custom_call_target="tpu_custom_call" | custom-call | flops 603979776 | bytes 1572864 | tf_op jit(solution)/shard_map/softmax_pass/pallas_call | solution.py:224
  175.7 6.1 permute_columns.2.rows_ref.in_ref
  181.8 3.2 copy-done
  200.4 6.8 %fusion.4.early_ref = f32[1024,512]{1,0:T(8,128)S(1)} fusion(bf16[3072,512]{1,0:T(8,128)(2,1)} %get-tuple-element.280, bf16[1024,4096]{1,0:T(8,128)(2,1)} %copy-done), kind=kOutput, calls=%fused_computation.4 | convolution fusion | flops 3221225472 | bytes 11534336 | tf_op jit(solution)/shard_map/dot_general | solution.py:76
  207.4 4.1 head_pass.4
  224.7 4.7 collective-permute-done.31
  230.2 6.8 %permute_columns.3.rows_ref.in_ref = bf16[1024,4096]{1,0:T(8,128)(2,1)S(1)} custom-call(s32[16]{0:T(128)S(1)} %fusion.129.order_ref, bf16[512,4096]{1,0:T(8,128)(2,1)} %constant_dynamic-update-slice_fusion.10.first_ref, bf16[512,4096]{1,0:T(8,128)(2,1)} %collective-permute-done.33.second_ref), custom_call_target="tpu_custom_call" | custom-call | bytes 8388608 | tf_op jit(solution)/shard_map/permute_columns/pallas_call | solution.py:112
  237.0 7.7 %fusion.early_ref = f32[1024,512]{1,0:T(8,128)S(1)} fusion(bf16[3072,512]{1,0:T(8,128)(2,1)} %get-tuple-element.280, bf16[1024,4096]{1,0:T(8,128)(2,1)S(1)} %permute_columns.3.rows_ref.in_ref), kind=kOutput, calls=%fused_computation | convolution fusion | flops 3221225472 | bytes 11534336 | tf_op jit(solution)/shard_map/dot_general | solution.py:76
  244.8 4.5 head_pass.6
  251.3 5.4 fusion.2.early_ref
  256.8 3.4 copy-done.2
  260.1 4.0 head_pass.7
  264.4 6.0 fusion.6.early_ref
  270.4 4.1 head_pass.5
  276.9 3.5 turn_rows.2.near_ref
  280.4 14.6 %collective-permute-done.35 = f32[512,384]{1,0:T(8,128)S(1)} collective-permute-done((f32[512,384]{1,0:T(8,128)S(1)}, f32[512,384]{1,0:T(8,128)S(1)}, u32[]{:S(2)}, u32[]{:S(2)}) %collective-permute-start.35) | collective-permute-done | bytes 786464 | tf_op jit(solution)/shard_map/ppermute | solution.py:22
  296.4 3.5 turn_rows.3.far_ref
  299.9 3.3 copy-done.5
  306.6 4.5 collective-permute-done.37
  313.6 5.5 collective-permute-done.38
  319.1 13.5 %softmax_pass.9 = (bf16[512,6144]{1,0:T(8,128)(2,1)}, f32[512,384]{1,0:T(8,128)S(1)}, f32[512,128]{1,0:T(8,128)S(1)}) custom-call(s32[1]{0:T(128)} %bitcast.refs_0_, bf16[512,384]{1,0:T(8,128)(2,1)S(1)} %maximum_select_fusion.4.refs_1_, bf16[384,24576]{1,0:T(8,128)(2,1)} %refs_3_.5, bf16[384,24576]{1,0:T(8,128)(2,1)} %refs_3_.5), custom_call_target="tpu_custom_call" | custom-call | flops 7247757312 | bytes 6291456 | tf_op jit(solution)/shard_map/softmax_pass/pallas_call | solution.py:224
  334.3 22.8 %softmax_pass.10 = (bf16[1024,6144]{1,0:T(8,128)(2,1)}, f32[1024,384]{1,0:T(8,128)S(1)}, f32[1024,128]{1,0:T(8,128)S(1)}) custom-call(s32[1]{0:T(128)} %bitcast.refs_0_, bf16[1024,384]{1,0:T(8,128)(2,1)S(1)} %pad_maximum_fusion.6.refs_1_, bf16[384,24576]{1,0:T(8,128)(2,1)} %refs_3_.5, bf16[384,24576]{1,0:T(8,128)(2,1)} %refs_3_.5), custom_call_target="tpu_custom_call" | custom-call | flops 14495514624 | bytes 12582912 | tf_op jit(solution)/shard_map/softmax_pass/pallas_call | solution.py:224
  358.8 13.6 %softmax_pass.11 = (bf16[512,6144]{1,0:T(8,128)(2,1)}, f32[512,384]{1,0:T(8,128)S(1)}, f32[512,128]{1,0:T(8,128)S(1)}) custom-call(s32[1]{0:T(128)} %bitcast.refs_0_, bf16[512,384]{1,0:T(8,128)(2,1)S(1)} %collective-permute-done.40.refs_1_, bf16[384,24576]{1,0:T(8,128)(2,1)} %refs_3_.5, bf16[384,24576]{1,0:T(8,128)(2,1)} %refs_3_.5), custom_call_target="tpu_custom_call" | custom-call | flops 7247757312 | bytes 6291456 | tf_op jit(solution)/shard_map/softmax_pass/pallas_call | solution.py:224
  373.2 4.4 collective-permute-done.41
  392.0 12.7 %proto_pass.2 = bf16[384,3072]{1,0:T(8,128)(2,1)S(1)} custom-call(bf16[384,2048]{1,0:T(8,128)(2,1)S(1)} %convolution_convert_fusion.n_ref, bf16[512,6144]{1,0:T(8,128)(2,1)} %get-tuple-element.202.refs_0_, f32[512,128]{1,0:T(8,128)S(1)} %broadcast_in_dim.15.refs_1_, bf16[512,6144]{1,0:T(8,128)(2,1)} %get-tuple-element.204.refs_2_, ...), custom_call_target="tpu_custom_call" | custom-call | flops 9663676416 | bytes 25165824 | tf_op jit(solution)/shard_map/proto_pass/pallas_call | solution.py:339
  406.9 12.9 %proto_pass.3 = bf16[384,3072]{1,0:T(8,128)(2,1)S(1)} custom-call(bf16[384,2048]{1,0:T(8,128)(2,1)S(1)} %convolution_convert_fusion.n_ref, bf16[512,6144]{1,0:T(8,128)(2,1)} %get-tuple-element.202.refs_0_, f32[512,128]{1,0:T(8,128)S(1)} %broadcast_in_dim.15.refs_1_, bf16[512,6144]{1,0:T(8,128)(2,1)} %get-tuple-element.204.refs_2_, ...), custom_call_target="tpu_custom_call" | custom-call | flops 9663676416 | bytes 25165824 | tf_op jit(solution)/shard_map/proto_pass/pallas_call | solution.py:339
  425.2 3.4 collective-permute-done.48
  429.9 3.8 collective-permute-done.49
  436.3 21.8 %collective-permute-done.53 = bf16[2,2,48,3072]{3,2,1,0:T(8,128)(2,1)S(1)} collective-permute-done((bf16[2,2,48,3072]{3,2,1,0:T(8,128)(2,1)S(1)}, bf16[2,2,48,3072]{3,2,1,0:T(8,128)(2,1)S(1)}, u32[]{:S(2)}, u32[]{:S(2)}) %collective-permute-start.53) | collective-permute-done | bytes 1179680 | tf_op jit(solution)/shard_map/ppermute | solution.py:22
  469.0 11.4 %grad_pass.2 = bf16[4096,512]{1,0:T(8,128)(2,1)S(1)} custom-call(bf16[4096,1024]{1,0:T(8,128)(2,1)S(1)} %bitcast.232, bf16[4096,1024]{1,0:T(8,128)(2,1)} %copy-done.5, bf16[1024,1024]{1,0:T(8,128)(2,1)S(1)} %multiply_convert_fusion.1.dnear_ref, bf16[1024,1024]{1,0:T(8,128)(2,1)S(1)} %multiply_convert_fusion.dfar_ref), custom_call_target="tpu_custom_call" | custom-call | flops 17179869184 | bytes 8388608 | tf_op jit(solution)/shard_map/grad_pass/pallas_call | solution.py:161
  480.4 11.7 %grad_pass.3 = bf16[4096,512]{1,0:T(8,128)(2,1)S(1)} custom-call(bf16[4096,1024]{1,0:T(8,128)(2,1)S(1)} %bitcast.232, bf16[4096,1024]{1,0:T(8,128)(2,1)} %copy-done.5, bf16[1024,1024]{1,0:T(8,128)(2,1)S(1)} %multiply_convert_fusion.1.dnear_ref, bf16[1024,1024]{1,0:T(8,128)(2,1)S(1)} %multiply_convert_fusion.dfar_ref), custom_call_target="tpu_custom_call" | custom-call | flops 17179869184 | bytes 8388608 | tf_op jit(solution)/shard_map/grad_pass/pallas_call | solution.py:161
  499.2 8.4 %collective-permute-done.55 = bf16[256,384]{1,0:T(8,128)(2,1)S(1)} collective-permute-done((bf16[256,384]{1,0:T(8,128)(2,1)S(1)}, bf16[256,384]{1,0:T(8,128)(2,1)S(1)}, u32[]{:S(2)}, u32[]{:S(2)}) %collective-permute-start.55) | collective-permute-done | bytes 196640 | tf_op jit(solution)/shard_map/ppermute | solution.py:22
  510.0 9.3 %collective-permute-done.82 = bf16[2,24,3072]{2,1,0:T(8,128)(2,1)S(1)} collective-permute-done((bf16[2,24,3072]{2,1,0:T(8,128)(2,1)S(1)}, bf16[2,24,3072]{2,1,0:T(8,128)(2,1)S(1)}, u32[]{:S(2)}, u32[]{:S(2)}) %collective-permute-start.82) | collective-permute-done | bytes 294944 | tf_op jit(solution)/shard_map/ppermute | solution.py:22
  523.9 17.4 %collective-permute-done.57 = bf16[2,2,512,256]{3,2,1,0:T(8,128)(2,1)S(1)} collective-permute-done((bf16[2,2,512,256]{3,2,1,0:T(8,128)(2,1)S(1)}, bf16[2,2,512,256]{3,2,1,0:T(8,128)(2,1)S(1)}, u32[]{:S(2)}, u32[]{:S(2)}) %collective-permute-start.57) | collective-permute-done | bytes 1048608 | tf_op jit(solution)/shard_map/ppermute | solution.py:22
  543.9 19.9 %collective-permute-done.73 = bf16[2,2,512,256]{3,2,1,0:T(8,128)(2,1)S(1)} collective-permute-done((bf16[2,2,512,256]{3,2,1,0:T(8,128)(2,1)S(1)}, bf16[2,2,512,256]{3,2,1,0:T(8,128)(2,1)S(1)}, u32[]{:S(2)}, u32[]{:S(2)}) %collective-permute-start.73) | collective-permute-done | bytes 1048608 | tf_op jit(solution)/shard_map/ppermute | solution.py:22
  565.0 21.3 %collective-permute-done.63 = bf16[2,2,512,256]{3,2,1,0:T(8,128)(2,1)S(1)} collective-permute-done((bf16[2,2,512,256]{3,2,1,0:T(8,128)(2,1)S(1)}, bf16[2,2,512,256]{3,2,1,0:T(8,128)(2,1)S(1)}, u32[]{:S(2)}, u32[]{:S(2)}) %collective-permute-start.63) | collective-permute-done | bytes 1048608 | tf_op jit(solution)/shard_map/ppermute | solution.py:22
  589.6 4.7 collective-permute-done.77
  598.9 23.8 %collective-permute-done.74 = bf16[2,512,256]{2,1,0:T(8,128)(2,1)S(1)} collective-permute-done((bf16[2,512,256]{2,1,0:T(8,128)(2,1)S(1)}, bf16[2,512,256]{2,1,0:T(8,128)(2,1)S(1)}, u32[]{:S(2)}, u32[]{:S(2)}) %collective-permute-start.74) | collective-permute-done | bytes 524320 | tf_op jit(solution)/shard_map/ppermute | solution.py:22
  624.2 9.6 %collective-permute-done.64 = bf16[2,512,256]{2,1,0:T(8,128)(2,1)S(1)} collective-permute-done((bf16[2,512,256]{2,1,0:T(8,128)(2,1)S(1)}, bf16[2,512,256]{2,1,0:T(8,128)(2,1)S(1)}, u32[]{:S(2)}, u32[]{:S(2)}) %collective-permute-start.64) | collective-permute-done | bytes 524320 | tf_op jit(solution)/shard_map/ppermute | solution.py:22
  640.6 3.4 collective-permute-start.62
  644.0 3.5 collective-permute-done.62
  653.7 3.6 collective-permute-done.76
  657.4 3.5 collective-permute-done.72
  (463 shorter events, 189.1 us)
Async XLA Ops:
  0.6 21.4 %collective-permute-start.7 = (bf16[512,4096]{1,0:T(8,128)(2,1)}, bf16[512,4096]{1,0:T(8,128)(2,1)}, u32[]{:S(2)}, u32[]{:S(2)}) collective-permute-start(bf16[512,4096]{1,0:T(8,128)(2,1)} %first_ref), channel_id=1, source_target_pairs={{0,2},{2,0},{4,6},{6,4},{8,10},{10,8},{12,14},{14,12},{16,18},{18,... | collective-permute-start | bytes 12582920 | tf_op jit(solution)/shard_map/ppermute | solution.py:22
  22.1 45.3 %collective-permute-start.8 = (bf16[512,1024]{1,0:T(8,128)(2,1)}, bf16[512,1024]{1,0:T(8,128)(2,1)}, u32[]{:S(2)}, u32[]{:S(2)}) collective-permute-start(bf16[512,1024]{1,0:T(8,128)(2,1)} %get-tuple-element.126), channel_id=1, source_target_pairs={{0,8},{2,10},{4,12},{6,14},{8,0},{10,2},{12,4},{14,6},{16,24},{18,... | collective-permute-start | bytes 3145736 | tf_op jit(solution)/shard_map/ppermute | solution.py:22
  23.6 43.7 %collective-permute-start.9 = (bf16[512,1024]{1,0:T(8,128)(2,1)S(1)}, bf16[512,1024]{1,0:T(8,128)(2,1)}, u32[]{:S(2)}, u32[]{:S(2)}) collective-permute-start(bf16[512,1024]{1,0:T(8,128)(2,1)S(1)} %get-tuple-element.127), channel_id=1, source_target_pairs={{0,4},{2,6},{4,0},{6,2},{8,12},{10,14},{12,8},{14,10},{16,20},{18,... | collective-permute-start | bytes 3145736 | tf_op jit(solution)/shard_map/ppermute | solution.py:22
  26.4 40.9 %collective-permute-start.10 = (bf16[512,512]{1,0:T(8,128)(2,1)S(1)}, bf16[512,512]{1,0:T(8,128)(2,1)S(1)}, u32[]{:S(2)}, u32[]{:S(2)}) collective-permute-start(bf16[512,512]{1,0:T(8,128)(2,1)S(1)} %get-tuple-element.293), channel_id=1, source_target_pairs={{0,16},{2,18},{4,20},{6,22},{8,24},{10,26},{12,28},{14,30},{16,0},... | collective-permute-start | bytes 1572872 | tf_op jit(solution)/shard_map/ppermute | solution.py:22
  29.0 38.3 %collective-permute-start.11 = (bf16[512,384]{1,0:T(8,128)(2,1)S(1)}, bf16[512,384]{1,0:T(8,128)(2,1)}, u32[]{:S(2)}, u32[]{:S(2)}) collective-permute-start(bf16[512,384]{1,0:T(8,128)(2,1)S(1)} %maximum_select_fusion.3.refs_1_), channel_id=1, source_target_pairs={{0,8},{2,10},{4,12},{6,14},{8,0},{10,2},{12,4},{14,6},{16,24},{18,... | collective-permute-start | bytes 1179656 | tf_op jit(solution)/shard_map/ppermute | solution.py:22
  67.3 35.9 %collective-permute-start.12 = (bf16[512,1024]{1,0:T(8,128)(2,1)S(1)}, bf16[512,1024]{1,0:T(8,128)(2,1)}, u32[]{:S(2)}, u32[]{:S(2)}) collective-permute-start(bf16[512,1024]{1,0:T(8,128)(2,1)S(1)} %get-tuple-element.130), channel_id=1, source_target_pairs={{0,8},{2,10},{4,12},{6,14},{8,0},{10,2},{12,4},{14,6},{16,24},{18,... | collective-permute-start | bytes 3145736 | tf_op jit(solution)/shard_map/ppermute | solution.py:22
  69.0 34.2 %collective-permute-start.13 = (bf16[512,1024]{1,0:T(8,128)(2,1)}, bf16[512,1024]{1,0:T(8,128)(2,1)S(1)}, u32[]{:S(2)}, u32[]{:S(2)}) collective-permute-start(bf16[512,1024]{1,0:T(8,128)(2,1)} %collective-permute-done.8), channel_id=1, source_target_pairs={{0,4},{2,6},{4,0},{6,2},{8,12},{10,14},{12,8},{14,10},{16,20},{18,... | collective-permute-start | bytes 3145736 | tf_op jit(solution)/shard_map/ppermute | solution.py:22
  70.5 32.7 %collective-permute-start.14 = (bf16[512,512]{1,0:T(8,128)(2,1)S(1)}, bf16[512,512]{1,0:T(8,128)(2,1)S(1)}, u32[]{:S(2)}, u32[]{:S(2)}) collective-permute-start(bf16[512,512]{1,0:T(8,128)(2,1)S(1)} %copy-done.45), channel_id=1, source_target_pairs={{0,16},{2,18},{4,20},{6,22},{8,24},{10,26},{12,28},{14,30},{16,0},... | collective-permute-start | bytes 1572872 | tf_op jit(solution)/shard_map/ppermute | solution.py:22
  73.2 30.0 %collective-permute-start.15 = (f32[512]{0:T(512)S(1)}, f32[512]{0:T(512)S(1)}, u32[]{:S(2)}, u32[]{:S(2)}) collective-permute-start(f32[512]{0:T(512)S(1)} %multiply_divide_fusion), channel_id=1, source_target_pairs={{0,8},{2,10},{4,12},{6,14},{8,0},{10,2},{12,4},{14,6},{16,24},{18,... | collective-permute-start | bytes 6152 | tf_op jit(solution)/shard_map/ppermute | solution.py:22
  103.2 39.1 %collective-permute-start.20 = (bf16[512,1024]{1,0:T(8,128)(2,1)}, bf16[512,1024]{1,0:T(8,128)(2,1)}, u32[]{:S(2)}, u32[]{:S(2)}) collective-permute-start(bf16[512,1024]{1,0:T(8,128)(2,1)} %collective-permute-done.12), channel_id=1, source_target_pairs={{0,1},{1,0},{2,3},{3,2},{4,5},{5,4},{6,7},{7,6},{8,9},{9,8},{10,11... | collective-permute-start | bytes 3145736 | tf_op jit(solution)/shard_map/ppermute | solution.py:22
  105.3 36.2 %collective-permute-start.17 = (bf16[512,1024]{1,0:T(8,128)(2,1)}, bf16[512,1024]{1,0:T(8,128)(2,1)S(1)}, u32[]{:S(2)}, u32[]{:S(2)}) collective-permute-start(bf16[512,1024]{1,0:T(8,128)(2,1)} %pad_maximum_fusion.4), channel_id=1, source_target_pairs={{0,4},{2,6},{4,0},{6,2},{8,12},{10,14},{12,8},{14,10},{16,20},{18,... | collective-permute-start | bytes 3145736 | tf_op jit(solution)/shard_map/ppermute | solution.py:22
  106.9 35.5 %collective-permute-start.16 = (bf16[512,1024]{1,0:T(8,128)(2,1)}, bf16[512,1024]{1,0:T(8,128)(2,1)}, u32[]{:S(2)}, u32[]{:S(2)}) collective-permute-start(bf16[512,1024]{1,0:T(8,128)(2,1)} %get-tuple-element.137), channel_id=1, source_target_pairs={{0,8},{2,10},{4,12},{6,14},{8,0},{10,2},{12,4},{14,6},{16,24},{18,... | collective-permute-start | bytes 3145736 | tf_op jit(solution)/shard_map/ppermute | solution.py:22
  114.0 27.5 %collective-permute-start.18 = (bf16[512,512]{1,0:T(8,128)(2,1)S(1)}, bf16[512,512]{1,0:T(8,128)(2,1)}, u32[]{:S(2)}, u32[]{:S(2)}) collective-permute-start(bf16[512,512]{1,0:T(8,128)(2,1)S(1)} %get-tuple-element.141), channel_id=1, source_target_pairs={{0,16},{2,18},{4,20},{6,22},{8,24},{10,26},{12,28},{14,30},{16,0},... | collective-permute-start | bytes 1572872 | tf_op jit(solution)/shard_map/ppermute | solution.py:22
  142.4 42.7 %collective-permute-start.24 = (bf16[512,1024]{1,0:T(8,128)(2,1)}, bf16[512,1024]{1,0:T(8,128)(2,1)S(1)}, u32[]{:S(2)}, u32[]{:S(2)}) collective-permute-start(bf16[512,1024]{1,0:T(8,128)(2,1)} %collective-permute-done.16), channel_id=1, source_target_pairs={{0,1},{1,0},{2,3},{3,2},{4,5},{5,4},{6,7},{7,6},{8,9},{9,8},{10,11... | collective-permute-start | bytes 3145736 | tf_op jit(solution)/shard_map/ppermute | solution.py:22
  145.1 39.9 %collective-permute-start.22 = (bf16[512,512]{1,0:T(8,128)(2,1)}, bf16[512,512]{1,0:T(8,128)(2,1)S(1)}, u32[]{:S(2)}, u32[]{:S(2)}) collective-permute-start(bf16[512,512]{1,0:T(8,128)(2,1)} %get-tuple-element.151), channel_id=1, source_target_pairs={{0,16},{2,18},{4,20},{6,22},{8,24},{10,26},{12,28},{14,30},{16,0},... | collective-permute-start | bytes 1572872 | tf_op jit(solution)/shard_map/ppermute | solution.py:22
  147.8 37.2 %collective-permute-start.21 = (bf16[512,512]{1,0:T(8,128)(2,1)}, bf16[512,512]{1,0:T(8,128)(2,1)S(1)}, u32[]{:S(2)}, u32[]{:S(2)}) collective-permute-start(bf16[512,512]{1,0:T(8,128)(2,1)} %collective-permute-done.18), channel_id=1, source_target_pairs={{0,4},{2,6},{4,0},{6,2},{8,12},{10,14},{12,8},{14,10},{16,20},{18,... | collective-permute-start | bytes 1572872 | tf_op jit(solution)/shard_map/ppermute | solution.py:22
  148.3 36.7 %collective-permute-start.23 = (f32[2,512]{1,0:T(2,128)S(1)}, f32[2,512]{1,0:T(2,128)S(1)}, u32[]{:S(2)}, u32[]{:S(2)}) collective-permute-start(f32[2,512]{1,0:T(2,128)S(1)} %pad_maximum_fusion.21), channel_id=1, source_target_pairs={{0,2},{2,0},{4,6},{6,4},{8,10},{10,8},{12,14},{14,12},{16,18},{18,... | collective-permute-start | bytes 12296 | tf_op jit(solution)/shard_map/ppermute | solution.py:22
  191.1 39.1 %collective-permute-start.33 = (bf16[512,4096]{1,0:T(8,128)(2,1)}, bf16[512,4096]{1,0:T(8,128)(2,1)}, u32[]{:S(2)}, u32[]{:S(2)}) collective-permute-start(bf16[512,4096]{1,0:T(8,128)(2,1)} %constant_dynamic-update-slice_fusion.10.first_ref), channel_id=1, source_target_pairs={{0,2},{2,0},{4,6},{6,4},{8,10},{10,8},{12,14},{14,12},{16,18},{18,... | collective-permute-start | bytes 12582920 | tf_op jit(solution)/shard_map/ppermute | solution.py:22
  194.7 19.9 %collective-permute-start.26 = (f32[2,2,512]{2,1,0:T(2,128)S(1)}, f32[2,2,512]{2,1,0:T(2,128)S(1)}, u32[]{:S(2)}, u32[]{:S(2)}) collective-permute-start(f32[2,2,512]{2,1,0:T(2,128)S(1)} %pad_maximum_fusion.19), channel_id=1, source_target_pairs={{0,8},{2,10},{4,12},{6,14},{8,0},{10,2},{12,4},{14,6},{16,24},{18,... | collective-permute-start | bytes 24584 | tf_op jit(solution)/shard_map/ppermute | solution.py:22
  195.5 28.0 %collective-permute-start.25 = (bf16[512,512]{1,0:T(8,128)(2,1)}, bf16[512,512]{1,0:T(8,128)(2,1)}, u32[]{:S(2)}, u32[]{:S(2)}) collective-permute-start(bf16[512,512]{1,0:T(8,128)(2,1)} %copy-done.42), channel_id=1, source_target_pairs={{0,4},{2,6},{4,0},{6,2},{8,12},{10,14},{12,8},{14,10},{16,20},{18,... | collective-permute-start | bytes 1572872 | tf_op jit(solution)/shard_map/ppermute | solution.py:22
  198.3 19.2 %collective-permute-start.27 = (bf16[1024,384]{1,0:T(8,128)(2,1)}, bf16[1024,384]{1,0:T(8,128)(2,1)}, u32[]{:S(2)}, u32[]{:S(2)}) collective-permute-start(bf16[1024,384]{1,0:T(8,128)(2,1)} %convert_element_type.94), channel_id=1, source_target_pairs={{0,8},{2,10},{4,12},{6,14},{8,0},{10,2},{12,4},{14,6},{16,24},{18,... | collective-permute-start | bytes 2359304 | tf_op jit(solution)/shard_map/ppermute | solution.py:22
  275.8 19.2 %collective-permute-start.35 = (f32[512,384]{1,0:T(8,128)S(1)}, f32[512,384]{1,0:T(8,128)S(1)}, u32[]{:S(2)}, u32[]{:S(2)}) collective-permute-start(f32[512,384]{1,0:T(8,128)S(1)} %slice_add_fusion), channel_id=1, source_target_pairs={{0,8},{2,10},{4,12},{6,14},{8,0},{10,2},{12,4},{14,6},{16,24},{18,... | collective-permute-start | bytes 2359304 | tf_op jit(solution)/shard_map/ppermute | solution.py:22
  313.6 44.3 %collective-permute-start.40 = (bf16[512,384]{1,0:T(8,128)(2,1)S(1)}, bf16[512,384]{1,0:T(8,128)(2,1)S(1)}, u32[]{:S(2)}, u32[]{:S(2)}) collective-permute-start(bf16[512,384]{1,0:T(8,128)(2,1)S(1)} %maximum_select_fusion.4.refs_1_), channel_id=1, source_target_pairs={{0,2},{2,0},{4,6},{6,4},{8,10},{10,8},{12,14},{14,12},{16,18},{18,... | collective-permute-start | bytes 1179656 | tf_op jit(solution)/shard_map/ppermute | solution.py:22
  358.1 19.6 %collective-permute-start.41 = (bf16[1024,384]{1,0:T(8,128)(2,1)S(1)}, bf16[1024,384]{1,0:T(8,128)(2,1)S(1)}, u32[]{:S(2)}, u32[]{:S(2)}) collective-permute-start(bf16[1024,384]{1,0:T(8,128)(2,1)S(1)} %convert_element_type.102), channel_id=1, source_target_pairs={{0,8},{2,10},{4,12},{6,14},{8,0},{10,2},{12,4},{14,6},{16,24},{18,... | collective-permute-start | bytes 2359304 | tf_op jit(solution)/shard_map/ppermute | solution.py:22
  388.4 16.9 %collective-permute-start.44 = (bf16[512,384]{1,0:T(8,128)(2,1)S(1)}, bf16[512,384]{1,0:T(8,128)(2,1)S(1)}, u32[]{:S(2)}, u32[]{:S(2)}) collective-permute-start(bf16[512,384]{1,0:T(8,128)(2,1)S(1)} %multiply_add_fusion.1), channel_id=1, source_target_pairs={{0,2},{2,0},{4,6},{6,4},{8,10},{10,8},{12,14},{14,12},{16,18},{18,... | collective-permute-start | bytes 1179656 | tf_op jit(solution)/shard_map/ppermute | solution.py:22
  404.8 28.9 %collective-permute-start.49 = (bf16[2,2,48,3072]{3,2,1,0:T(8,128)(2,1)S(1)}, bf16[2,2,48,3072]{3,2,1,0:T(8,128)(2,1)S(1)}, u32[]{:S(2)}, u32[]{:S(2)}) collective-permute-start(bf16[2,2,48,3072]{3,2,1,0:T(8,128)(2,1)S(1)} %slice_bitcast_fusion.2), channel_id=1, source_target_pairs={{0,4},{2,6},{4,0},{6,2},{8,12},{10,14},{12,8},{14,10},{16,20},{18,... | collective-permute-start | bytes 3538952 | tf_op jit(solution)/shard_map/ppermute | solution.py:22
  421.5 36.6 %collective-permute-start.53 = (bf16[2,2,48,3072]{3,2,1,0:T(8,128)(2,1)S(1)}, bf16[2,2,48,3072]{3,2,1,0:T(8,128)(2,1)S(1)}, u32[]{:S(2)}, u32[]{:S(2)}) collective-permute-start(bf16[2,2,48,3072]{3,2,1,0:T(8,128)(2,1)S(1)} %slice_bitcast_fusion), channel_id=1, source_target_pairs={{0,4},{2,6},{4,0},{6,2},{8,12},{10,14},{12,8},{14,10},{16,20},{18,... | collective-permute-start | bytes 3538952 | tf_op jit(solution)/shard_map/ppermute | solution.py:22
  433.8 24.4 %collective-permute-start.51 = (bf16[512,384]{1,0:T(8,128)(2,1)S(1)}, bf16[512,384]{1,0:T(8,128)(2,1)S(1)}, u32[]{:S(2)}, u32[]{:S(2)}) collective-permute-start(bf16[512,384]{1,0:T(8,128)(2,1)S(1)} %maximum_select_fusion.5), channel_id=1, source_target_pairs={{0,8},{2,10},{4,12},{6,14},{8,0},{10,2},{12,4},{14,6},{16,24},{18,... | collective-permute-start | bytes 1179656 | tf_op jit(solution)/shard_map/ppermute | solution.py:22
  435.0 23.4 %collective-permute-start.50 = (bf16[512,384]{1,0:T(8,128)(2,1)S(1)}, bf16[512,384]{1,0:T(8,128)(2,1)S(1)}, u32[]{:S(2)}, u32[]{:S(2)}) collective-permute-start(bf16[512,384]{1,0:T(8,128)(2,1)S(1)} %maximum_select_fusion.5), channel_id=1, source_target_pairs={{0,2},{2,0},{4,6},{6,4},{8,10},{10,8},{12,14},{14,12},{16,18},{18,... | collective-permute-start | bytes 1179656 | tf_op jit(solution)/shard_map/ppermute | solution.py:22
  435.1 29.4 %collective-permute-start.80 = (bf16[2,48,3072]{2,1,0:T(8,128)(2,1)S(1)}, bf16[2,48,3072]{2,1,0:T(8,128)(2,1)S(1)}, u32[]{:S(2)}, u32[]{:S(2)}) collective-permute-start(bf16[2,48,3072]{2,1,0:T(8,128)(2,1)S(1)} %slice_bitcast_fusion.13), channel_id=1, source_target_pairs={{0,16},{2,18},{4,20},{6,22},{8,24},{10,26},{12,28},{14,30},{16,0},... | collective-permute-start | bytes 1769480 | tf_op jit(solution)/shard_map/ppermute | solution.py:22
  464.6 31.6 %collective-permute-start.81 = (bf16[2,24,3072]{2,1,0:T(8,128)(2,1)S(1)}, bf16[2,24,3072]{2,1,0:T(8,128)(2,1)S(1)}, u32[]{:S(2)}, u32[]{:S(2)}) collective-permute-start(bf16[2,24,3072]{2,1,0:T(8,128)(2,1)S(1)} %get-tuple-element.303), channel_id=1, source_target_pairs={{0,2},{2,0},{4,6},{6,4},{8,10},{10,8},{12,14},{14,12},{16,18},{18,... | collective-permute-start | bytes 884744 | tf_op jit(solution)/shard_map/ppermute | solution.py:22
  467.7 27.3 %collective-permute-start.54 = (bf16[512,384]{1,0:T(8,128)(2,1)S(1)}, bf16[512,384]{1,0:T(8,128)(2,1)S(1)}, u32[]{:S(2)}, u32[]{:S(2)}) collective-permute-start(bf16[512,384]{1,0:T(8,128)(2,1)S(1)} %constant_dynamic-slice_fusion.4), channel_id=1, source_target_pairs={{0,4},{2,6},{4,0},{6,2},{8,12},{10,14},{12,8},{14,10},{16,20},{18,... | collective-permute-start | bytes 1179656 | tf_op jit(solution)/shard_map/ppermute | solution.py:22
  468.3 39.3 %collective-permute-start.83 = (bf16[2,48,3072]{2,1,0:T(8,128)(2,1)S(1)}, bf16[2,48,3072]{2,1,0:T(8,128)(2,1)S(1)}, u32[]{:S(2)}, u32[]{:S(2)}) collective-permute-start(bf16[2,48,3072]{2,1,0:T(8,128)(2,1)S(1)} %slice_bitcast_fusion.12), channel_id=1, source_target_pairs={{0,16},{2,18},{4,20},{6,22},{8,24},{10,26},{12,28},{14,30},{16,0},... | collective-permute-start | bytes 1769480 | tf_op jit(solution)/shard_map/ppermute | solution.py:22
  492.8 29.3 %collective-permute-start.67 = (bf16[2,2,512,256]{3,2,1,0:T(8,128)(2,1)S(1)}, bf16[2,2,512,256]{3,2,1,0:T(8,128)(2,1)S(1)}, u32[]{:S(2)}, u32[]{:S(2)}) collective-permute-start(bf16[2,2,512,256]{3,2,1,0:T(8,128)(2,1)S(1)} %slice_bitcast_fusion.6), channel_id=1, source_target_pairs={{0,4},{2,6},{4,0},{6,2},{8,12},{10,14},{12,8},{14,10},{16,20},{18,... | collective-permute-start | bytes 3145736 | tf_op jit(solution)/shard_map/ppermute | solution.py:22
  493.8 47.5 %collective-permute-start.57 = (bf16[2,2,512,256]{3,2,1,0:T(8,128)(2,1)S(1)}, bf16[2,2,512,256]{3,2,1,0:T(8,128)(2,1)S(1)}, u32[]{:S(2)}, u32[]{:S(2)}) collective-permute-start(bf16[2,2,512,256]{3,2,1,0:T(8,128)(2,1)S(1)} %slice_bitcast_fusion.10), channel_id=1, source_target_pairs={{0,4},{2,6},{4,0},{6,2},{8,12},{10,14},{12,8},{14,10},{16,20},{18,... | collective-permute-start | bytes 3145736 | tf_op jit(solution)/shard_map/ppermute | solution.py:22
  495.0 68.8 %collective-permute-start.73 = (bf16[2,2,512,256]{3,2,1,0:T(8,128)(2,1)S(1)}, bf16[2,2,512,256]{3,2,1,0:T(8,128)(2,1)S(1)}, u32[]{:S(2)}, u32[]{:S(2)}) collective-permute-start(bf16[2,2,512,256]{3,2,1,0:T(8,128)(2,1)S(1)} %slice_bitcast_fusion.4), channel_id=1, source_target_pairs={{0,4},{2,6},{4,0},{6,2},{8,12},{10,14},{12,8},{14,10},{16,20},{18,... | collective-permute-start | bytes 3145736 | tf_op jit(solution)/shard_map/ppermute | solution.py:22
  519.3 67.0 %collective-permute-start.63 = (bf16[2,2,512,256]{3,2,1,0:T(8,128)(2,1)S(1)}, bf16[2,2,512,256]{3,2,1,0:T(8,128)(2,1)S(1)}, u32[]{:S(2)}, u32[]{:S(2)}) collective-permute-start(bf16[2,2,512,256]{3,2,1,0:T(8,128)(2,1)S(1)} %slice_bitcast_fusion.8), channel_id=1, source_target_pairs={{0,4},{2,6},{4,0},{6,2},{8,12},{10,14},{12,8},{14,10},{16,20},{18,... | collective-permute-start | bytes 3145736 | tf_op jit(solution)/shard_map/ppermute | solution.py:22
  522.0 66.7 %collective-permute-start.85 = (bf16[2,24,3072]{2,1,0:T(8,128)(2,1)S(1)}, bf16[2,24,3072]{2,1,0:T(8,128)(2,1)S(1)}, u32[]{:S(2)}, u32[]{:S(2)}) collective-permute-start(bf16[2,24,3072]{2,1,0:T(8,128)(2,1)S(1)} %get-tuple-element.297), channel_id=1, source_target_pairs={{0,8},{2,10},{4,12},{6,14},{8,0},{10,2},{12,4},{14,6},{16,24},{18,... | collective-permute-start | bytes 884744 | tf_op jit(solution)/shard_map/ppermute | solution.py:22
  522.3 73.3 %collective-permute-start.68 = (bf16[2,512,256]{2,1,0:T(8,128)(2,1)S(1)}, bf16[2,512,256]{2,1,0:T(8,128)(2,1)S(1)}, u32[]{:S(2)}, u32[]{:S(2)}) collective-permute-start(bf16[2,512,256]{2,1,0:T(8,128)(2,1)S(1)} %slice_bitcast_fusion.14), channel_id=1, source_target_pairs={{0,16},{2,18},{4,20},{6,22},{8,24},{10,26},{12,28},{14,30},{16,0},... | collective-permute-start | bytes 1572872 | tf_op jit(solution)/shard_map/ppermute | solution.py:22
  541.5 54.3 %collective-permute-start.58 = (bf16[2,512,256]{2,1,0:T(8,128)(2,1)S(1)}, bf16[2,512,256]{2,1,0:T(8,128)(2,1)S(1)}, u32[]{:S(2)}, u32[]{:S(2)}) collective-permute-start(bf16[2,512,256]{2,1,0:T(8,128)(2,1)S(1)} %slice_bitcast_fusion.19), channel_id=1, source_target_pairs={{0,16},{2,18},{4,20},{6,22},{8,24},{10,26},{12,28},{14,30},{16,0},... | collective-permute-start | bytes 1572872 | tf_op jit(solution)/shard_map/ppermute | solution.py:22
  563.9 30.4 %collective-permute-start.77 = (bf16[512,384]{1,0:T(8,128)(2,1)S(1)}, bf16[512,384]{1,0:T(8,128)(2,1)S(1)}, u32[]{:S(2)}, u32[]{:S(2)}) collective-permute-start(bf16[512,384]{1,0:T(8,128)(2,1)S(1)} %maximum_select_fusion.6), channel_id=1, source_target_pairs={{0,4},{2,6},{4,0},{6,2},{8,12},{10,14},{12,8},{14,10},{16,20},{18,... | collective-permute-start | bytes 1179656 | tf_op jit(solution)/shard_map/ppermute | solution.py:22
  586.3 36.4 %collective-permute-start.74 = (bf16[2,512,256]{2,1,0:T(8,128)(2,1)S(1)}, bf16[2,512,256]{2,1,0:T(8,128)(2,1)S(1)}, u32[]{:S(2)}, u32[]{:S(2)}) collective-permute-start(bf16[2,512,256]{2,1,0:T(8,128)(2,1)S(1)} %slice_bitcast_fusion.18), channel_id=1, source_target_pairs={{0,16},{2,18},{4,20},{6,22},{8,24},{10,26},{12,28},{14,30},{16,0},... | collective-permute-start | bytes 1572872 | tf_op jit(solution)/shard_map/ppermute | solution.py:22
  588.8 45.0 %collective-permute-start.64 = (bf16[2,512,256]{2,1,0:T(8,128)(2,1)S(1)}, bf16[2,512,256]{2,1,0:T(8,128)(2,1)S(1)}, u32[]{:S(2)}, u32[]{:S(2)}) collective-permute-start(bf16[2,512,256]{2,1,0:T(8,128)(2,1)S(1)} %slice_bitcast_fusion.16), channel_id=1, source_target_pairs={{0,16},{2,18},{4,20},{6,22},{8,24},{10,26},{12,28},{14,30},{16,0},... | collective-permute-start | bytes 1572872 | tf_op jit(solution)/shard_map/ppermute | solution.py:22
  594.6 53.9 %collective-permute-start.78 = (bf16[1024,384]{1,0:T(8,128)(2,1)S(1)}, bf16[1024,384]{1,0:T(8,128)(2,1)S(1)}, u32[]{:S(2)}, u32[]{:S(2)}) collective-permute-start(bf16[1024,384]{1,0:T(8,128)(2,1)S(1)} %maximum_select_fusion.2), channel_id=1, source_target_pairs={{0,8},{2,10},{4,12},{6,14},{8,0},{10,2},{12,4},{14,6},{16,24},{18,... | collective-permute-start | bytes 2359304 | tf_op jit(solution)/shard_map/ppermute | solution.py:22
  595.7 27.1 %collective-permute-start.69 = (bf16[2,256,256]{2,1,0:T(8,128)(2,1)S(1)}, bf16[2,256,256]{2,1,0:T(8,128)(2,1)S(1)}, u32[]{:S(2)}, u32[]{:S(2)}) collective-permute-start(bf16[2,256,256]{2,1,0:T(8,128)(2,1)S(1)} %get-tuple-element.315), channel_id=1, source_target_pairs={{0,2},{2,0},{4,6},{6,4},{8,10},{10,8},{12,14},{14,12},{16,18},{18,... | collective-permute-start | bytes 786440 | tf_op jit(solution)/shard_map/ppermute | solution.py:22
  595.8 38.0 %collective-permute-start.59 = (f32[1]{0:T(128)}, f32[1]{0:T(128)}, u32[]{:S(2)}, u32[]{:S(2)}) collective-permute-start(f32[1]{0:T(128)} %add.338), channel_id=1, source_target_pairs={{0,4},{2,6},{4,0},{6,2},{8,12},{10,14},{12,8},{14,10},{16,20},{18,... | collective-permute-start | bytes 20 | tf_op jit(solution)/shard_map/ppermute | solution.py:22
  622.8 25.4 %collective-permute-start.75 = (bf16[2,256,256]{2,1,0:T(8,128)(2,1)S(1)}, bf16[2,256,256]{2,1,0:T(8,128)(2,1)S(1)}, u32[]{:S(2)}, u32[]{:S(2)}) collective-permute-start(bf16[2,256,256]{2,1,0:T(8,128)(2,1)S(1)} %get-tuple-element.311), channel_id=1, source_target_pairs={{0,2},{2,0},{4,6},{6,4},{8,10},{10,8},{12,14},{14,12},{16,18},{18,... | collective-permute-start | bytes 786440 | tf_op jit(solution)/shard_map/ppermute | solution.py:22
  624.2 24.1 %collective-permute-start.70 = (bf16[2,256,256]{2,1,0:T(8,128)(2,1)S(1)}, bf16[2,256,256]{2,1,0:T(8,128)(2,1)S(1)}, u32[]{:S(2)}, u32[]{:S(2)}) collective-permute-start(bf16[2,256,256]{2,1,0:T(8,128)(2,1)S(1)} %get-tuple-element.313), channel_id=1, source_target_pairs={{0,8},{2,10},{4,12},{6,14},{8,0},{10,2},{12,4},{14,6},{16,24},{18,... | collective-permute-start | bytes 786440 | tf_op jit(solution)/shard_map/ppermute | solution.py:22
  (110 other events, 1387.9 us)
